TPU v7x, 32 devices: a whole 2x2x4 slice. The times are simulated.
32 devices in a mesh: rows: 8 (over z, y), zone: 4 (over x, core).
Axes of the slice: x: 2, y: 2, z: 4, core: 2. Of those that a mesh axis runs over, the one named last changes fastest.
Arguments:
- snapshots: float32 [262144, 256], P(('rows', 'zone')), may hold values from -6 to 6
- tangent: bfloat16 [262144, 512], P(('rows', 'zone')), may hold values from -0.25 to 0.25
- pattern: int32 [2048, 4], P(('rows', 'zone')), may hold values from 0 to 259, as said below
- forcing: float32 [262144], P(('rows', 'zone')), may hold values from -6 to 6
- step_index: int32 [256], replicated, may hold values from 0 to 255, each once
Outputs:
- basis: float32 [262144, 256], P(('rows', 'zone'))
- coefficients: float32 [3, 256], replicated
- residual: float32 [262144], P(('rows', 'zone'))
Inputs may be any that keep to these rules, and one draw needn't show every extreme that they name: `pattern`: codes of sources 1 and 3 name one of the last 4 blocks of the neighbour, codes of sources 2 and 4 one of its first 4 blocks. `step_index`: each step index once.
All inputs are finite; a program needn't handle non-finite values.
Results may differ from a plain program's by a relative error of at most 0.0003.
Values sent between devices are 32-bit elements; how exact they have to be, the bound alone decides.
No kernel may reach another device: no remote copies, remote signals or barrier semaphores. Data moves between devices by JAX's collectives and lax.ppermute only.
A program may use at most 320 MiB of HBM per device.

v0:
```python
import jax
import jax.numpy as jnp
from jax import lax
from jax.sharding import PartitionSpec as P

HALO = 4
STEPS = 3


step_size = 0.25


def shifted(value, axis, steps):
    count = lax.axis_size(axis)
    pairs = [(source, (source + steps) % count) for source in range(count)]
    return lax.ppermute(value, axis, pairs)


def from_behind(shard, axis, by):
    devices = lax.axis_size(axis)
    pairs = [(i, i + by) for i in range(devices) if 0 <= i + by < devices]
    return lax.ppermute(shard, axis, pairs)


def tangent_product(field_in, tangent, pattern):
    highest = lax.Precision.HIGHEST
    block_count, coupled = pattern.shape
    row_count, snap_count = field_in.shape
    block_rows = row_count // block_count
    edge_rows = HALO * block_rows
    tail_part = field_in[row_count - edge_rows :]
    head_part = field_in[:edge_rows]
    rows_prev = shifted(tail_part, "rows", 1)
    rows_next = shifted(head_part, "rows", -1)
    zone_prev = from_behind(tail_part, "zone", 1)
    zone_next = from_behind(head_part, "zone", -1)
    candidates = jnp.concatenate([field_in, rows_prev, rows_next, zone_prev, zone_next], 0)
    source = pattern // block_count
    block_pick = pattern % block_count
    offset_tail = block_pick - (block_count - HALO)
    index_map = jnp.where(
        source == 0,
        block_pick,
        jnp.where(
            source == 1,
            block_count + offset_tail,
            jnp.where(
                source == 2,
                block_count + HALO + block_pick,
                jnp.where(
                    source == 3,
                    block_count + 2 * HALO + offset_tail,
                    block_count + 3 * HALO + block_pick,
                ),
            ),
        ),
    )
    candidates = candidates.reshape(candidates.shape[0] // block_rows, block_rows, snap_count)
    picked = candidates[index_map]
    tile_blocks = tangent.reshape(block_count, block_rows, coupled, block_rows).astype(jnp.float32)
    product = jnp.einsum("gbec,gecs->gbs", tile_blocks, picked, precision=highest)
    return product.reshape(row_count, snap_count)


def shards(snapshots, tangent, pattern, forcing, step_index):
    highest = lax.Precision.HIGHEST
    row_count, snap_count = snapshots.shape
    inverse_count = 1.0 / (row_count * lax.axis_size("rows") * lax.axis_size("zone"))
    identity = jnp.eye(snap_count, dtype=jnp.float32)
    gram_local = jnp.dot(snapshots.T, snapshots, precision=highest) * inverse_count
    gram_matrix = lax.psum(gram_local, ("rows", "zone"))
    factor_low = jnp.linalg.cholesky(gram_matrix)
    inverse = jax.scipy.linalg.solve_triangular(factor_low, identity, lower=True).T
    basis = jnp.dot(snapshots, inverse, precision=highest)
    tangent_image = tangent_product(basis, tangent, pattern)
    trial_basis = basis + step_size * tangent_image
    normal, project, load_vector = lax.psum(
        (
            jnp.dot(trial_basis.T, trial_basis, precision=highest) * inverse_count,
            jnp.dot(trial_basis.T, basis, precision=highest) * inverse_count,
            jnp.dot(trial_basis.T, forcing, precision=highest) * inverse_count,
        ),
        ("rows", "zone"),
    )
    latest = (step_index == jnp.max(step_index)).astype(jnp.float32)
    coeff_now = jnp.dot(latest, factor_low, precision=highest)
    normal_low = jnp.linalg.cholesky(normal)
    history = []
    coeff_old = coeff_now
    for iteration in range(STEPS):
        coeff_old = coeff_now
        right_side = jnp.dot(project, coeff_now, precision=highest) + step_size * load_vector
        coeff_now = jax.scipy.linalg.cho_solve((normal_low, True), right_side)
        history.append(coeff_now)
    residual = (
        jnp.dot(trial_basis, coeff_now, precision=highest)
        - jnp.dot(basis, coeff_old, precision=highest)
        - step_size * forcing
    )
    return (basis, jnp.stack(history), residual)


def solution(mesh):
    in_specs = (
        P(("rows", "zone"), None),
        P(("rows", "zone"), None),
        P(("rows", "zone"), None),
        P(("rows", "zone")),
        P(),
    )
    out_specs = (P(("rows", "zone"), None), P(), P(("rows", "zone")))
    return jax.shard_map(shards, mesh=mesh, in_specs=in_specs, out_specs=out_specs, check_vma=False)
```

profile of v0, /device:TPU:0, one launch (start us, length us, event | category | flops | bytes accessed | tf_op | source)
XLA Modules:
  0.0 581.6 jit_solution(15135478761900624268)
XLA Ops:
  7.2 19.9 %convolution_multiply_fusion.2 = f32[256,256]{0,1:T(8,128)} fusion(f32[8192,256]{1,0:T(8,128)} %param.8), kind=kOutput, calls=%fused_computation.12 | convolution fusion | flops 6442516480 | bytes 8650752 | tf_op jit(solution)/shard_map/dot_general | solution.py:70
  28.1 126.9 %all-reduce.5.cloned.1.call-done = f32[256,256]{0,1:T(8,128)} async-done(((f32[256,256]{0,1:T(8,128)}), f32[256,256]{0,1:T(8,128)}) %all-reduce.5.cloned.1.call-update) | async-done | bytes 262160 | tf_op jit(solution)/shard_map/psum | solution.py:71
  157.1 11.7 %cholesky.130 = f32[128,128]{1,0:T(8,128)S(1)} custom-call(f32[128,128]{1,0:T(8,128)S(1)} %cholesky.194), custom_call_target="Cholesky" | custom-call | tf_op jit(solution)/shard_map/jit(cholesky)/cholesky | solution.py:72
  168.8 9.8 %custom-call.21 = f32[1,128,128]{1,2,0:T(8,128)S(1)} custom-call(f32[1,128,128]{2,1,0:T(8,128)S(1)} %get-tuple-element.73), custom_call_target="InvertDiagBlocksLowerTriangular" | custom-call | tf_op jit(solution)/shard_map/jit(cholesky)/cholesky | solution.py:72
  179.2 11.7 %cholesky.147 = f32[128,128]{1,0:T(8,128)S(1)} custom-call(f32[128,128]{1,0:T(8,128)S(1)} %convolution_subtract_fusion.2), custom_call_target="Cholesky" | custom-call | tf_op jit(solution)/shard_map/jit(cholesky)/cholesky | solution.py:72
  193.1 4.4 while.7
  194.0 1.4 bitcast_dynamic-update-slice_fusion.4
  196.0 1.4 bitcast_dynamic-update-slice_fusion.4
  197.5 19.7 %custom-call.17 = f32[2,128,128]{1,2,0:T(8,128)S(1)} custom-call(f32[2,128,128]{2,1,0:T(8,128)S(1)} %get-tuple-element.20), custom_call_target="InvertDiagBlocksLowerTriangular" | custom-call | tf_op jit(solution)/shard_map/jit(_solve_triangular)/triangular_solve | solution.py:73
  218.0 11.7 %constant_dynamic-update-slice_fusion.4 = (f32[10240,256]{0,1:T(8,128)}, f32[256,8192]{1,0:T(8,128)S(1)}) fusion(f32[8192,256]{1,0:T(8,128)} %param.8, f32[128,256]{1,0:T(8,128)S(1)} %fusion.33, f32[128,256]{1,0:T(8,128)S(1)} %fusion.27), kind=kOutput, calls=%fused_computation.96 | convolution fusion | flops 6442516480 | bytes 25427968 | tf_op jit(solution)/shard_map/dot_general | solution.py:74
  229.7 3.3 copy-done
  234.0 1.4 collective-permute-start
  235.4 3.3 collective-permute-start.1
  240.8 12.5 %reshape.63 = bf16[64,128,4,128]{3,2,1,0:T(4,128)(2,1)} reshape(bf16[8192,512]{1,0:T(8,128)(2,1)} %param.9) | data formatting | bytes 16777216 | tf_op jit(solution)/shard_map/reshape | solution.py:60
  254.6 9.5 %copy.26 = f32[8192,256]{1,0:T(8,128)} copy(f32[8192,256]{0,1:T(8,128)} %bitcast.247) | data formatting | bytes 16777216
  267.8 11.4 %copy.31 = f32[10240,256]{1,0:T(8,128)} copy(f32[10240,256]{0,1:T(8,128)} %constant_dynamic-update-slice_fusion) | data formatting | bytes 20971520 | tf_op jit(solution)/shard_map/reshape | solution.py:58
  279.3 18.9 %gather_fusion = f32[256,128,256]{2,1,0:T(8,128)} fusion(f32[80,128,256]{2,1,0:T(8,128)} %bitcast.249, s32[1024]{0:T(1024)S(1)} %pad_clamp_fusion), kind=kCustom, calls=%fused_computation | custom fusion | bytes 67109888 | tf_op jit(solution)/shard_map/gather | solution.py:59
  298.1 25.2 %bitcast_multiply_fusion = f32[64,256,128]{1,2,0:T(8,128)} fusion(f32[64,4,128,256]{3,2,1,0:T(8,128)} %bitcast.248, bf16[64,128,4,128]{3,2,1,0:T(4,128)(2,1)} %reshape.63), kind=kOutput, calls=%fused_computation.7 | convolution fusion | flops 12886999040 | bytes 50331648 | tf_op jit(solution)/shard_map/gbec,gecs->gbs/dot_general | solution.py:61
  323.3 8.9 %copy.32 = f32[8192,256]{0,1:T(8,128)} copy(f32[8192,256]{1,0:T(8,128)} %bitcast.250) | data formatting | bytes 16777216 | tf_op jit(solution)/shard_map/mul | solution.py:76
  332.3 13.1 %convolution_multiply_fusion = f32[256,256]{0,1:T(8,128)} fusion(f32[256,8192]{1,0:T(8,128)} %copy-done, f32[8192,256]{0,1:T(8,128)} %copy.32), kind=kOutput, calls=%fused_computation.10 | convolution fusion | flops 6444613632 | bytes 17039360 | tf_op jit(solution)/shard_map/dot_general | solution.py:80
  345.4 12.3 %convolution_multiply_fusion.1 = f32[256,256]{0,1:T(8,128)} fusion(f32[8192,256]{0,1:T(8,128)S(1)} %copy-done.1, f32[256,8192]{1,0:T(8,128)} %copy-done), kind=kOutput, calls=%fused_computation.11 | convolution fusion | flops 6444613632 | bytes 17039360 | tf_op jit(solution)/shard_map/dot_general | solution.py:79
  357.7 10.2 %fusion = f32[1,256]{1,0:T(1,128)S(1)} fusion(f32[8192,1]{0,1:T(1,128)S(1)} %bitcast.251, f32[8192,256]{0,1:T(8,128)} %copy.32, f32[256,8192]{1,0:T(8,128)} %copy-done), kind=kOutput, calls=%fused_computation.5 | convolution fusion | flops 27262976 | bytes 16811008 | tf_op jit(solution)/shard_map/dot_general | solution.py:81
  367.9 40.0 %psum.31 = f32[256]{0:T(256)S(1)} all-reduce(f32[256]{0:T(256)S(1)} %broadcast_multiply_fusion), channel_id=1, replica_groups=mesh['rows'=8,'zone'=4] {'rows','zone'}, use_global_device_ids=true, to_apply=%region_8.10 | all-reduce | flops 256 | bytes 2048 | tf_op jit(solution)/shard_map/psum | solution.py:77
  407.9 78.3 %all-reduce.7.cloned.1.call-done = (f32[256,256]{0,1:T(8,128)}, f32[256,256]{0,1:T(8,128)}) async-done(((f32[256,256]{0,1:T(8,128)}, f32[256,256]{0,1:T(8,128)}), (f32[256,256]{0,1:T(8,128)}, f32[256,256]{0,1:T(8,128)})) %all-reduce.7.cloned.1.call-update) | async-done | bytes 524304 | tf_op jit(solution)/shard_map/psum | solution.py:77
  488.3 11.7 %cholesky.164 = f32[128,128]{1,0:T(8,128)S(1)} custom-call(f32[128,128]{1,0:T(8,128)S(1)} %cholesky.197), custom_call_target="Cholesky" | custom-call | tf_op jit(solution)/shard_map/jit(cholesky)/cholesky | solution.py:87
  500.1 9.8 %custom-call.22 = f32[1,128,128]{1,2,0:T(8,128)S(1)} custom-call(f32[1,128,128]{2,1,0:T(8,128)S(1)} %get-tuple-element.69), custom_call_target="InvertDiagBlocksLowerTriangular" | custom-call | tf_op jit(solution)/shard_map/jit(cholesky)/cholesky | solution.py:87
  510.4 11.7 %cholesky.181 = f32[128,128]{1,0:T(8,128)S(1)} custom-call(f32[128,128]{1,0:T(8,128)S(1)} %convolution_subtract_fusion.1), custom_call_target="Cholesky" | custom-call | tf_op jit(solution)/shard_map/jit(cholesky)/cholesky | solution.py:87
  524.8 4.0 while.8
  527.4 1.4 bitcast_dynamic-update-slice_fusion.5
  528.7 19.9 %custom-call.23 = f32[2,128,128]{1,2,0:T(8,128)S(1)} custom-call(f32[2,128,128]{2,1,0:T(8,128)S(1)} %get-tuple-element.33), custom_call_target="InvertDiagBlocksLowerTriangular" | custom-call | tf_op jit(solution)/shard_map/jit(_cho_solve)/triangular_solve | solution.py:93
  553.4 7.9 %fusion.58 = f32[1,8192]{1,0:T(1,128)S(1)} fusion(f32[256,8192]{1,0:T(8,128)} %copy-done, f32[128,1]{0,1:T(1,128)S(1)} %convolution_bitcast_fusion.8, f32[128,1]{0,1:T(1,128)S(1)} %convolution_bitcast_fusion.6), kind=kOutput, calls=%fused_computation.134 | convolution fusion | flops 25166080 | bytes 8422400 | tf_op jit(solution)/shard_map/dot_general | solution.py:97
  562.7 10.4 %fusion.63 = f32[1,8192]{1,0:T(1,128)S(1)} fusion(f32[128,1]{0,1:T(1,128)S(1)} %convolution_bitcast_fusion.3, f32[128,1]{0,1:T(1,128)S(1)} %convolution_bitcast_fusion.1, f32[8192,256]{0,1:T(8,128)} %copy.32, f32[256,8192]{1,0:T(8,128)} %copy-done), kind=kOutput, calls=%fused_computation.140 | convolution fusion | flops 27263232 | bytes 16811008 | tf_op jit(solution)/shard_map/dot_general | solution.py:96
  (102 shorter events, 28.4 us)
Async XLA Ops:
  7.2 20.3 %copy-start.5 = (s32[64,4]{0,1:T(4,128)S(1)}, s32[64,4]{0,1:T(4,128)}, u32[]{:S(2)}) copy-start(s32[64,4]{0,1:T(4,128)} %param.10) | copy-start | bytes 3076
  7.2 20.3 %copy-start.4 = (s32[256]{0:T(256)S(1)}, s32[256]{0:T(256)}, u32[]{:S(2)}) copy-start(s32[256]{0:T(256)} %param.12) | copy-start | bytes 3076
  7.2 147.8 %all-reduce.5.cloned.1.call-start = ((), (), s32[]{:S(2)}) async-start(), calls=%async_computation | async-start | bytes 524288 | tf_op jit(solution)/shard_map/psum | solution.py:71
  27.2 459.1 %all-reduce.7.cloned.1.call-start = ((), (), s32[]{:S(2)}) async-start(), calls=%async_computation.1 | async-start | bytes 1048576 | tf_op jit(solution)/shard_map/psum | solution.py:77
  229.7 3.3 copy-start
  234.0 30.3 %collective-permute-start = (f32[512,256]{0,1:T(8,128)}, f32[512,256]{0,1:T(8,128)S(1)}, u32[]{:S(2)}, u32[]{:S(2)}) collective-permute-start(f32[512,256]{0,1:T(8,128)} %get-tuple-element.65), channel_id=1, source_target_pairs={{0,4},{4,8},{8,12},{12,16},{16,20},{20,24},{24,28},{28,0},{1,5},{5... | collective-permute-start | bytes 1572872 | tf_op jit(solution)/shard_map/ppermute | solution.py:16
  235.4 29.8 %collective-permute-start.1 = (f32[512,256]{0,1:T(8,128)S(1)}, f32[512,256]{0,1:T(8,128)S(1)}, u32[]{:S(2)}, u32[]{:S(2)}) collective-permute-start(f32[512,256]{0,1:T(8,128)S(1)} %get-tuple-element.64), channel_id=1, source_target_pairs={{0,28},{4,0},{8,4},{12,8},{16,12},{20,16},{24,20},{28,24},{1,29},{... | collective-permute-start | bytes 1572872 | tf_op jit(solution)/shard_map/ppermute | solution.py:16
  239.4 26.7 %collective-permute-start.2 = (f32[512,256]{0,1:T(8,128)}, f32[512,256]{0,1:T(8,128)S(1)}, u32[]{:S(2)}, u32[]{:S(2)}) collective-permute-start(f32[512,256]{0,1:T(8,128)} %get-tuple-element.65), channel_id=1, source_target_pairs={{0,1},{1,2},{2,3},{4,5},{5,6},{6,7},{8,9},{9,10},{10,11},{12,13},{... | collective-permute-start | bytes 1572872 | tf_op jit(solution)/shard_map/ppermute | solution.py:22
  253.3 13.6 %collective-permute-start.3 = (f32[512,256]{0,1:T(8,128)S(1)}, f32[512,256]{0,1:T(8,128)S(1)}, u32[]{:S(2)}, u32[]{:S(2)}) collective-permute-start(f32[512,256]{0,1:T(8,128)S(1)} %get-tuple-element.64), channel_id=1, source_target_pairs={{1,0},{2,1},{3,2},{5,4},{6,5},{7,6},{9,8},{10,9},{11,10},{13,12},{... | collective-permute-start | bytes 1572872 | tf_op jit(solution)/shard_map/ppermute | solution.py:22
  332.3 13.1 %copy-start.1 = (f32[8192,256]{0,1:T(8,128)S(1)}, f32[8192,256]{0,1:T(8,128)}, u32[]{:S(2)}) copy-start(f32[8192,256]{0,1:T(8,128)} %copy.32) | copy-start | bytes 25165828
  345.4 12.3 %copy-start.3 = (f32[8192]{0:T(1024)S(1)}, f32[8192]{0:T(1024)}, u32[]{:S(2)}) copy-start(f32[8192]{0:T(1024)} %param.11) | copy-start | bytes 98308
  486.2 75.1 %copy-start.2 = (f32[256,256]{0,1:T(8,128)S(1)}, f32[256,256]{0,1:T(8,128)}, u32[]{:S(2)}) copy-start(f32[256,256]{0,1:T(8,128)} %get-tuple-element.59) | copy-start | bytes 786436
Sparse Core Ops, SparseCore 0:
  27.3 127.6 all-reduce.4
  357.8 128.3 all-reduce.6
where the time goes:
time: 588 us; the launch traced here: 582 us
  waiting for transfers between devices  205 us (35%)
  matrix products  119 us (20%)
  other arithmetic  113 us (19%)
  local copies, waits for them, and re-layouts  79.5 us (14%)
  blocking collectives  40 us (7%)
  between operations  17.5 us (3%)
  starting transfers between devices  7.62 us (1%)
    psum x1, waiting for transfers between devices, shards(): gram_matrix = lax.psum(gram_local, ('rows', 'zone'))  127 us
    psum x1, waiting for transfers between devices, shards(): lax.psum((jnp.dot(trial_basis.T, trial_basis, precision=highest) * invers...  78.3 us
    psum x1, blocking collectives, shards(): lax.psum((jnp.dot(trial_basis.T, trial_basis, precision=highest) * invers...  40 us
    another operation x7, other arithmetic, shards(): normal_low = jnp.linalg.cholesky(normal)  34.6 us
    another operation x6, other arithmetic, shards(): factor_low = jnp.linalg.cholesky(gram_matrix)  34 us
    dot_general x1, matrix products, tangent_product(): jnp.einsum('gbec,gecs->gbs', tile_blocks, picked, precision=highest)  25.2 us
    another operation x2, other arithmetic, shards(): coeff_now = jax.scipy.linalg.cho_solve((normal_low, True), right_side)  20 us
    dot_general x1, matrix products, shards(): jnp.dot(snapshots.T, snapshots, precision=highest) * inverse_count  19.9 us
  transfers between devices with their start and end apart: 6, of which 2 were waited for; matrix products, arithmetic and copies ran while one was open for 6% of the time, Pallas kernels for 0%

commit v1 on v0

v1 whole, which is shorter than its diff:
```python
import functools

import jax
import jax.numpy as jnp
from jax import lax
from jax.experimental import pallas as pl
from jax.experimental.pallas import tpu as pltpu
from jax.sharding import PartitionSpec as P

HALO = 4
STEPS = 3
STEP_SIZE = 0.25
CHUNK = 1024
LIMIT = 56 * 1024 * 1024
F32 = jnp.float32
BF16 = jnp.bfloat16
HIGHEST = lax.Precision.HIGHEST


def split(value):
    high = value.astype(BF16)
    low = (value - high.astype(F32)).astype(BF16)
    return high, low


def contract_rows(left, right):
    return lax.dot_general(left, right, (((0,), (0,)), ((), ())), preferred_element_type=F32)


def matmul(left, right, precision=None):
    return lax.dot_general(
        left, right, (((1,), (0,)), ((), ())), preferred_element_type=F32, precision=precision
    )


def reversed_bits(value, count):
    result = value * 0
    for bit in range(count):
        result = result | (((value >> bit) & 1) << (count - 1 - bit))
    return result


def gram_kernel(snap_ref, out_ref):
    high, low = split(snap_ref[...])
    part = contract_rows(high, jnp.concatenate([high, low], 1))

    @pl.when(pl.program_id(0) == 0)
    def _():
        out_ref[...] = part

    @pl.when(pl.program_id(0) > 0)
    def _():
        out_ref[...] += part


def gram_call(snapshots):
    rows, snaps = snapshots.shape
    return pl.pallas_call(
        gram_kernel,
        out_shape=jax.ShapeDtypeStruct((snaps, 2 * snaps), F32),
        grid=(rows // CHUNK,),
        in_specs=[pl.BlockSpec((CHUNK, snaps), lambda i: (i, 0))],
        out_specs=pl.BlockSpec((snaps, 2 * snaps), lambda i: (0, 0)),
        compiler_params=pltpu.CompilerParams(vmem_limit_bytes=LIMIT),
        cost_estimate=pl.CostEstimate(
            flops=4 * rows * snaps * snaps, bytes_accessed=4 * rows * snaps, transcendentals=0
        ),
        name="gram",
    )(snapshots)


def tangent_kernel(
    parts,
    pattern_ref,
    place_ref,
    snap_any,
    prev_any,
    next_any,
    left_any,
    right_any,
    tangent_ref,
    force_ref,
    gram_ref,
    image_ref,
    pack_ref,
    snap,
    halo,
    field,
    shared,
    acc,
    cross,
    load,
    sems,
):
    step = pl.program_id(0)
    rows, snaps = snap.shape
    block_count = pattern_ref.shape[0]
    block = rows // block_count
    edge = HALO * block
    chunks = rows // CHUNK
    per_chunk = CHUNK // block

    @pl.when(step == 0)
    def _():
        copies = []
        for i in range(chunks):
            at = pl.ds(i * CHUNK, CHUNK)
            copies.append(pltpu.make_async_copy(snap_any.at[at, :], snap.at[at, :], sems.at[i]))
        for i, ref in enumerate((prev_any, next_any, left_any, right_any)):
            at = pl.ds(i * edge, edge)
            copies.append(pltpu.make_async_copy(ref, halo.at[at, :], sems.at[chunks + i]))
        for copy in copies:
            copy.start()
        for i in range(chunks):
            copies[i].wait()
            at = pl.ds(i * CHUNK, CHUNK)
            high, low = split(snap[at, :])
            field[at, :snaps] = high
            field[at, snaps:] = low
        for i in range(4):
            copies[chunks + i].wait()
            high, low = split(halo[pl.ds(i * edge, edge), :])
            at = pl.ds(rows + i * edge, edge)
            field[at, :snaps] = high
            field[at, snaps:] = low
        shared[...] = jnp.zeros_like(shared)
        acc[...] = jnp.zeros_like(acc)
        cross[...] = jnp.zeros_like(cross)
        load[...] = jnp.zeros_like(load)

    @pl.when(step < chunks)
    def _():
        force_columns = force_ref[...].T
        load_part = jnp.zeros((1, snaps), F32)
        trial_parts = []
        for k in range(per_chunk):
            g = step * per_chunk + k
            picked = []
            for e in range(pattern_ref.shape[1]):
                code = pattern_ref[g, e]
                source = lax.div(code, block_count)
                pick = lax.rem(code, block_count)
                tail = (source == 1) | (source == 3)
                base = jnp.where(source == 0, 0, block_count + (source - 1) * HALO)
                place = base + jnp.where(tail, pick - (block_count - HALO), pick)
                picked.append(field[pl.ds(pl.multiple_of(place * block, block), block), :])
            both = matmul(tangent_ref[k * block : (k + 1) * block, :], jnp.concatenate(picked, 0))
            image = STEP_SIZE * (both[:, :snaps] + both[:, snaps:])
            image_ref[k * block : (k + 1) * block, :] = image
            start = pl.multiple_of(g * block, block)
            trial = snap[pl.ds(start, block), :] + image
            load_part += jnp.sum(trial * force_columns[:, k : k + 1], 0, keepdims=True)
            trial_parts.append(trial)
        trial_high, trial_low = split(jnp.concatenate(trial_parts, 0))
        here = field[pl.ds(pl.multiple_of(step * CHUNK, CHUNK), CHUNK), :]
        shared[...] += contract_rows(trial_high, here)
        acc[...] += contract_rows(trial_high, jnp.concatenate([trial_high, trial_low], 1))
        cross[...] += contract_rows(here[:, :snaps], trial_low)
        load[...] += load_part

    @pl.when(step == chunks)
    def _():
        gram = gram_ref[:, :snaps] + gram_ref[:, snaps:] + gram_ref[:, snaps:].T
        project = shared[:, :snaps] + shared[:, snaps:] + cross[...].T
        mixed = acc[:, snaps:]
        normal = acc[:, :snaps] + mixed + mixed.T
        row = lax.broadcasted_iota(jnp.int32, (snaps, snaps), 0)
        column = lax.broadcasted_iota(jnp.int32, (snaps, snaps), 1)
        packed = jnp.where(row <= column, gram, normal)
        diagonal = jnp.sum(jnp.where(row == column, normal, 0.0), 0, keepdims=True)
        share = snaps // parts
        extra_row = lax.broadcasted_iota(jnp.int32, (8, snaps), 0)
        extra = jnp.where(extra_row == 0, load[...], jnp.where(extra_row == 1, diagonal, 0.0))
        bits = parts.bit_length() - 1
        for c in range(parts):
            at = reversed_bits(place_ref[0] ^ c, bits)
            pack_ref[at, :share, :] = packed[c * share : (c + 1) * share]
            pack_ref[at, share : 2 * share, :] = project[c * share : (c + 1) * share]
            pack_ref[at, 2 * share :, :] = extra


def tangent_call(snapshots, halos, tangent, pattern, force, gram, place, parts):
    rows, snaps = snapshots.shape
    blocks, coupled = pattern.shape
    block = rows // blocks
    share = snaps // parts
    chunks = rows // CHUNK
    hbm = pl.BlockSpec(memory_space=pl.ANY)
    return pl.pallas_call(
        functools.partial(tangent_kernel, parts),
        out_shape=(
            jax.ShapeDtypeStruct((rows, snaps), F32),
            jax.ShapeDtypeStruct((parts, 2 * share + 8, snaps), F32),
        ),
        grid_spec=pltpu.PrefetchScalarGridSpec(
            num_scalar_prefetch=2,
            grid=(chunks + 1,),
            in_specs=[
                hbm,
                hbm,
                hbm,
                hbm,
                hbm,
                pl.BlockSpec((CHUNK, coupled * block), lambda i, *_: (jnp.minimum(i, chunks - 1), 0)),
                pl.BlockSpec((CHUNK // block, block), lambda i, *_: (jnp.minimum(i, chunks - 1), 0)),
                pl.BlockSpec((snaps, 2 * snaps), lambda i, *_: (0, 0)),
            ],
            out_specs=[
                pl.BlockSpec((CHUNK, snaps), lambda i, *_: (jnp.minimum(i, chunks - 1), 0)),
                pl.BlockSpec((parts, 2 * share + 8, snaps), lambda i, *_: (0, 0, 0)),
            ],
            scratch_shapes=[
                pltpu.VMEM((rows, snaps), F32),
                pltpu.VMEM((4 * HALO * block, snaps), F32),
                pltpu.VMEM((rows + 4 * HALO * block, 2 * snaps), BF16),
                pltpu.VMEM((snaps, 2 * snaps), F32),
                pltpu.VMEM((snaps, 2 * snaps), F32),
                pltpu.VMEM((snaps, snaps), F32),
                pltpu.VMEM((1, snaps), F32),
                pltpu.SemaphoreType.DMA((chunks + 4,)),
            ],
        ),
        compiler_params=pltpu.CompilerParams(vmem_limit_bytes=LIMIT),
        cost_estimate=pl.CostEstimate(
            flops=18 * rows * snaps * snaps, bytes_accessed=12 * rows * snaps, transcendentals=0
        ),
        name="tangent",
    )(pattern, place, snapshots, *halos, tangent, force, gram)


def inverse_factors(blocks):
    size = blocks[0].shape[0]
    groups = size // 8
    lane = lax.broadcasted_iota(jnp.int32, (8, size), 1)
    sub = lax.broadcasted_iota(jnp.int32, (8, size), 0)
    spread = lambda value: jnp.broadcast_to(value, (8, size))
    count = len(blocks)
    rows = [[value[8 * g : 8 * g + 8, :] for g in range(groups)] for value in blocks]
    done = [[] for _ in blocks]
    for g in range(groups):
        first = 8 * g
        inside = (lane >= first) & (lane < first + 8)
        unit = jnp.where(lane == sub + first, 1.0, 0.0)
        columns = [
            [spread(rows[m][g][:, first + j : first + j + 1]) for j in range(8)] for m in range(count)
        ]
        work = [jnp.where(inside, unit, rows[m][g]) for m in range(count)]
        kept = [jnp.zeros((8, size), F32) for _ in range(count)]
        for j in range(8):
            for m in range(count):
                pivot = spread(columns[m][j][j : j + 1, :])
                inverse = 1.0 / pivot
                root = lax.rsqrt(pivot)
                root = root * (1.5 - 0.5 * pivot * root * root)
                mine = sub == j
                for k in range(j + 1, 8):
                    scaled = spread(columns[m][k][j : j + 1, :]) * inverse
                    columns[m][k] = jnp.where(mine, scaled, columns[m][k] - columns[m][j] * scaled)
                row = spread(work[m][j : j + 1, :])
                kept[m] = jnp.where(mine, row * root, kept[m])
                scaled = row * inverse
                work[m] = jnp.where(mine, scaled, work[m] - columns[m][j] * scaled)
        for m in range(count):
            done[m].append(jnp.where(lane < first + 8, kept[m], 0.0))
            pivots = [spread(work[m][j : j + 1, :]) for j in range(8)]
            for i in range(g + 1, groups):
                old = rows[m][i]
                new = jnp.where(inside, 0.0, old)
                for j in range(8):
                    new = new - spread(old[:, first + j : first + j + 1]) * pivots[j]
                rows[m][i] = new
    return [jnp.concatenate(values, 0) for values in done]


def dot_last(left, right):
    return lax.dot_general(
        left, right, (((1,), (1,)), ((), ())), preferred_element_type=F32, precision=HIGHEST
    )


def reduced_kernel(parts, inverse_count, place_ref, pack_ref, index_ref, root_ref, coeff_ref, state_ref):
    snaps = pack_ref.shape[2]
    share = snaps // parts
    half = snaps // 2
    bits = parts.bit_length() - 1
    order = [reversed_bits(place_ref[0] ^ c, bits) for c in range(parts)]
    packed = jnp.concatenate([pack_ref[at, :share, :] for at in order], 0) * inverse_count
    project = jnp.concatenate([pack_ref[at, share : 2 * share, :] for at in order], 0) * inverse_count
    load = pack_ref[order[0], 2 * share : 2 * share + 1, :] * inverse_count
    diagonal = pack_ref[order[0], 2 * share + 1 : 2 * share + 2, :] * inverse_count
    row = lax.broadcasted_iota(jnp.int32, (snaps, snaps), 0)
    column = lax.broadcasted_iota(jnp.int32, (snaps, snaps), 1)
    turned = packed.T
    gram = jnp.where(row <= column, packed, turned)
    normal = jnp.where(row > column, packed, jnp.where(row == column, diagonal, turned))

    pair = (gram, normal)
    upper = inverse_factors([value[:half, :half] for value in pair])
    below = [dot_last(value[half:, :half], inv) for value, inv in zip(pair, upper)]
    rest = [value[half:, half:] - dot_last(low, low) for value, low in zip(pair, below)]
    lower = inverse_factors(rest)
    inverses = []
    for top, low, bottom in zip(upper, below, lower):
        corner = -matmul(bottom, matmul(low, top, HIGHEST), HIGHEST)
        inverses.append(
            jnp.concatenate(
                [
                    jnp.concatenate([top, jnp.zeros((half, half), F32)], 1),
                    jnp.concatenate([corner, bottom], 1),
                ],
                0,
            )
        )
    gram_inverse, normal_inverse = inverses
    root = gram_inverse.T
    high, low = split(root)
    root_ref[:, :snaps] = high
    root_ref[:, snaps:] = low

    across = lambda matrix, vector: jnp.sum(matrix * vector, 1, keepdims=True)
    down = lambda matrix, vector: jnp.sum(matrix * vector, 0, keepdims=True)
    index = index_ref[...]
    state = jnp.where(index == jnp.max(index), 1.0, 0.0)
    eye = jnp.where(row == column, 1.0, 0.0)
    for n in range(STEPS):
        old = state
        right = down(eye, across(project, state)) + STEP_SIZE * load
        state = down(normal_inverse, across(normal_inverse, right))
        coeff_ref[n : n + 1, :] = down(root, across(gram, state))
    state_ref[0:1, :] = state - old
    state_ref[1:2, :] = state


def reduced_call(packed, step_index, place, parts, inverse_count):
    snaps = packed.shape[2]
    vmem = pl.BlockSpec(memory_space=pltpu.VMEM)
    return pl.pallas_call(
        functools.partial(reduced_kernel, parts, inverse_count),
        out_shape=(
            jax.ShapeDtypeStruct((snaps, 2 * snaps), BF16),
            jax.ShapeDtypeStruct((STEPS, snaps), F32),
            jax.ShapeDtypeStruct((2, snaps), F32),
        ),
        in_specs=[pl.BlockSpec(memory_space=pltpu.SMEM), vmem, vmem],
        out_specs=[vmem, vmem, vmem],
        compiler_params=pltpu.CompilerParams(vmem_limit_bytes=LIMIT),
        name="reduced",
    )(place, packed, step_index)


def basis_kernel(snap_ref, image_ref, force_ref, root_ref, state_ref, basis_ref, residual_ref):
    rows, snaps = snap_ref.shape
    block = force_ref.shape[1]
    snap = snap_ref[...]
    high, low = split(snap)
    both = matmul(high, root_ref[...])
    basis_ref[...] = both[:, :snaps] + both[:, snaps:] + matmul(low, root_ref[:, :snaps])
    sums = jnp.sum(snap * state_ref[0:1, :] + image_ref[...] * state_ref[1:2, :], 1, keepdims=True)
    lane = lax.broadcasted_iota(jnp.int32, (block, block), 1)
    tile = jnp.zeros((block, block), F32)
    for k in range(rows // block):
        tile = jnp.where(lane == k, sums[k * block : (k + 1) * block], tile)
    residual_ref[...] = tile.T[: rows // block] - STEP_SIZE * force_ref[...]


def basis_call(snapshots, image, force, root, state):
    rows, snaps = snapshots.shape
    block = force.shape[1]
    panel = pl.BlockSpec((CHUNK, snaps), lambda i: (i, 0))
    line = pl.BlockSpec((CHUNK // block, block), lambda i: (i, 0))
    return pl.pallas_call(
        basis_kernel,
        out_shape=(
            jax.ShapeDtypeStruct((rows, snaps), F32),
            jax.ShapeDtypeStruct((rows // block, block), F32),
        ),
        grid=(rows // CHUNK,),
        in_specs=[
            panel,
            panel,
            line,
            pl.BlockSpec((snaps, 2 * snaps), lambda i: (0, 0)),
            pl.BlockSpec((2, snaps), lambda i: (0, 0)),
        ],
        out_specs=[panel, line],
        compiler_params=pltpu.CompilerParams(vmem_limit_bytes=LIMIT),
        name="basis",
    )(snapshots, image, force, root, state)


def shifted(value, axis, steps):
    count = lax.axis_size(axis)
    pairs = [(source, (source + steps) % count) for source in range(count)]
    return lax.ppermute(value, axis, pairs)


def from_behind(shard, axis, by):
    devices = lax.axis_size(axis)
    pairs = [(i, i + by) for i in range(devices) if 0 <= i + by < devices]
    return lax.ppermute(shard, axis, pairs)


def partner(value, axis, bit):
    count = lax.axis_size(axis)
    return lax.ppermute(value, axis, [(i, i ^ bit) for i in range(count)])


def reduce_packed(value):
    zone_bits = lax.axis_size("zone").bit_length() - 1
    row_bits = lax.axis_size("rows").bit_length() - 1
    for bit in range(zone_bits):
        half = value.shape[0] // 2
        value = value[:half] + partner(value[half:], "zone", 1 << bit)
    for bit in range(row_bits):
        value = value + partner(value, "rows", 1 << bit)
    for bit in reversed(range(zone_bits)):
        value = jnp.concatenate([value, partner(value, "zone", 1 << bit)], 0)
    return value


def shards(snapshots, tangent, pattern, forcing, step_index):
    rows, snaps = snapshots.shape
    blocks = pattern.shape[0]
    block = rows // blocks
    edge = HALO * block
    parts = lax.axis_size("zone")
    inverse_count = 1.0 / (rows * lax.axis_size("rows") * parts)
    place = jnp.reshape(lax.axis_index("zone"), (1,)).astype(jnp.int32)
    force = forcing.reshape(blocks, block)
    head, tail = snapshots[:edge], snapshots[rows - edge :]
    halos = (
        shifted(tail, "rows", 1),
        shifted(head, "rows", -1),
        from_behind(tail, "zone", 1),
        from_behind(head, "zone", -1),
    )
    gram = gram_call(snapshots)
    image, packed = tangent_call(snapshots, halos, tangent, pattern, force, gram, place, parts)
    packed = reduce_packed(packed)
    root, coefficients, state = reduced_call(
        packed, step_index.reshape(1, snaps), place, parts, inverse_count
    )
    basis, residual = basis_call(snapshots, image, force, root, state)
    return basis, coefficients, residual.reshape(rows)


def solution(mesh):
    in_specs = (
        P(("rows", "zone"), None),
        P(("rows", "zone"), None),
        P(("rows", "zone"), None),
        P(("rows", "zone")),
        P(),
    )
    out_specs = (P(("rows", "zone"), None), P(), P(("rows", "zone")))
    return jax.shard_map(shards, mesh=mesh, in_specs=in_specs, out_specs=out_specs, check_vma=False)
```

time: 588 us -> 117 us (0.20)
  waiting for transfers between devices: 205 us -> 31.2 us
  matrix products: 119 us -> 0 us
  other arithmetic: 113 us -> 1.96 us
  local copies, waits for them, and re-layouts: 79.5 us -> 4.49 us
  Pallas kernels: 0 us -> 56.5 us
  blocking collectives: 40 us -> 0 us
  between operations: 17.5 us -> 0.71 us
  starting transfers between devices: 7.62 us -> 21.2 us
    psum x2 -> x0, waiting for transfers between devices: 205 us -> none  [the longest x1 127 us: shards(): gram_matrix = lax.psum(gram_local, ('rows', 'zone'))]
    dot_general x12 -> x0, matrix products: 113 us -> none  [the longest x1 25.2 us: tangent_product(): jnp.einsum('gbec,gecs->gbs', tile_blocks, picked, precision=highest)]
    another operation x22 -> x0, other arithmetic: 109 us -> none  [the longest x7 34.6 us: shards(): normal_low = jnp.linalg.cholesky(normal)]
    pallas_call x0 -> x4, Pallas kernels: none -> 56.5 us  [the longest x1 21 us: tangent_call(): pl.pallas_call(functools.partial(tangent_kernel, parts), out_shape=(jax.S...]
    psum x1 -> x0, blocking collectives: 40 us -> none  [shards(): lax.psum((jnp.dot(trial_basis.T, trial_basis, precision=highest) * invers...]
    reshape x2 -> x0, local copies, waits for them, and re-layouts: 24 us -> none  [the longest x1 12.5 us: tangent_product(): tangent.reshape(block_count, block_rows, coupled, block_rows)]
    ppermute x0 -> x7, waiting for transfers between devices: none -> 22.5 us  [partner(): return lax.ppermute(value, axis, [(i, i ^ bit) for i in range(count)])]
    gather x1 -> x0, local copies, waits for them, and re-layouts: 18.9 us -> none  [tangent_product(): picked = candidates[index_map]]
  transfers between devices with their start and end apart: 6 -> 11, of which waited for: 2 -> 9; matrix products, arithmetic and copies ran while one was open for 6% -> 1% of each run, Pallas kernels for 0% -> 7%
where the time goes in v1:
time: 117 us; the launch traced here: 116 us
  Pallas kernels  56.5 us (48%)
  waiting for transfers between devices  31.2 us (27%)
  starting transfers between devices  21.2 us (18%)
  local copies, waits for them, and re-layouts  4.49 us (4%)
  other arithmetic  1.96 us (2%)
    ppermute x7, waiting for transfers between devices, partner(): return lax.ppermute(value, axis, [(i, i ^ bit) for i in range(count)])  22.5 us
    pallas_call x1, Pallas kernels, tangent_call(): pl.pallas_call(functools.partial(tangent_kernel, parts), out_shape=(jax.S...  21 us
    pallas_call x1, Pallas kernels, reduced_call(): pl.pallas_call(functools.partial(reduced_kernel, parts, inverse_count), o...  14.1 us
    pallas_call x1, Pallas kernels, basis_call(): pl.pallas_call(basis_kernel, out_shape=(jax.ShapeDtypeStruct((rows, snaps...  13 us
    ppermute x7, starting transfers between devices, partner(): return lax.ppermute(value, axis, [(i, i ^ bit) for i in range(count)])  11.1 us
    ppermute x2, waiting for transfers between devices, shifted(): return lax.ppermute(value, axis, pairs)  8.61 us
    pallas_call x1, Pallas kernels, gram_call(): pl.pallas_call(gram_kernel, out_shape=jax.ShapeDtypeStruct((snaps, 2 * sn...  8.49 us
    ppermute x2, starting transfers between devices, shifted(): return lax.ppermute(value, axis, pairs)  6.12 us
  transfers between devices with their start and end apart: 11, of which 9 were waited for; matrix products, arithmetic and copies ran while one was open for 1% of the time, Pallas kernels for 7%

profile of v1, /device:TPU:0, one launch (start us, length us, event | category | flops | bytes accessed | tf_op | source)
XLA Modules:
  0.0 116.1 jit_solution(1078923326723181519)
XLA Ops:
  0.6 1.3 %fusion = (f32[512,256]{1,0:T(8,128)S(1)}, f32[512,256]{1,0:T(8,128)S(1)}) fusion(f32[8192,256]{1,0:T(8,128)} %snap_ref.3), kind=kLoop, calls=%fused_computation.4 | loop fusion | bytes 2097152 | tf_op jit(solution)/shard_map/slice | solution.py:430
  1.9 1.3 %collective-permute-start.3 = (f32[512,256]{1,0:T(8,128)S(1)}, f32[512,256]{1,0:T(8,128)S(1)}, u32[]{:S(2)}, u32[]{:S(2)}) collective-permute-start(f32[512,256]{1,0:T(8,128)S(1)} %get-tuple-element.17), channel_id=1, source_target_pairs={{1,0},{2,1},{3,2},{5,4},{6,5},{7,6},{9,8},{10,9},{11,10},{13,12},{... | collective-permute-start | bytes 1572872 | tf_op jit(solution)/shard_map/ppermute | solution.py:400
  3.2 6.1 %collective-permute-start.1 = (f32[512,256]{1,0:T(8,128)S(1)}, f32[512,256]{1,0:T(8,128)S(1)}, u32[]{:S(2)}, u32[]{:S(2)}) collective-permute-start(f32[512,256]{1,0:T(8,128)S(1)} %get-tuple-element.17), channel_id=1, source_target_pairs={{0,28},{4,0},{8,4},{12,8},{16,12},{20,16},{24,20},{28,24},{1,29},{... | collective-permute-start | bytes 1572872 | tf_op jit(solution)/shard_map/ppermute | solution.py:394
  9.3 2.8 %collective-permute-start.2 = (f32[512,256]{1,0:T(8,128)S(1)}, f32[512,256]{1,0:T(8,128)S(1)}, u32[]{:S(2)}, u32[]{:S(2)}) collective-permute-start(f32[512,256]{1,0:T(8,128)S(1)} %get-tuple-element.18), channel_id=1, source_target_pairs={{0,1},{1,2},{2,3},{4,5},{5,6},{6,7},{8,9},{9,10},{10,11},{12,13},{... | collective-permute-start | bytes 1572872 | tf_op jit(solution)/shard_map/ppermute | solution.py:400
  12.0 0.1 collective-permute-start
  12.1 1.4 %copy.8.pattern_ref = s32[64,4]{1,0:T(8,128)} copy(s32[64,4]{0,1:T(4,128)} %param.7) | data formatting | bytes 2048 | tf_op args[2]
  13.5 8.5 %gram.1.gram_ref = f32[256,512]{1,0:T(8,128)} custom-call(f32[8192,256]{1,0:T(8,128)} %snap_ref.3), custom_call_target="tpu_custom_call" | custom-call | flops 2147483648 | bytes 8388608 | tf_op jit(solution)/shard_map/gram/pallas_call | solution.py:58
  22.0 7.9 %collective-permute-done.1.next_any = f32[512,256]{1,0:T(8,128)S(1)} collective-permute-done((f32[512,256]{1,0:T(8,128)S(1)}, f32[512,256]{1,0:T(8,128)S(1)}, u32[]{:S(2)}, u32[]{:S(2)}) %collective-permute-start.1) | collective-permute-done | bytes 524320 | tf_op jit(solution)/shard_map/ppermute | solution.py:394
  29.9 0.7 collective-permute-done.prev_any
  30.6 0.1 copy-done.1
  30.7 0.2 copy-done.2
  30.8 0.6 copy-done.3
  31.4 21.0 %tangent.1 = (f32[8192,256]{1,0:T(8,128)}, f32[4,136,256]{2,1,0:T(8,128)}) custom-call(s32[64,4]{1,0:T(8,128)} %copy.8.pattern_ref, s32[1]{0:T(128)} %bitcast.place_ref, f32[8192,256]{1,0:T(8,128)} %snap_ref.3, f32[512,256]{1,0:T(8,128)} %copy-done.3, f32[512,256]{1,0:T(8,128)} %copy-done.1, f32[512,256]{1,0:T(8,128)} %copy-done.2, f32[512,256]{1,0:T(8,128)} %copy-done, ...), custom_call_target="tpu_custom_call" | custom-call | flops 9663676416 | bytes 25165824 | tf_op jit(solution)/shard_map/tangent/pallas_call | solution.py:189
  52.4 1.0 slice.21
  53.4 0.3 collective-permute-start.4
  53.7 1.3 %collective-permute-done.4 = f32[2,136,256]{2,1,0:T(8,128)S(1)} collective-permute-done((f32[2,136,256]{2,1,0:T(8,128)S(1)}, f32[2,136,256]{2,1,0:T(8,128)S(1)}, u32[]{:S(2)}, u32[]{:S(2)}) %collective-permute-start.4) | collective-permute-done | bytes 278560 | tf_op jit(solution)/shard_map/ppermute | solution.py:405
  55.0 1.0 slice_add_fusion
  56.0 2.2 %collective-permute-start.5 = (f32[1,136,256]{2,1,0:T(8,128)S(1)}, f32[1,136,256]{2,1,0:T(8,128)S(1)}, u32[]{:S(2)}, u32[]{:S(2)}) collective-permute-start(f32[1,136,256]{2,1,0:T(8,128)S(1)} %slice.25), channel_id=1, source_target_pairs={{0,2},{1,3},{2,0},{3,1},{4,6},{5,7},{6,4},{7,5},{8,10},{9,11},{10,... | collective-permute-start | bytes 417800 | tf_op jit(solution)/shard_map/ppermute | solution.py:405
  58.3 4.0 %collective-permute-done.5 = f32[1,136,256]{2,1,0:T(8,128)S(1)} collective-permute-done((f32[1,136,256]{2,1,0:T(8,128)S(1)}, f32[1,136,256]{2,1,0:T(8,128)S(1)}, u32[]{:S(2)}, u32[]{:S(2)}) %collective-permute-start.5) | collective-permute-done | bytes 139296 | tf_op jit(solution)/shard_map/ppermute | solution.py:405
  62.3 2.1 %collective-permute-start.6 = (f32[1,136,256]{2,1,0:T(8,128)S(1)}, f32[1,136,256]{2,1,0:T(8,128)S(1)}, u32[]{:S(2)}, u32[]{:S(2)}) collective-permute-start(f32[1,136,256]{2,1,0:T(8,128)S(1)} %slice_add_fusion.1), channel_id=1, source_target_pairs={{0,4},{4,0},{8,12},{12,8},{16,20},{20,16},{24,28},{28,24},{1,5},{5... | collective-permute-start | bytes 417800 | tf_op jit(solution)/shard_map/ppermute | solution.py:405
  64.4 3.1 %collective-permute-done.6 = f32[1,136,256]{2,1,0:T(8,128)S(1)} collective-permute-done((f32[1,136,256]{2,1,0:T(8,128)S(1)}, f32[1,136,256]{2,1,0:T(8,128)S(1)}, u32[]{:S(2)}, u32[]{:S(2)}) %collective-permute-start.6) | collective-permute-done | bytes 139296 | tf_op jit(solution)/shard_map/ppermute | solution.py:405
  67.6 1.7 %collective-permute-start.7 = (f32[1,136,256]{2,1,0:T(8,128)S(1)}, f32[1,136,256]{2,1,0:T(8,128)S(1)}, u32[]{:S(2)}, u32[]{:S(2)}) collective-permute-start(f32[1,136,256]{2,1,0:T(8,128)S(1)} %add.17), channel_id=1, source_target_pairs={{0,8},{4,12},{8,0},{12,4},{16,24},{20,28},{24,16},{28,20},{1,9},{5... | collective-permute-start | bytes 417800 | tf_op jit(solution)/shard_map/ppermute | solution.py:405
  69.2 3.5 %collective-permute-done.7 = f32[1,136,256]{2,1,0:T(8,128)S(1)} collective-permute-done((f32[1,136,256]{2,1,0:T(8,128)S(1)}, f32[1,136,256]{2,1,0:T(8,128)S(1)}, u32[]{:S(2)}, u32[]{:S(2)}) %collective-permute-start.7) | collective-permute-done | bytes 139296 | tf_op jit(solution)/shard_map/ppermute | solution.py:405
  72.7 4.0 %collective-permute-start.8 = (f32[1,136,256]{2,1,0:T(8,128)S(1)}, f32[1,136,256]{2,1,0:T(8,128)S(1)}, u32[]{:S(2)}, u32[]{:S(2)}) collective-permute-start(f32[1,136,256]{2,1,0:T(8,128)S(1)} %add.18), channel_id=1, source_target_pairs={{0,16},{4,20},{8,24},{12,28},{16,0},{20,4},{24,8},{28,12},{1,17},{... | collective-permute-start | bytes 417800 | tf_op jit(solution)/shard_map/ppermute | solution.py:405
  76.7 4.6 %collective-permute-done.8 = f32[1,136,256]{2,1,0:T(8,128)S(1)} collective-permute-done((f32[1,136,256]{2,1,0:T(8,128)S(1)}, f32[1,136,256]{2,1,0:T(8,128)S(1)}, u32[]{:S(2)}, u32[]{:S(2)}) %collective-permute-start.8) | collective-permute-done | bytes 139296 | tf_op jit(solution)/shard_map/ppermute | solution.py:405
  81.4 0.6 collective-permute-start.9
  82.0 4.5 %collective-permute-done.9 = f32[1,136,256]{2,1,0:T(8,128)S(1)} collective-permute-done((f32[1,136,256]{2,1,0:T(8,128)S(1)}, f32[1,136,256]{2,1,0:T(8,128)S(1)}, u32[]{:S(2)}, u32[]{:S(2)}) %collective-permute-start.9) | collective-permute-done | bytes 139296 | tf_op jit(solution)/shard_map/ppermute | solution.py:405
  86.5 0.1 collective-permute-start.10
  86.6 1.5 %collective-permute-done.10 = f32[2,136,256]{2,1,0:T(8,128)S(1)} collective-permute-done((f32[2,136,256]{2,1,0:T(8,128)S(1)}, f32[2,136,256]{2,1,0:T(8,128)S(1)}, u32[]{:S(2)}, u32[]{:S(2)}) %collective-permute-start.10) | collective-permute-done | bytes 278560 | tf_op jit(solution)/shard_map/ppermute | solution.py:405
  88.2 0.9 pad_maximum_fusion.pack_ref
  89.0 14.1 %reduced.1 = (bf16[256,512]{1,0:T(8,128)(2,1)}, f32[3,256]{1,0:T(4,128)}, f32[2,256]{1,0:T(2,128)}) custom-call(s32[1]{0:T(128)} %bitcast.place_ref, f32[4,136,256]{2,1,0:T(8,128)} %pad_maximum_fusion.pack_ref, s32[1,256]{1,0:T(1,128)} %bitcast.6), custom_call_target="tpu_custom_call" | custom-call | tf_op jit(solution)/shard_map/reduced/pallas_call | solution.py:337
  103.1 13.0 %basis.1 = (f32[8192,256]{1,0:T(8,128)}, f32[64,128]{1,0:T(8,128)}) custom-call(f32[8192,256]{1,0:T(8,128)} %snap_ref.3, f32[8192,256]{1,0:T(8,128)} %get-tuple-element.10.image_ref, f32[64,128]{1,0:T(8,128)} %bitcast.5, bf16[256,512]{1,0:T(8,128)(2,1)} %get-tuple-element.12.root_ref, f32[2,256]{1,0:T(2,128)} %get-tuple-element.13.state_ref), custom_call_target="tpu_custom_call" | custom-call | tf_op jit(solution)/shard_map/basis/pallas_call | solution.py:371
  (13 shorter events, 0.1 us)
Async XLA Ops:
  1.9 20.1 %collective-permute-start.3 = (f32[512,256]{1,0:T(8,128)S(1)}, f32[512,256]{1,0:T(8,128)S(1)}, u32[]{:S(2)}, u32[]{:S(2)}) collective-permute-start(f32[512,256]{1,0:T(8,128)S(1)} %get-tuple-element.17), channel_id=1, source_target_pairs={{1,0},{2,1},{3,2},{5,4},{6,5},{7,6},{9,8},{10,9},{11,10},{13,12},{... | collective-permute-start | bytes 1572872 | tf_op jit(solution)/shard_map/ppermute | solution.py:400
  3.2 26.7 %collective-permute-start.1 = (f32[512,256]{1,0:T(8,128)S(1)}, f32[512,256]{1,0:T(8,128)S(1)}, u32[]{:S(2)}, u32[]{:S(2)}) collective-permute-start(f32[512,256]{1,0:T(8,128)S(1)} %get-tuple-element.17), channel_id=1, source_target_pairs={{0,28},{4,0},{8,4},{12,8},{16,12},{20,16},{24,20},{28,24},{1,29},{... | collective-permute-start | bytes 1572872 | tf_op jit(solution)/shard_map/ppermute | solution.py:394
  9.3 20.6 %collective-permute-start.2 = (f32[512,256]{1,0:T(8,128)S(1)}, f32[512,256]{1,0:T(8,128)S(1)}, u32[]{:S(2)}, u32[]{:S(2)}) collective-permute-start(f32[512,256]{1,0:T(8,128)S(1)} %get-tuple-element.18), channel_id=1, source_target_pairs={{0,1},{1,2},{2,3},{4,5},{5,6},{6,7},{8,9},{9,10},{10,11},{12,13},{... | collective-permute-start | bytes 1572872 | tf_op jit(solution)/shard_map/ppermute | solution.py:400
  12.0 18.6 %collective-permute-start = (f32[512,256]{1,0:T(8,128)S(1)}, f32[512,256]{1,0:T(8,128)S(1)}, u32[]{:S(2)}, u32[]{:S(2)}) collective-permute-start(f32[512,256]{1,0:T(8,128)S(1)} %get-tuple-element.18), channel_id=1, source_target_pairs={{0,4},{4,8},{8,12},{12,16},{16,20},{20,24},{24,28},{28,0},{1,5},{5... | collective-permute-start | bytes 1572872 | tf_op jit(solution)/shard_map/ppermute | solution.py:394
  22.0 8.6 %copy-start = (f32[512,256]{1,0:T(8,128)}, f32[512,256]{1,0:T(8,128)S(1)}, u32[]{:S(2)}) copy-start(f32[512,256]{1,0:T(8,128)S(1)} %collective-permute-done.3.right_any) | copy-start | bytes 1572868
  29.9 0.8 copy-start.1
  29.9 1.0 copy-start.2
  30.6 0.8 copy-start.3
  53.4 1.6 %collective-permute-start.4 = (f32[2,136,256]{2,1,0:T(8,128)S(1)}, f32[2,136,256]{2,1,0:T(8,128)S(1)}, u32[]{:S(2)}, u32[]{:S(2)}) collective-permute-start(f32[2,136,256]{2,1,0:T(8,128)S(1)} %slice.21), channel_id=1, source_target_pairs={{0,1},{1,0},{2,3},{3,2},{4,5},{5,4},{6,7},{7,6},{8,9},{9,8},{10,11... | collective-permute-start | bytes 835592 | tf_op jit(solution)/shard_map/ppermute | solution.py:405
  56.0 6.2 %collective-permute-start.5 = (f32[1,136,256]{2,1,0:T(8,128)S(1)}, f32[1,136,256]{2,1,0:T(8,128)S(1)}, u32[]{:S(2)}, u32[]{:S(2)}) collective-permute-start(f32[1,136,256]{2,1,0:T(8,128)S(1)} %slice.25), channel_id=1, source_target_pairs={{0,2},{1,3},{2,0},{3,1},{4,6},{5,7},{6,4},{7,5},{8,10},{9,11},{10,... | collective-permute-start | bytes 417800 | tf_op jit(solution)/shard_map/ppermute | solution.py:405
  62.3 5.3 %collective-permute-start.6 = (f32[1,136,256]{2,1,0:T(8,128)S(1)}, f32[1,136,256]{2,1,0:T(8,128)S(1)}, u32[]{:S(2)}, u32[]{:S(2)}) collective-permute-start(f32[1,136,256]{2,1,0:T(8,128)S(1)} %slice_add_fusion.1), channel_id=1, source_target_pairs={{0,4},{4,0},{8,12},{12,8},{16,20},{20,16},{24,28},{28,24},{1,5},{5... | collective-permute-start | bytes 417800 | tf_op jit(solution)/shard_map/ppermute | solution.py:405
  67.6 5.1 %collective-permute-start.7 = (f32[1,136,256]{2,1,0:T(8,128)S(1)}, f32[1,136,256]{2,1,0:T(8,128)S(1)}, u32[]{:S(2)}, u32[]{:S(2)}) collective-permute-start(f32[1,136,256]{2,1,0:T(8,128)S(1)} %add.17), channel_id=1, source_target_pairs={{0,8},{4,12},{8,0},{12,4},{16,24},{20,28},{24,16},{28,20},{1,9},{5... | collective-permute-start | bytes 417800 | tf_op jit(solution)/shard_map/ppermute | solution.py:405
  72.7 8.7 %collective-permute-start.8 = (f32[1,136,256]{2,1,0:T(8,128)S(1)}, f32[1,136,256]{2,1,0:T(8,128)S(1)}, u32[]{:S(2)}, u32[]{:S(2)}) collective-permute-start(f32[1,136,256]{2,1,0:T(8,128)S(1)} %add.18), channel_id=1, source_target_pairs={{0,16},{4,20},{8,24},{12,28},{16,0},{20,4},{24,8},{28,12},{1,17},{... | collective-permute-start | bytes 417800 | tf_op jit(solution)/shard_map/ppermute | solution.py:405
  81.4 5.1 %collective-permute-start.9 = (f32[1,136,256]{2,1,0:T(8,128)S(1)}, f32[1,136,256]{2,1,0:T(8,128)S(1)}, u32[]{:S(2)}, u32[]{:S(2)}) collective-permute-start(f32[1,136,256]{2,1,0:T(8,128)S(1)} %add.19), channel_id=1, source_target_pairs={{0,2},{1,3},{2,0},{3,1},{4,6},{5,7},{6,4},{7,5},{8,10},{9,11},{10,... | collective-permute-start | bytes 417800 | tf_op jit(solution)/shard_map/ppermute | solution.py:405
  86.5 1.6 %collective-permute-start.10 = (f32[2,136,256]{2,1,0:T(8,128)S(1)}, f32[2,136,256]{2,1,0:T(8,128)S(1)}, u32[]{:S(2)}, u32[]{:S(2)}) collective-permute-start(f32[2,136,256]{2,1,0:T(8,128)S(1)} %pad_maximum_fusion.1), channel_id=1, source_target_pairs={{0,1},{1,0},{2,3},{3,2},{4,5},{5,4},{6,7},{7,6},{8,9},{9,8},{10,11... | collective-permute-start | bytes 835592 | tf_op jit(solution)/shard_map/ppermute | solution.py:405

commit v2 on v1

--- a/solution.py
+++ b/solution.py
@@ -82,7 +82,8 @@
     force_ref,
     gram_ref,
     image_ref,
-    pack_ref,
+    keep_ref,
+    send_ref,
     snap,
     halo,
     field,
@@ -90,6 +91,7 @@
     acc,
     cross,
     load,
+    packed,
     sems,
 ):
     step = pl.program_id(0)
@@ -166,17 +168,20 @@
         normal = acc[:, :snaps] + mixed + mixed.T
         row = lax.broadcasted_iota(jnp.int32, (snaps, snaps), 0)
         column = lax.broadcasted_iota(jnp.int32, (snaps, snaps), 1)
-        packed = jnp.where(row <= column, gram, normal)
         diagonal = jnp.sum(jnp.where(row == column, normal, 0.0), 0, keepdims=True)
+        packed[0] = jnp.where(row <= column, gram, normal)
+        packed[1] = project
         share = snaps // parts
         extra_row = lax.broadcasted_iota(jnp.int32, (8, snaps), 0)
         extra = jnp.where(extra_row == 0, load[...], jnp.where(extra_row == 1, diagonal, 0.0))
         bits = parts.bit_length() - 1
-        for c in range(parts):
-            at = reversed_bits(place_ref[0] ^ c, bits)
-            pack_ref[at, :share, :] = packed[c * share : (c + 1) * share]
-            pack_ref[at, share : 2 * share, :] = project[c * share : (c + 1) * share]
-            pack_ref[at, 2 * share :, :] = extra
+        for at in range(parts):
+            out = keep_ref if at < parts // 2 else send_ref
+            slot = at % (parts // 2)
+            start = pl.multiple_of((place_ref[0] ^ reversed_bits(at, bits)) * share, 8)
+            out[slot, :share, :] = packed[0, pl.ds(start, share), :]
+            out[slot, share : 2 * share, :] = packed[1, pl.ds(start, share), :]
+            out[slot, 2 * share :, :] = extra
 
 
 def tangent_call(snapshots, halos, tangent, pattern, force, gram, place, parts):
@@ -190,7 +195,8 @@
         functools.partial(tangent_kernel, parts),
         out_shape=(
             jax.ShapeDtypeStruct((rows, snaps), F32),
-            jax.ShapeDtypeStruct((parts, 2 * share + 8, snaps), F32),
+            jax.ShapeDtypeStruct((parts // 2, 2 * share + 8, snaps), F32),
+            jax.ShapeDtypeStruct((parts // 2, 2 * share + 8, snaps), F32),
         ),
         grid_spec=pltpu.PrefetchScalarGridSpec(
             num_scalar_prefetch=2,
@@ -207,7 +213,8 @@
             ],
             out_specs=[
                 pl.BlockSpec((CHUNK, snaps), lambda i, *_: (jnp.minimum(i, chunks - 1), 0)),
-                pl.BlockSpec((parts, 2 * share + 8, snaps), lambda i, *_: (0, 0, 0)),
+                pl.BlockSpec((parts // 2, 2 * share + 8, snaps), lambda i, *_: (0, 0, 0)),
+                pl.BlockSpec((parts // 2, 2 * share + 8, snaps), lambda i, *_: (0, 0, 0)),
             ],
             scratch_shapes=[
                 pltpu.VMEM((rows, snaps), F32),
@@ -217,6 +224,7 @@
                 pltpu.VMEM((snaps, 2 * snaps), F32),
                 pltpu.VMEM((snaps, snaps), F32),
                 pltpu.VMEM((1, snaps), F32),
+                pltpu.VMEM((2, snaps, snaps), F32),
                 pltpu.SemaphoreType.DMA((chunks + 4,)),
             ],
         ),
@@ -278,16 +286,16 @@
     )
 
 
-def reduced_kernel(parts, inverse_count, place_ref, pack_ref, index_ref, root_ref, coeff_ref, state_ref):
-    snaps = pack_ref.shape[2]
+def reduced_system(parts, inverse_count, place, pack, index):
+    snaps = pack.shape[2]
     share = snaps // parts
     half = snaps // 2
     bits = parts.bit_length() - 1
-    order = [reversed_bits(place_ref[0] ^ c, bits) for c in range(parts)]
-    packed = jnp.concatenate([pack_ref[at, :share, :] for at in order], 0) * inverse_count
-    project = jnp.concatenate([pack_ref[at, share : 2 * share, :] for at in order], 0) * inverse_count
-    load = pack_ref[order[0], 2 * share : 2 * share + 1, :] * inverse_count
-    diagonal = pack_ref[order[0], 2 * share + 1 : 2 * share + 2, :] * inverse_count
+    order = [reversed_bits(place ^ c, bits) for c in range(parts)]
+    packed = jnp.concatenate([pack[at, :share, :] for at in order], 0) * inverse_count
+    project = jnp.concatenate([pack[at, share : 2 * share, :] for at in order], 0) * inverse_count
+    load = pack[order[0], 2 * share : 2 * share + 1, :] * inverse_count
+    diagonal = pack[order[0], 2 * share + 1 : 2 * share + 2, :] * inverse_count
     row = lax.broadcasted_iota(jnp.int32, (snaps, snaps), 0)
     column = lax.broadcasted_iota(jnp.int32, (snaps, snaps), 1)
     turned = packed.T
@@ -313,79 +321,101 @@
         )
     gram_inverse, normal_inverse = inverses
     root = gram_inverse.T
+
+    across = lambda matrix, vector: jnp.sum(matrix * vector, 1, keepdims=True)
+    down = lambda matrix, vector: jnp.sum(matrix * vector, 0, keepdims=True)
+    state = jnp.where(index == jnp.max(index), 1.0, 0.0)
+    eye = jnp.where(row == column, 1.0, 0.0)
+    history = []
+    for _ in range(STEPS):
+        old = state
+        right = down(eye, across(project, state)) + STEP_SIZE * load
+        state = down(normal_inverse, across(normal_inverse, right))
+        history.append(down(root, across(gram, state)))
+    return root, history, state - old, state
+
+
+def final_kernel(parts, inverse_count, count, place_ref, *refs):
+    pieces = refs[:count]
+    index_ref, force_ref, snap_any, image_any, basis_any, coeff_ref, residual_ref = refs[count : count + 7]
+    snap, image, pack, root_ref, change_ref, state_ref, sems = refs[count + 7 :]
+    rows, snaps = snap.shape
+    block = force_ref.shape[1]
+    chunks = rows // CHUNK
+    per_chunk = CHUNK // block
+    copies = [
+        pltpu.make_async_copy(snap_any, snap, sems.at[0]),
+        pltpu.make_async_copy(image_any, image, sems.at[1]),
+    ]
+    for copy in copies:
+        copy.start()
+    first = 0
+    for piece in pieces:
+        pack[first : first + piece.shape[0]] = piece[...]
+        first += piece.shape[0]
+    root, history, change, state = reduced_system(parts, inverse_count, place_ref[0], pack, index_ref[...])
     high, low = split(root)
     root_ref[:, :snaps] = high
     root_ref[:, snaps:] = low
-
-    across = lambda matrix, vector: jnp.sum(matrix * vector, 1, keepdims=True)
-    down = lambda matrix, vector: jnp.sum(matrix * vector, 0, keepdims=True)
-    index = index_ref[...]
-    state = jnp.where(index == jnp.max(index), 1.0, 0.0)
-    eye = jnp.where(row == column, 1.0, 0.0)
     for n in range(STEPS):
-        old = state
-        right = down(eye, across(project, state)) + STEP_SIZE * load
-        state = down(normal_inverse, across(normal_inverse, right))
-        coeff_ref[n : n + 1, :] = down(root, across(gram, state))
-    state_ref[0:1, :] = state - old
-    state_ref[1:2, :] = state
-
-
-def reduced_call(packed, step_index, place, parts, inverse_count):
-    snaps = packed.shape[2]
+        coeff_ref[n : n + 1, :] = history[n]
+    change_ref[...] = change
+    state_ref[...] = state
+    for copy in copies:
+        copy.wait()
+
+    lane = lax.broadcasted_iota(jnp.int32, (block, block), 1)
+
+    def out_copy(i):
+        at = pl.ds(pl.multiple_of(i * CHUNK, CHUNK), CHUNK)
+        return pltpu.make_async_copy(snap.at[at, :], basis_any.at[at, :], sems.at[2 + i])
+
+    @pl.loop(0, chunks)
+    def _(i):
+        at = pl.ds(pl.multiple_of(i * CHUNK, CHUNK), CHUNK)
+        panel = snap[at, :]
+        sums = jnp.sum(panel * change_ref[...] + image[at, :] * state_ref[...], 1, keepdims=True)
+        tile = jnp.zeros((block, block), F32)
+        for k in range(per_chunk):
+            tile = jnp.where(lane == k, sums[k * block : (k + 1) * block], tile)
+        line = pl.ds(pl.multiple_of(i * per_chunk, per_chunk), per_chunk)
+        residual_ref[line, :] = tile.T[:per_chunk] - STEP_SIZE * force_ref[line, :]
+        panel_high, panel_low = split(panel)
+        both = matmul(panel_high, root_ref[...])
+        snap[at, :] = both[:, :snaps] + both[:, snaps:] + matmul(panel_low, root_ref[:, :snaps])
+        out_copy(i).start()
+
+    @pl.loop(0, chunks)
+    def _(i):
+        out_copy(i).wait()
+
+
+def final_call(pieces, step_index, place, snapshots, image, force, inverse_count):
+    rows, snaps = snapshots.shape
+    parts = sum(piece.shape[0] for piece in pieces)
     vmem = pl.BlockSpec(memory_space=pltpu.VMEM)
+    hbm = pl.BlockSpec(memory_space=pl.ANY)
     return pl.pallas_call(
-        functools.partial(reduced_kernel, parts, inverse_count),
-        out_shape=(
-            jax.ShapeDtypeStruct((snaps, 2 * snaps), BF16),
-            jax.ShapeDtypeStruct((STEPS, snaps), F32),
-            jax.ShapeDtypeStruct((2, snaps), F32),
-        ),
-        in_specs=[pl.BlockSpec(memory_space=pltpu.SMEM), vmem, vmem],
-        out_specs=[vmem, vmem, vmem],
-        compiler_params=pltpu.CompilerParams(vmem_limit_bytes=LIMIT),
-        name="reduced",
-    )(place, packed, step_index)
-
-
-def basis_kernel(snap_ref, image_ref, force_ref, root_ref, state_ref, basis_ref, residual_ref):
-    rows, snaps = snap_ref.shape
-    block = force_ref.shape[1]
-    snap = snap_ref[...]
-    high, low = split(snap)
-    both = matmul(high, root_ref[...])
-    basis_ref[...] = both[:, :snaps] + both[:, snaps:] + matmul(low, root_ref[:, :snaps])
-    sums = jnp.sum(snap * state_ref[0:1, :] + image_ref[...] * state_ref[1:2, :], 1, keepdims=True)
-    lane = lax.broadcasted_iota(jnp.int32, (block, block), 1)
-    tile = jnp.zeros((block, block), F32)
-    for k in range(rows // block):
-        tile = jnp.where(lane == k, sums[k * block : (k + 1) * block], tile)
-    residual_ref[...] = tile.T[: rows // block] - STEP_SIZE * force_ref[...]
-
-
-def basis_call(snapshots, image, force, root, state):
-    rows, snaps = snapshots.shape
-    block = force.shape[1]
-    panel = pl.BlockSpec((CHUNK, snaps), lambda i: (i, 0))
-    line = pl.BlockSpec((CHUNK // block, block), lambda i: (i, 0))
-    return pl.pallas_call(
-        basis_kernel,
+        functools.partial(final_kernel, parts, inverse_count, len(pieces)),
         out_shape=(
             jax.ShapeDtypeStruct((rows, snaps), F32),
-            jax.ShapeDtypeStruct((rows // block, block), F32),
+            jax.ShapeDtypeStruct((STEPS, snaps), F32),
+            jax.ShapeDtypeStruct(force.shape, F32),
         ),
-        grid=(rows // CHUNK,),
-        in_specs=[
-            panel,
-            panel,
-            line,
-            pl.BlockSpec((snaps, 2 * snaps), lambda i: (0, 0)),
-            pl.BlockSpec((2, snaps), lambda i: (0, 0)),
+        in_specs=[pl.BlockSpec(memory_space=pltpu.SMEM)] + [vmem] * (len(pieces) + 2) + [hbm, hbm],
+        out_specs=[hbm, vmem, vmem],
+        scratch_shapes=[
+            pltpu.VMEM((rows, snaps), F32),
+            pltpu.VMEM((rows, snaps), F32),
+            pltpu.VMEM((parts,) + pieces[0].shape[1:], F32),
+            pltpu.VMEM((snaps, 2 * snaps), BF16),
+            pltpu.VMEM((1, snaps), F32),
+            pltpu.VMEM((1, snaps), F32),
+            pltpu.SemaphoreType.DMA((2 + rows // CHUNK,)),
         ],
-        out_specs=[panel, line],
         compiler_params=pltpu.CompilerParams(vmem_limit_bytes=LIMIT),
-        name="basis",
-    )(snapshots, image, force, root, state)
+        name="final",
+    )(place, *pieces, step_index, force, snapshots, image)
 
 
 def shifted(value, axis, steps):
@@ -405,17 +435,19 @@
     return lax.ppermute(value, axis, [(i, i ^ bit) for i in range(count)])
 
 
-def reduce_packed(value):
+def reduce_packed(keep, send):
     zone_bits = lax.axis_size("zone").bit_length() - 1
     row_bits = lax.axis_size("rows").bit_length() - 1
-    for bit in range(zone_bits):
+    value = keep + partner(send, "zone", 1)
+    for bit in range(1, zone_bits):
         half = value.shape[0] // 2
         value = value[:half] + partner(value[half:], "zone", 1 << bit)
     for bit in range(row_bits):
         value = value + partner(value, "rows", 1 << bit)
+    pieces = [value]
     for bit in reversed(range(zone_bits)):
-        value = jnp.concatenate([value, partner(value, "zone", 1 << bit)], 0)
-    return value
+        pieces += [partner(piece, "zone", 1 << bit) for piece in pieces]
+    return pieces
 
 
 def shards(snapshots, tangent, pattern, forcing, step_index):
@@ -435,12 +467,11 @@
         from_behind(head, "zone", -1),
     )
     gram = gram_call(snapshots)
-    image, packed = tangent_call(snapshots, halos, tangent, pattern, force, gram, place, parts)
-    packed = reduce_packed(packed)
-    root, coefficients, state = reduced_call(
-        packed, step_index.reshape(1, snaps), place, parts, inverse_count
+    image, keep, send = tangent_call(snapshots, halos, tangent, pattern, force, gram, place, parts)
+    pieces = reduce_packed(keep, send)
+    basis, coefficients, residual = final_call(
+        pieces, step_index.reshape(1, snaps), place, snapshots, image, force, inverse_count
     )
-    basis, residual = basis_call(snapshots, image, force, root, state)
     return basis, coefficients, residual.reshape(rows)
 
 

time: 117 us -> 114 us (0.974)
  Pallas kernels: 56.5 us -> 54.8 us
    pallas_call x2 -> x1, Pallas kernels: 27.1 us -> 25.3 us  [final_call(): pl.pallas_call(functools.partial(final_kernel, parts, inverse_count, len(...]
    unnamed x9 -> x17, local copies, waits for them, and re-layouts: 2.23 us -> 2.84 us
    ppermute x7 -> x8, starting transfers between devices: 11.1 us -> 11 us  [partner(): return lax.ppermute(value, axis, [(i, i ^ bit) for i in range(count)])]
    ppermute x7 -> x8, waiting for transfers between devices: 22.5 us -> 22.5 us  [partner(): return lax.ppermute(value, axis, [(i, i ^ bit) for i in range(count)])]
  transfers between devices with their start and end apart: 11 -> 12, of which waited for: 9 -> 9; matrix products, arithmetic and copies ran while one was open for 1% -> 1% of each run, Pallas kernels for 7% -> 8%
where the time goes in v2:
time: 114 us; the launch traced here: 113 us
  Pallas kernels  54.8 us (48%)
  waiting for transfers between devices  31.1 us (27%)
  starting transfers between devices  21.2 us (19%)
  local copies, waits for them, and re-layouts  4.12 us (4%)
    pallas_call x1, Pallas kernels, final_call(): pl.pallas_call(functools.partial(final_kernel, parts, inverse_count, len(...  25.3 us
    ppermute x8, waiting for transfers between devices, partner(): return lax.ppermute(value, axis, [(i, i ^ bit) for i in range(count)])  22.5 us
    pallas_call x1, Pallas kernels, tangent_call(): pl.pallas_call(functools.partial(tangent_kernel, parts), out_shape=(jax.S...  21 us
    ppermute x8, starting transfers between devices, partner(): return lax.ppermute(value, axis, [(i, i ^ bit) for i in range(count)])  11 us
    ppermute x2, waiting for transfers between devices, shifted(): return lax.ppermute(value, axis, pairs)  8.57 us
    pallas_call x1, Pallas kernels, gram_call(): pl.pallas_call(gram_kernel, out_shape=jax.ShapeDtypeStruct((snaps, 2 * sn...  8.52 us
    ppermute x2, starting transfers between devices, shifted(): return lax.ppermute(value, axis, pairs)  6.12 us
    ppermute x2, starting transfers between devices, from_behind(): return lax.ppermute(shard, axis, pairs)  4.06 us
  transfers between devices with their start and end apart: 12, of which 9 were waited for; matrix products, arithmetic and copies ran while one was open for 1% of the time, Pallas kernels for 8%

profile of v2, /device:TPU:0, one launch (start us, length us, event | category | flops | bytes accessed | tf_op | source)
XLA Modules:
  0.0 113.2 jit_solution(16485083405168511)
XLA Ops:
  0.6 1.3 %fusion = (f32[512,256]{1,0:T(8,128)S(1)}, f32[512,256]{1,0:T(8,128)S(1)}) fusion(f32[8192,256]{1,0:T(8,128)} %refs_6_.1), kind=kLoop, calls=%fused_computation.1 | loop fusion | bytes 2097152 | tf_op jit(solution)/shard_map/slice | solution.py:462
  1.9 1.3 %collective-permute-start.3 = (f32[512,256]{1,0:T(8,128)S(1)}, f32[512,256]{1,0:T(8,128)S(1)}, u32[]{:S(2)}, u32[]{:S(2)}) collective-permute-start(f32[512,256]{1,0:T(8,128)S(1)} %get-tuple-element.15), channel_id=1, source_target_pairs={{1,0},{2,1},{3,2},{5,4},{6,5},{7,6},{9,8},{10,9},{11,10},{13,12},{... | collective-permute-start | bytes 1572872 | tf_op jit(solution)/shard_map/ppermute | solution.py:430
  3.2 6.1 %collective-permute-start.1 = (f32[512,256]{1,0:T(8,128)S(1)}, f32[512,256]{1,0:T(8,128)S(1)}, u32[]{:S(2)}, u32[]{:S(2)}) collective-permute-start(f32[512,256]{1,0:T(8,128)S(1)} %get-tuple-element.15), channel_id=1, source_target_pairs={{0,28},{4,0},{8,4},{12,8},{16,12},{20,16},{24,20},{28,24},{1,29},{... | collective-permute-start | bytes 1572872 | tf_op jit(solution)/shard_map/ppermute | solution.py:424
  9.3 2.8 %collective-permute-start.2 = (f32[512,256]{1,0:T(8,128)S(1)}, f32[512,256]{1,0:T(8,128)S(1)}, u32[]{:S(2)}, u32[]{:S(2)}) collective-permute-start(f32[512,256]{1,0:T(8,128)S(1)} %get-tuple-element.16), channel_id=1, source_target_pairs={{0,1},{1,2},{2,3},{4,5},{5,6},{6,7},{8,9},{9,10},{10,11},{12,13},{... | collective-permute-start | bytes 1572872 | tf_op jit(solution)/shard_map/ppermute | solution.py:430
  12.0 0.1 collective-permute-start
  12.1 1.4 %copy.8.pattern_ref = s32[64,4]{1,0:T(8,128)} copy(s32[64,4]{0,1:T(4,128)} %param.7) | data formatting | bytes 2048 | tf_op args[2]
  13.5 8.5 %gram.1.gram_ref = f32[256,512]{1,0:T(8,128)} custom-call(f32[8192,256]{1,0:T(8,128)} %refs_6_.1), custom_call_target="tpu_custom_call" | custom-call | flops 2147483648 | bytes 8388608 | tf_op jit(solution)/shard_map/gram/pallas_call | solution.py:58
  22.0 0.0 collective-permute-done.3.right_any
  22.0 7.9 %collective-permute-done.1.next_any = f32[512,256]{1,0:T(8,128)S(1)} collective-permute-done((f32[512,256]{1,0:T(8,128)S(1)}, f32[512,256]{1,0:T(8,128)S(1)}, u32[]{:S(2)}, u32[]{:S(2)}) %collective-permute-start.1) | collective-permute-done | bytes 524320 | tf_op jit(solution)/shard_map/ppermute | solution.py:424
  29.9 0.0 collective-permute-done.2.left_any
  29.9 0.7 collective-permute-done.prev_any
  30.6 0.1 copy-done.5
  30.7 0.2 copy-done.6
  30.9 0.5 copy-done.7
  31.4 21.0 %tangent.1 = (f32[8192,256]{1,0:T(8,128)}, f32[2,136,256]{2,1,0:T(8,128)}, f32[2,136,256]{2,1,0:T(8,128)}) custom-call(s32[64,4]{1,0:T(8,128)} %copy.8.pattern_ref, s32[1]{0:T(128)} %bitcast.place_ref, f32[8192,256]{1,0:T(8,128)} %refs_6_.1, f32[512,256]{1,0:T(8,128)} %copy-done.7, f32[512,256]{1,0:T(8,128)} %copy-done.5, f32[512,256]{1,0:T(8,128)} %copy-done.6, ...), custom_call_target="tpu_custom_call" | custom-call | flops 9663676416 | bytes 25165824 | tf_op jit(solution)/shard_map/tangent/pallas_call | solution.py:194
  52.4 0.3 collective-permute-start.4
  52.7 1.5 %collective-permute-done.4 = f32[2,136,256]{2,1,0:T(8,128)S(1)} collective-permute-done((f32[2,136,256]{2,1,0:T(8,128)}, f32[2,136,256]{2,1,0:T(8,128)S(1)}, u32[]{:S(2)}, u32[]{:S(2)}) %collective-permute-start.4) | collective-permute-done | bytes 278560 | tf_op jit(solution)/shard_map/ppermute | solution.py:435
  54.2 1.0 add.15
  55.3 2.2 %collective-permute-start.5 = (f32[1,136,256]{2,1,0:T(8,128)S(1)}, f32[1,136,256]{2,1,0:T(8,128)S(1)}, u32[]{:S(2)}, u32[]{:S(2)}) collective-permute-start(f32[1,136,256]{2,1,0:T(8,128)S(1)} %slice.17), channel_id=1, source_target_pairs={{0,2},{1,3},{2,0},{3,1},{4,6},{5,7},{6,4},{7,5},{8,10},{9,11},{10,... | collective-permute-start | bytes 417800 | tf_op jit(solution)/shard_map/ppermute | solution.py:435
  57.5 4.0 %collective-permute-done.5 = f32[1,136,256]{2,1,0:T(8,128)S(1)} collective-permute-done((f32[1,136,256]{2,1,0:T(8,128)S(1)}, f32[1,136,256]{2,1,0:T(8,128)S(1)}, u32[]{:S(2)}, u32[]{:S(2)}) %collective-permute-start.5) | collective-permute-done | bytes 139296 | tf_op jit(solution)/shard_map/ppermute | solution.py:435
  61.5 2.1 %collective-permute-start.6 = (f32[1,136,256]{2,1,0:T(8,128)S(1)}, f32[1,136,256]{2,1,0:T(8,128)S(1)}, u32[]{:S(2)}, u32[]{:S(2)}) collective-permute-start(f32[1,136,256]{2,1,0:T(8,128)S(1)} %slice_add_fusion), channel_id=1, source_target_pairs={{0,4},{4,0},{8,12},{12,8},{16,20},{20,16},{24,28},{28,24},{1,5},{5... | collective-permute-start | bytes 417800 | tf_op jit(solution)/shard_map/ppermute | solution.py:435
  63.6 3.1 %collective-permute-done.6 = f32[1,136,256]{2,1,0:T(8,128)S(1)} collective-permute-done((f32[1,136,256]{2,1,0:T(8,128)S(1)}, f32[1,136,256]{2,1,0:T(8,128)S(1)}, u32[]{:S(2)}, u32[]{:S(2)}) %collective-permute-start.6) | collective-permute-done | bytes 139296 | tf_op jit(solution)/shard_map/ppermute | solution.py:435
  66.8 1.7 %collective-permute-start.7 = (f32[1,136,256]{2,1,0:T(8,128)S(1)}, f32[1,136,256]{2,1,0:T(8,128)S(1)}, u32[]{:S(2)}, u32[]{:S(2)}) collective-permute-start(f32[1,136,256]{2,1,0:T(8,128)S(1)} %add.17), channel_id=1, source_target_pairs={{0,8},{4,12},{8,0},{12,4},{16,24},{20,28},{24,16},{28,20},{1,9},{5... | collective-permute-start | bytes 417800 | tf_op jit(solution)/shard_map/ppermute | solution.py:435
  68.5 3.4 %collective-permute-done.7 = f32[1,136,256]{2,1,0:T(8,128)S(1)} collective-permute-done((f32[1,136,256]{2,1,0:T(8,128)S(1)}, f32[1,136,256]{2,1,0:T(8,128)S(1)}, u32[]{:S(2)}, u32[]{:S(2)}) %collective-permute-start.7) | collective-permute-done | bytes 139296 | tf_op jit(solution)/shard_map/ppermute | solution.py:435
  71.9 4.0 %collective-permute-start.8 = (f32[1,136,256]{2,1,0:T(8,128)S(1)}, f32[1,136,256]{2,1,0:T(8,128)S(1)}, u32[]{:S(2)}, u32[]{:S(2)}) collective-permute-start(f32[1,136,256]{2,1,0:T(8,128)S(1)} %add.18), channel_id=1, source_target_pairs={{0,16},{4,20},{8,24},{12,28},{16,0},{20,4},{24,8},{28,12},{1,17},{... | collective-permute-start | bytes 417800 | tf_op jit(solution)/shard_map/ppermute | solution.py:435
  76.0 4.6 %collective-permute-done.8 = f32[1,136,256]{2,1,0:T(8,128)S(1)} collective-permute-done((f32[1,136,256]{2,1,0:T(8,128)S(1)}, f32[1,136,256]{2,1,0:T(8,128)S(1)}, u32[]{:S(2)}, u32[]{:S(2)}) %collective-permute-start.8) | collective-permute-done | bytes 139296 | tf_op jit(solution)/shard_map/ppermute | solution.py:435
  80.6 0.7 collective-permute-start.9
  81.3 0.0 collective-permute-start.10
  81.3 4.5 %collective-permute-done.9.refs_1_ = f32[1,136,256]{2,1,0:T(8,128)S(1)} collective-permute-done((f32[1,136,256]{2,1,0:T(8,128)S(1)}, f32[1,136,256]{2,1,0:T(8,128)S(1)}, u32[]{:S(2)}, u32[]{:S(2)}) %collective-permute-start.9) | collective-permute-done | bytes 139296 | tf_op jit(solution)/shard_map/ppermute | solution.py:435
  85.8 1.3 %collective-permute-done.11.refs_3_ = f32[1,136,256]{2,1,0:T(8,128)S(1)} collective-permute-done((f32[1,136,256]{2,1,0:T(8,128)S(1)}, f32[1,136,256]{2,1,0:T(8,128)S(1)}, u32[]{:S(2)}, u32[]{:S(2)}) %collective-permute-start.11) | collective-permute-done | bytes 139296 | tf_op jit(solution)/shard_map/ppermute | solution.py:435
  87.1 0.6 copy-done.3
  87.8 25.3 %final.1 = (f32[8192,256]{1,0:T(8,128)}, f32[3,256]{1,0:T(4,128)}, f32[64,128]{1,0:T(8,128)}) custom-call(s32[1]{0:T(128)} %bitcast.place_ref, f32[1,136,256]{2,1,0:T(8,128)} %copy-done, f32[1,136,256]{2,1,0:T(8,128)} %copy-done.1, f32[1,136,256]{2,1,0:T(8,128)} %copy-done.2, f32[1,136,256]{2,1,0:T(8,128)} %copy-done.3, s32[1,256]{1,0:T(1,128)} %bitcast.6, ...), custom_call_target="tpu_custom_call" | custom-call | tf_op jit(solution)/shard_map/final/pallas_call | solution.py:398
  (19 shorter events, 0.1 us)
Async XLA Ops:
  1.9 20.1 %collective-permute-start.3 = (f32[512,256]{1,0:T(8,128)S(1)}, f32[512,256]{1,0:T(8,128)S(1)}, u32[]{:S(2)}, u32[]{:S(2)}) collective-permute-start(f32[512,256]{1,0:T(8,128)S(1)} %get-tuple-element.15), channel_id=1, source_target_pairs={{1,0},{2,1},{3,2},{5,4},{6,5},{7,6},{9,8},{10,9},{11,10},{13,12},{... | collective-permute-start | bytes 1572872 | tf_op jit(solution)/shard_map/ppermute | solution.py:430
  3.2 26.7 %collective-permute-start.1 = (f32[512,256]{1,0:T(8,128)S(1)}, f32[512,256]{1,0:T(8,128)S(1)}, u32[]{:S(2)}, u32[]{:S(2)}) collective-permute-start(f32[512,256]{1,0:T(8,128)S(1)} %get-tuple-element.15), channel_id=1, source_target_pairs={{0,28},{4,0},{8,4},{12,8},{16,12},{20,16},{24,20},{28,24},{1,29},{... | collective-permute-start | bytes 1572872 | tf_op jit(solution)/shard_map/ppermute | solution.py:424
  9.3 20.6 %collective-permute-start.2 = (f32[512,256]{1,0:T(8,128)S(1)}, f32[512,256]{1,0:T(8,128)S(1)}, u32[]{:S(2)}, u32[]{:S(2)}) collective-permute-start(f32[512,256]{1,0:T(8,128)S(1)} %get-tuple-element.16), channel_id=1, source_target_pairs={{0,1},{1,2},{2,3},{4,5},{5,6},{6,7},{8,9},{9,10},{10,11},{12,13},{... | collective-permute-start | bytes 1572872 | tf_op jit(solution)/shard_map/ppermute | solution.py:430
  12.0 18.6 %collective-permute-start = (f32[512,256]{1,0:T(8,128)S(1)}, f32[512,256]{1,0:T(8,128)S(1)}, u32[]{:S(2)}, u32[]{:S(2)}) collective-permute-start(f32[512,256]{1,0:T(8,128)S(1)} %get-tuple-element.16), channel_id=1, source_target_pairs={{0,4},{4,8},{8,12},{12,16},{16,20},{20,24},{24,28},{28,0},{1,5},{5... | collective-permute-start | bytes 1572872 | tf_op jit(solution)/shard_map/ppermute | solution.py:424
  22.0 8.6 %copy-start.4 = (f32[512,256]{1,0:T(8,128)}, f32[512,256]{1,0:T(8,128)S(1)}, u32[]{:S(2)}) copy-start(f32[512,256]{1,0:T(8,128)S(1)} %collective-permute-done.3.right_any) | copy-start | bytes 1572868
  29.9 0.9 copy-start.5
  29.9 1.1 copy-start.6
  30.6 0.8 copy-start.7
  52.4 1.8 %collective-permute-start.4 = (f32[2,136,256]{2,1,0:T(8,128)}, f32[2,136,256]{2,1,0:T(8,128)S(1)}, u32[]{:S(2)}, u32[]{:S(2)}) collective-permute-start(f32[2,136,256]{2,1,0:T(8,128)} %get-tuple-element.10), channel_id=1, source_target_pairs={{0,1},{1,0},{2,3},{3,2},{4,5},{5,4},{6,7},{7,6},{8,9},{9,8},{10,11... | collective-permute-start | bytes 835592 | tf_op jit(solution)/shard_map/ppermute | solution.py:435
  55.3 6.2 %collective-permute-start.5 = (f32[1,136,256]{2,1,0:T(8,128)S(1)}, f32[1,136,256]{2,1,0:T(8,128)S(1)}, u32[]{:S(2)}, u32[]{:S(2)}) collective-permute-start(f32[1,136,256]{2,1,0:T(8,128)S(1)} %slice.17), channel_id=1, source_target_pairs={{0,2},{1,3},{2,0},{3,1},{4,6},{5,7},{6,4},{7,5},{8,10},{9,11},{10,... | collective-permute-start | bytes 417800 | tf_op jit(solution)/shard_map/ppermute | solution.py:435
  61.5 5.3 %collective-permute-start.6 = (f32[1,136,256]{2,1,0:T(8,128)S(1)}, f32[1,136,256]{2,1,0:T(8,128)S(1)}, u32[]{:S(2)}, u32[]{:S(2)}) collective-permute-start(f32[1,136,256]{2,1,0:T(8,128)S(1)} %slice_add_fusion), channel_id=1, source_target_pairs={{0,4},{4,0},{8,12},{12,8},{16,20},{20,16},{24,28},{28,24},{1,5},{5... | collective-permute-start | bytes 417800 | tf_op jit(solution)/shard_map/ppermute | solution.py:435
  66.8 5.1 %collective-permute-start.7 = (f32[1,136,256]{2,1,0:T(8,128)S(1)}, f32[1,136,256]{2,1,0:T(8,128)S(1)}, u32[]{:S(2)}, u32[]{:S(2)}) collective-permute-start(f32[1,136,256]{2,1,0:T(8,128)S(1)} %add.17), channel_id=1, source_target_pairs={{0,8},{4,12},{8,0},{12,4},{16,24},{20,28},{24,16},{28,20},{1,9},{5... | collective-permute-start | bytes 417800 | tf_op jit(solution)/shard_map/ppermute | solution.py:435
  71.9 8.7 %collective-permute-start.8 = (f32[1,136,256]{2,1,0:T(8,128)S(1)}, f32[1,136,256]{2,1,0:T(8,128)S(1)}, u32[]{:S(2)}, u32[]{:S(2)}) collective-permute-start(f32[1,136,256]{2,1,0:T(8,128)S(1)} %add.18), channel_id=1, source_target_pairs={{0,16},{4,20},{8,24},{12,28},{16,0},{20,4},{24,8},{28,12},{1,17},{... | collective-permute-start | bytes 417800 | tf_op jit(solution)/shard_map/ppermute | solution.py:435
  80.6 6.5 %copy-start = (f32[1,136,256]{2,1,0:T(8,128)}, f32[1,136,256]{2,1,0:T(8,128)S(1)}, u32[]{:S(2)}) copy-start(f32[1,136,256]{2,1,0:T(8,128)S(1)} %add.19.refs_0_) | copy-start | bytes 417796
  80.6 5.1 %collective-permute-start.9 = (f32[1,136,256]{2,1,0:T(8,128)S(1)}, f32[1,136,256]{2,1,0:T(8,128)S(1)}, u32[]{:S(2)}, u32[]{:S(2)}) collective-permute-start(f32[1,136,256]{2,1,0:T(8,128)S(1)} %add.19.refs_0_), channel_id=1, source_target_pairs={{0,2},{1,3},{2,0},{3,1},{4,6},{5,7},{6,4},{7,5},{8,10},{9,11},{10,... | collective-permute-start | bytes 417800 | tf_op jit(solution)/shard_map/ppermute | solution.py:435
  81.3 4.5 %collective-permute-start.10 = (f32[1,136,256]{2,1,0:T(8,128)S(1)}, f32[1,136,256]{2,1,0:T(8,128)S(1)}, u32[]{:S(2)}, u32[]{:S(2)}) collective-permute-start(f32[1,136,256]{2,1,0:T(8,128)S(1)} %add.19.refs_0_), channel_id=1, source_target_pairs={{0,1},{1,0},{2,3},{3,2},{4,5},{5,4},{6,7},{7,6},{8,9},{9,8},{10,11... | collective-permute-start | bytes 417800 | tf_op jit(solution)/shard_map/ppermute | solution.py:435
  85.8 1.4 %copy-start.1 = (f32[1,136,256]{2,1,0:T(8,128)}, f32[1,136,256]{2,1,0:T(8,128)S(1)}, u32[]{:S(2)}) copy-start(f32[1,136,256]{2,1,0:T(8,128)S(1)} %collective-permute-done.9.refs_1_) | copy-start | bytes 417796
  85.8 1.4 %collective-permute-start.11 = (f32[1,136,256]{2,1,0:T(8,128)S(1)}, f32[1,136,256]{2,1,0:T(8,128)S(1)}, u32[]{:S(2)}, u32[]{:S(2)}) collective-permute-start(f32[1,136,256]{2,1,0:T(8,128)S(1)} %collective-permute-done.9.refs_1_), channel_id=1, source_target_pairs={{0,1},{1,0},{2,3},{3,2},{4,5},{5,4},{6,7},{7,6},{8,9},{9,8},{10,11... | collective-permute-start | bytes 417800 | tf_op jit(solution)/shard_map/ppermute | solution.py:435
  85.8 1.4 %copy-start.2 = (f32[1,136,256]{2,1,0:T(8,128)}, f32[1,136,256]{2,1,0:T(8,128)S(1)}, u32[]{:S(2)}) copy-start(f32[1,136,256]{2,1,0:T(8,128)S(1)} %collective-permute-done.10.refs_2_) | copy-start | bytes 417796
  87.1 0.7 copy-start.3

commit v3 on v2

v3 whole, which is shorter than its diff:
```python
import functools

import jax
import jax.numpy as jnp
from jax import lax
from jax.experimental import pallas as pl
from jax.experimental.pallas import tpu as pltpu
from jax.sharding import PartitionSpec as P

HALO = 4
STEPS = 3
STEP_SIZE = 0.25
CHUNK = 1024
LIMIT = 24 * 1024 * 1024
PARTS = 8
F32 = jnp.float32
BF16 = jnp.bfloat16
HIGHEST = lax.Precision.HIGHEST


def split(value):
    high = value.astype(BF16)
    low = (value - high.astype(F32)).astype(BF16)
    return high, low


def contract_rows(left, right):
    return lax.dot_general(left, right, (((0,), (0,)), ((), ())), preferred_element_type=F32)


def matmul(left, right, precision=None):
    return lax.dot_general(
        left, right, (((1,), (0,)), ((), ())), preferred_element_type=F32, precision=precision
    )


def first_piece(at):
    return ((at >> 2) & 1) | (at & 2) | ((at & 1) << 2)


def second_piece(at):
    return ((at >> 2) & 1) | ((at & 1) << 1) | ((at & 2) << 1)


def second_place(piece):
    return ((piece & 1) << 2) | ((piece >> 1) & 1) | ((piece >> 1) & 2)


def force_product(panel, force):
    columns = force.T
    block = force.shape[1]
    total = jnp.zeros((1, panel.shape[1]), F32)
    for k in range(force.shape[0]):
        total += jnp.sum(panel[k * block : (k + 1) * block] * columns[:, k : k + 1], 0, keepdims=True)
    return total


def gram_kernel(snap_ref, force_ref, field_ref, turned_ref, gram_ref, load_ref):
    panel = snap_ref[...]
    snaps = panel.shape[1]
    high, low = split(panel)
    turned = high.T
    field_ref[:, :snaps] = high
    field_ref[:, snaps:] = low
    turned_ref[:snaps, :] = turned
    turned_ref[snaps:, :] = low.T
    gram = matmul(turned, jnp.concatenate([high, low], 1))
    load = force_product(panel, force_ref[...])

    @pl.when(pl.program_id(0) == 0)
    def _():
        gram_ref[...] = gram
        load_ref[...] = load

    @pl.when(pl.program_id(0) > 0)
    def _():
        gram_ref[...] += gram
        load_ref[...] += load


def gram_call(snapshots, force):
    rows, snaps = snapshots.shape
    block = force.shape[1]
    return pl.pallas_call(
        gram_kernel,
        out_shape=(
            jax.ShapeDtypeStruct((rows, 2 * snaps), BF16),
            jax.ShapeDtypeStruct((2 * snaps, rows), BF16),
            jax.ShapeDtypeStruct((snaps, 2 * snaps), F32),
            jax.ShapeDtypeStruct((1, snaps), F32),
        ),
        grid=(rows // CHUNK,),
        in_specs=[
            pl.BlockSpec((CHUNK, snaps), lambda i: (i, 0)),
            pl.BlockSpec((CHUNK // block, block), lambda i: (i, 0)),
        ],
        out_specs=[
            pl.BlockSpec((CHUNK, 2 * snaps), lambda i: (i, 0)),
            pl.BlockSpec((2 * snaps, CHUNK), lambda i: (0, i)),
            pl.BlockSpec((snaps, 2 * snaps), lambda i: (0, 0)),
            pl.BlockSpec((1, snaps), lambda i: (0, 0)),
        ],
        compiler_params=pltpu.CompilerParams(vmem_limit_bytes=LIMIT),
        cost_estimate=pl.CostEstimate(
            flops=4 * rows * snaps * snaps, bytes_accessed=12 * rows * snaps, transcendentals=0
        ),
        name="gram",
    )(snapshots, force)


def tangent_kernel(
    pattern_ref,
    place_ref,
    field,
    turned,
    prev_ref,
    next_ref,
    left_ref,
    right_ref,
    tangent_ref,
    force_ref,
    gram_ref,
    load_ref,
    image_ref,
    keep_first,
    send_first,
    keep_second,
    send_second,
    mixed,
    rest,
    load,
    packed,
    halo,
):
    rows, snaps = image_ref.shape
    block_count, coupled = pattern_ref.shape
    block = rows // block_count
    edge = HALO * block
    chunks = rows // CHUNK
    per_chunk = CHUNK // block
    for i, ref in enumerate((prev_ref, next_ref, left_ref, right_ref)):
        high, low = split(ref[...])
        at = pl.ds(i * edge, edge)
        halo[at, :snaps] = high
        halo[at, snaps:] = low
    mixed[...] = jnp.zeros_like(mixed)
    rest[...] = jnp.zeros_like(rest)
    load[...] = load_ref[...]

    @pl.loop(0, chunks)
    def _(step):
        start = pl.multiple_of(step * CHUNK, CHUNK)
        images = []
        for k in range(per_chunk):
            g = step * per_chunk + k
            picked = []
            for e in range(coupled):
                code = pattern_ref[g, e]
                source = lax.div(code, block_count)
                pick = lax.rem(code, block_count)
                here = source == 0
                tail = (source == 1) | (source == 3)
                beyond = (source - 1) * HALO + jnp.where(tail, pick - (block_count - HALO), pick)
                beyond = jnp.where(here, 0, beyond)
                inner = field[pl.ds(pl.multiple_of(pick * block, block), block), :]
                outer = halo[pl.ds(pl.multiple_of(beyond * block, block), block), :]
                picked.append(lax.select(here, inner, outer))
            own = pl.ds(pl.multiple_of(start + k * block, block), block)
            both = matmul(tangent_ref[own, :], jnp.concatenate(picked, 0))
            image = STEP_SIZE * (both[:, :snaps] + both[:, snaps:])
            image_ref[own, :] = image
            images.append(image)
        image = jnp.concatenate(images, 0)
        load[...] += force_product(image, force_ref[pl.ds(pl.multiple_of(step * per_chunk, per_chunk), per_chunk), :])
        high, low = split(image)
        high_turned = high.T
        panels = turned[:, pl.ds(start, CHUNK)]
        mixed[...] += matmul(jnp.concatenate([panels, high_turned], 0), high)
        rest[...] += matmul(jnp.concatenate([panels[:snaps], high_turned], 0), low)

    gram = gram_ref[:, :snaps] + gram_ref[:, snaps:] + gram_ref[:, snaps:].T
    cross = mixed[:snaps] + mixed[snaps : 2 * snaps] + rest[:snaps]
    square = mixed[2 * snaps :] + rest[snaps:] + rest[snaps:].T
    row = lax.broadcasted_iota(jnp.int32, (snaps, snaps), 0)
    column = lax.broadcasted_iota(jnp.int32, (snaps, snaps), 1)
    diagonal = jnp.sum(jnp.where(row == column, square, 0.0), 0, keepdims=True)
    packed[0] = jnp.where(row <= column, gram, square)
    packed[1] = cross
    extra_row = lax.broadcasted_iota(jnp.int32, (8, snaps), 0)
    extra = jnp.where(extra_row == 0, load[...], jnp.where(extra_row == 1, diagonal, 0.0))
    share = snaps // PARTS
    for at in range(PARTS):
        first = keep_first if at < PARTS // 2 else send_first
        second = keep_second if at < PARTS // 2 else send_second
        slot = at % (PARTS // 2)
        begin = pl.multiple_of((place_ref[0] ^ first_piece(at)) * share, 8)
        first[slot, :share, :] = packed[0, pl.ds(begin, share), :]
        first[slot, share:, :] = extra
        begin = pl.multiple_of((place_ref[0] ^ second_piece(at)) * share, 8)
        second[slot] = packed[1, pl.ds(begin, share), :]


def tangent_call(field, turned, halos, tangent, pattern, force, gram, load, place):
    rows = tangent.shape[0]
    snaps = gram.shape[0]
    share = snaps // PARTS
    vmem = pl.BlockSpec(memory_space=pltpu.VMEM)
    smem = pl.BlockSpec(memory_space=pltpu.SMEM)
    first = jax.ShapeDtypeStruct((PARTS // 2, share + 8, snaps), F32)
    second = jax.ShapeDtypeStruct((PARTS // 2, share, snaps), F32)
    return pl.pallas_call(
        tangent_kernel,
        out_shape=(
            jax.ShapeDtypeStruct((rows, snaps), F32),
            first,
            first,
            second,
            second,
        ),
        in_specs=[smem, smem] + [vmem] * 10,
        out_specs=[vmem] * 5,
        scratch_shapes=[
            pltpu.VMEM((3 * snaps, snaps), F32),
            pltpu.VMEM((2 * snaps, snaps), F32),
            pltpu.VMEM((1, snaps), F32),
            pltpu.VMEM((2, snaps, snaps), F32),
            pltpu.VMEM((4 * halos[0].shape[0], 2 * snaps), BF16),
        ],
        compiler_params=pltpu.CompilerParams(vmem_limit_bytes=LIMIT),
        name="tangent",
    )(pattern, place, field, turned, *halos, tangent, force, gram, load)


def inverse_factors(blocks):
    size = blocks[0].shape[0]
    groups = size // 8
    lane = lax.broadcasted_iota(jnp.int32, (8, size), 1)
    sub = lax.broadcasted_iota(jnp.int32, (8, size), 0)
    spread = lambda value: jnp.broadcast_to(value, (8, size))
    count = len(blocks)
    rows = [[value[8 * g : 8 * g + 8, :] for g in range(groups)] for value in blocks]
    done = [[] for _ in blocks]
    for g in range(groups):
        first = 8 * g
        inside = (lane >= first) & (lane < first + 8)
        unit = jnp.where(lane == sub + first, 1.0, 0.0)
        columns = [
            [spread(rows[m][g][:, first + j : first + j + 1]) for j in range(8)] for m in range(count)
        ]
        work = [jnp.where(inside, unit, rows[m][g]) for m in range(count)]
        kept = [jnp.zeros((8, size), F32) for _ in range(count)]
        for j in range(8):
            for m in range(count):
                pivot = spread(columns[m][j][j : j + 1, :])
                inverse = 1.0 / pivot
                root = lax.rsqrt(pivot)
                root = root * (1.5 - 0.5 * pivot * root * root)
                mine = sub == j
                for k in range(j + 1, 8):
                    scaled = spread(columns[m][k][j : j + 1, :]) * inverse
                    columns[m][k] = jnp.where(mine, scaled, columns[m][k] - columns[m][j] * scaled)
                row = spread(work[m][j : j + 1, :])
                kept[m] = jnp.where(mine, row * root, kept[m])
                scaled = row * inverse
                work[m] = jnp.where(mine, scaled, work[m] - columns[m][j] * scaled)
        for m in range(count):
            done[m].append(jnp.where(lane < first + 8, kept[m], 0.0))
            pivots = [spread(work[m][j : j + 1, :]) for j in range(8)]
            for i in range(g + 1, groups):
                old = rows[m][i]
                new = jnp.where(inside, 0.0, old)
                for j in range(8):
                    new = new - spread(old[:, first + j : first + j + 1]) * pivots[j]
                rows[m][i] = new
    return [jnp.concatenate(values, 0) for values in done]


def dot_last(left, right):
    return lax.dot_general(
        left, right, (((1,), (1,)), ((), ())), preferred_element_type=F32, precision=HIGHEST
    )


def reduced_system(inverse_count, place, first, second, index):
    snaps = first.shape[2]
    share = snaps // PARTS
    half = snaps // 2
    order = [first_piece(place ^ c) for c in range(PARTS)]
    packed = jnp.concatenate([first[at, :share, :] for at in order], 0) * inverse_count
    load = first[0, share : share + 1, :] * inverse_count
    diagonal = first[0, share + 1 : share + 2, :] * inverse_count
    order = [second_place(place ^ c) for c in range(PARTS)]
    cross = jnp.concatenate([second[at] for at in order], 0) * inverse_count
    row = lax.broadcasted_iota(jnp.int32, (snaps, snaps), 0)
    column = lax.broadcasted_iota(jnp.int32, (snaps, snaps), 1)
    turned = packed.T
    gram = jnp.where(row <= column, packed, turned)
    square = jnp.where(row > column, packed, jnp.where(row == column, diagonal, turned))
    project = gram + cross.T
    normal = project + cross + square

    pair = (gram, normal)
    upper = inverse_factors([value[:half, :half] for value in pair])
    below = [dot_last(value[half:, :half], inv) for value, inv in zip(pair, upper)]
    rest = [value[half:, half:] - dot_last(low, low) for value, low in zip(pair, below)]
    lower = inverse_factors(rest)
    inverses = []
    for top, low, bottom in zip(upper, below, lower):
        corner = -matmul(bottom, matmul(low, top, HIGHEST), HIGHEST)
        inverses.append(
            jnp.concatenate(
                [
                    jnp.concatenate([top, jnp.zeros((half, half), F32)], 1),
                    jnp.concatenate([corner, bottom], 1),
                ],
                0,
            )
        )
    gram_inverse, normal_inverse = inverses
    root = gram_inverse.T

    across = lambda matrix, vector: jnp.sum(matrix * vector, 1, keepdims=True)
    down = lambda matrix, vector: jnp.sum(matrix * vector, 0, keepdims=True)
    state = jnp.where(index == jnp.max(index), 1.0, 0.0)
    eye = jnp.where(row == column, 1.0, 0.0)
    history = []
    for _ in range(STEPS):
        old = state
        right = down(eye, across(project, state)) + STEP_SIZE * load
        state = down(normal_inverse, across(normal_inverse, right))
        history.append(down(root, across(gram, state)))
    return root, history, state - old, state


def final_kernel(inverse_count, place_ref, *refs):
    pieces = refs[:4]
    index_ref, force_ref, image, snap_any, basis_any, coeff_ref, residual_ref = refs[4:11]
    snap, first, second, root_ref, change_ref, state_ref, tile, sems = refs[11:]
    rows, snaps = snap.shape
    block = force_ref.shape[1]
    chunks = rows // CHUNK
    per_chunk = CHUNK // block
    copy = pltpu.make_async_copy(snap_any, snap, sems.at[chunks])
    copy.start()
    for i, pack in enumerate((first, second)):
        pack[: PARTS // 2] = pieces[2 * i][...]
        pack[PARTS // 2 :] = pieces[2 * i + 1][...]
    root, history, change, state = reduced_system(inverse_count, place_ref[0], first, second, index_ref[...])
    high, low = split(root)
    root_ref[:, :snaps] = high
    root_ref[:, snaps:] = low
    for n in range(STEPS):
        coeff_ref[n : n + 1, :] = history[n]
    change_ref[...] = change
    state_ref[...] = state
    copy.wait()
    tile[...] = jnp.zeros_like(tile)
    lane = lax.broadcasted_iota(jnp.int32, (block, block), 1)

    def out_copy(i):
        at = pl.ds(pl.multiple_of(i * CHUNK, CHUNK), CHUNK)
        return pltpu.make_async_copy(snap.at[at, :], basis_any.at[at, :], sems.at[i])

    @pl.loop(0, chunks)
    def _(i):
        at = pl.ds(pl.multiple_of(i * CHUNK, CHUNK), CHUNK)
        panel = snap[at, :]
        sums = jnp.sum(panel * change_ref[...] + image[at, :] * state_ref[...], 1, keepdims=True)
        gathered = tile[...]
        for k in range(per_chunk):
            gathered = jnp.where(lane == i * per_chunk + k, sums[k * block : (k + 1) * block], gathered)
        tile[...] = gathered
        panel_high, panel_low = split(panel)
        both = matmul(panel_high, root_ref[...])
        snap[at, :] = both[:, :snaps] + both[:, snaps:] + matmul(panel_low, root_ref[:, :snaps])
        out_copy(i).start()

    residual_ref[...] = tile[...].T[: rows // block] - STEP_SIZE * force_ref[...]

    @pl.loop(0, chunks)
    def _(i):
        out_copy(i).wait()


def final_call(pieces, step_index, place, snapshots, image, force, inverse_count):
    rows, snaps = snapshots.shape
    block = force.shape[1]
    share = snaps // PARTS
    vmem = pl.BlockSpec(memory_space=pltpu.VMEM)
    hbm = pl.BlockSpec(memory_space=pl.ANY)
    return pl.pallas_call(
        functools.partial(final_kernel, inverse_count),
        out_shape=(
            jax.ShapeDtypeStruct((rows, snaps), F32),
            jax.ShapeDtypeStruct((STEPS, snaps), F32),
            jax.ShapeDtypeStruct(force.shape, F32),
        ),
        in_specs=[pl.BlockSpec(memory_space=pltpu.SMEM)] + [vmem] * 7 + [hbm],
        out_specs=[hbm, vmem, vmem],
        scratch_shapes=[
            pltpu.VMEM((rows, snaps), F32),
            pltpu.VMEM((PARTS, share + 8, snaps), F32),
            pltpu.VMEM((PARTS, share, snaps), F32),
            pltpu.VMEM((snaps, 2 * snaps), BF16),
            pltpu.VMEM((1, snaps), F32),
            pltpu.VMEM((1, snaps), F32),
            pltpu.VMEM((block, block), F32),
            pltpu.SemaphoreType.DMA((rows // CHUNK + 1,)),
        ],
        compiler_params=pltpu.CompilerParams(vmem_limit_bytes=LIMIT),
        name="final",
    )(place, *pieces, step_index, force, image, snapshots)


def shifted(value, axis, steps):
    count = lax.axis_size(axis)
    pairs = [(source, (source + steps) % count) for source in range(count)]
    return lax.ppermute(value, axis, pairs)


def from_behind(shard, axis, by):
    devices = lax.axis_size(axis)
    pairs = [(i, i + by) for i in range(devices) if 0 <= i + by < devices]
    return lax.ppermute(shard, axis, pairs)


def partner(value, axis, bit):
    count = lax.axis_size(axis)
    return lax.ppermute(value, axis, [(i, i ^ bit) for i in range(count)])


def reduce_packed(keep_first, send_first, keep_second, send_second):
    core, x, y = ("zone", 1), ("zone", 2), ("rows", 1)
    first = keep_first + partner(send_first, *core)
    second = keep_second + partner(send_second, *core)
    for way_first, way_second in ((x, y), (y, x)):
        half = first.shape[0] // 2
        first = first[:half] + partner(first[half:], *way_first)
        second = second[:half] + partner(second[half:], *way_second)
    edge = first.shape[1]
    value = jnp.concatenate([first, second], 1)
    for axis, least in (("rows", 2), ("zone", 4)):
        bit = least
        while bit < lax.axis_size(axis):
            value = value + partner(value, axis, bit)
            bit *= 2
    first, second = value[:, :edge], value[:, edge:]
    for way_first, way_second in ((y, x), (x, y)):
        first = jnp.concatenate([first, partner(first, *way_first)], 0)
        second = jnp.concatenate([second, partner(second, *way_second)], 0)
    return first, partner(first, *core), second, partner(second, *core)


def shards(snapshots, tangent, pattern, forcing, step_index):
    rows, snaps = snapshots.shape
    blocks = pattern.shape[0]
    block = rows // blocks
    edge = HALO * block
    inverse_count = 1.0 / (rows * lax.axis_size("rows") * lax.axis_size("zone"))
    place = (lax.axis_index("zone") & 3) | ((lax.axis_index("rows") & 1) << 2)
    place = jnp.reshape(place, (1,)).astype(jnp.int32)
    force = forcing.reshape(blocks, block)
    head, tail = snapshots[:edge], snapshots[rows - edge :]
    rows_prev = shifted(tail, "rows", 1)
    rows_next = shifted(head, "rows", -1)
    field, turned, gram, load = gram_call(snapshots, force)
    head, tail, load = lax.optimization_barrier((head, tail, load))
    halos = (rows_prev, rows_next, from_behind(tail, "zone", 1), from_behind(head, "zone", -1))
    image, *packed = tangent_call(field, turned, halos, tangent, pattern, force, gram, load, place)
    pieces = reduce_packed(*packed)
    basis, coefficients, residual = final_call(
        pieces, step_index.reshape(1, snaps), place, snapshots, image, force, inverse_count
    )
    return basis, coefficients, residual.reshape(rows)


def solution(mesh):
    in_specs = (
        P(("rows", "zone"), None),
        P(("rows", "zone"), None),
        P(("rows", "zone"), None),
        P(("rows", "zone")),
        P(),
    )
    out_specs = (P(("rows", "zone"), None), P(), P(("rows", "zone")))
    return jax.shard_map(shards, mesh=mesh, in_specs=in_specs, out_specs=out_specs, check_vma=False)
```

time: 114 us -> 117 us (1.026)
  local copies, waits for them, and re-layouts: 4.12 us -> 20.1 us
  Pallas kernels: 54.8 us -> 44.6 us
  waiting for transfers between devices: 31.1 us -> 24.1 us
  starting transfers between devices: 21.2 us -> 26.9 us
    unnamed x17 -> x23, local copies, waits for them, and re-layouts: 2.84 us -> 17.9 us
    pallas_call x3, Pallas kernels: 54.8 us -> 44.6 us  [the longest x1 20.8 us: final_call(): pl.pallas_call(functools.partial(final_kernel, inverse_count), out_shape=...]
    ppermute x2, waiting for transfers between devices: 8.57 us -> 0.01 us  [shifted(): return lax.ppermute(value, axis, pairs)]
    ppermute x8 -> x14, starting transfers between devices: 11 us -> 18.1 us  [partner(): return lax.ppermute(value, axis, [(i, i ^ bit) for i in range(count)])]
    ppermute x2, waiting for transfers between devices: 0.01 us -> 3.91 us  [from_behind(): return lax.ppermute(shard, axis, pairs)]
    ppermute x8 -> x14, waiting for transfers between devices: 22.5 us -> 20.2 us  [partner(): return lax.ppermute(value, axis, [(i, i ^ bit) for i in range(count)])]
    ppermute x2, starting transfers between devices: 4.06 us -> 2.76 us  [from_behind(): return lax.ppermute(shard, axis, pairs)]
  transfers between devices with their start and end apart: 12 -> 18, of which waited for: 9 -> 14; matrix products, arithmetic and copies ran while one was open for 1% -> 0% of each run, Pallas kernels for 8% -> 6%
where the time goes in v3:
time: 117 us
  Pallas kernels  44.6 us (38%)
  starting transfers between devices  26.9 us (23%)
  waiting for transfers between devices  24.1 us (21%)
  local copies, waits for them, and re-layouts  20.1 us (17%)
    pallas_call x1, Pallas kernels, final_call(): pl.pallas_call(functools.partial(final_kernel, inverse_count), out_shape=...  20.8 us
    ppermute x14, waiting for transfers between devices, partner(): return lax.ppermute(value, axis, [(i, i ^ bit) for i in range(count)])  20.2 us
    ppermute x14, starting transfers between devices, partner(): return lax.ppermute(value, axis, [(i, i ^ bit) for i in range(count)])  18.1 us
    unnamed x23, local copies, waits for them, and re-layouts  17.9 us
    pallas_call x1, Pallas kernels, tangent_call(): pl.pallas_call(tangent_kernel, out_shape=(jax.ShapeDtypeStruct((rows, sna...  17.1 us
    pallas_call x1, Pallas kernels, gram_call(): pl.pallas_call(gram_kernel, out_shape=(jax.ShapeDtypeStruct((rows, 2 * sn...  6.74 us
    ppermute x2, starting transfers between devices, shifted(): return lax.ppermute(value, axis, pairs)  6.01 us
    ppermute x2, waiting for transfers between devices, from_behind(): return lax.ppermute(shard, axis, pairs)  3.91 us
  transfers between devices with their start and end apart: 18, of which 14 were waited for; matrix products, arithmetic and copies ran while one was open for 0% of the time, Pallas kernels for 6%

profile of v3, /device:TPU:0, one launch (start us, length us, event | category | flops | bytes accessed | tf_op | source)
XLA Modules:
  0.0 116.9 jit_solution(14776915258080789729)
XLA Ops:
  0.7 2.1 %fusion.1 = (f32[512,256]{1,0:T(8,128)S(1)}, f32[512,256]{1,0:T(8,128)}) fusion(f32[8192,256]{1,0:T(8,128)} %refs_7_.1), kind=kLoop, calls=%fused_computation.10 | loop fusion | bytes 2097152 | tf_op jit(solution)/shard_map/slice | solution.py:463
  2.8 6.0 %collective-permute-start.1 = (f32[512,256]{1,0:T(8,128)S(1)}, f32[512,256]{1,0:T(8,128)S(1)}, u32[]{:S(2)}, u32[]{:S(2)}) collective-permute-start(f32[512,256]{1,0:T(8,128)S(1)} %get-tuple-element.22), channel_id=1, source_target_pairs={{0,28},{4,0},{8,4},{12,8},{16,12},{20,16},{24,20},{28,24},{1,29},{... | collective-permute-start | bytes 1572872 | tf_op jit(solution)/shard_map/ppermute | solution.py:418
  8.8 3.4 %copy-done = f32[8192,256]{1,0:T(8,128)S(1)} copy-done((f32[8192,256]{1,0:T(8,128)S(1)}, f32[8192,256]{1,0:T(8,128)}, u32[]{:S(2)}) %copy-start) | copy-done | bytes 8388632
  12.2 0.8 copy-done.5
  12.9 6.7 %gram.1 = (bf16[8192,512]{1,0:T(8,128)(2,1)S(1)}, bf16[512,8192]{1,0:T(8,128)(2,1)S(1)}, f32[256,512]{1,0:T(8,128)S(1)}, f32[1,256]{1,0:T(1,128)S(1)}) custom-call(f32[8192,256]{1,0:T(8,128)S(1)} %copy-done, f32[64,128]{1,0:T(8,128)S(1)} %bitcast.6), custom_call_target="tpu_custom_call" | custom-call | flops 2147483648 | bytes 25165824 | tf_op jit(solution)/shard_map/gram/pallas_call | solution.py:84
  19.7 3.4 %copy-done.1 = bf16[8192,512]{1,0:T(8,128)(2,1)} copy-done((bf16[8192,512]{1,0:T(8,128)(2,1)}, bf16[8192,512]{1,0:T(8,128)(2,1)S(1)}, u32[]{:S(2)}) %copy-start.1) | copy-done | bytes 8388632
  23.1 3.3 %copy-done.3 = bf16[512,8192]{1,0:T(8,128)(2,1)} copy-done((bf16[512,8192]{1,0:T(8,128)(2,1)}, bf16[512,8192]{1,0:T(8,128)(2,1)S(1)}, u32[]{:S(2)}) %copy-start.3) | copy-done | bytes 8388632
  26.4 1.5 %collective-permute-start.2 = (f32[512,256]{1,0:T(8,128)}, f32[512,256]{1,0:T(8,128)S(1)}, u32[]{:S(2)}, u32[]{:S(2)}) collective-permute-start(f32[512,256]{1,0:T(8,128)} %get-tuple-element.21), channel_id=1, source_target_pairs={{0,1},{1,2},{2,3},{4,5},{5,6},{6,7},{8,9},{9,10},{10,11},{12,13},{... | collective-permute-start | bytes 1572872 | tf_op jit(solution)/shard_map/ppermute | solution.py:424
  27.8 1.3 %collective-permute-start.3 = (f32[512,256]{1,0:T(8,128)S(1)}, f32[512,256]{1,0:T(8,128)S(1)}, u32[]{:S(2)}, u32[]{:S(2)}) collective-permute-start(f32[512,256]{1,0:T(8,128)S(1)} %get-tuple-element.22), channel_id=1, source_target_pairs={{1,0},{2,1},{3,2},{5,4},{6,5},{7,6},{9,8},{10,9},{11,10},{13,12},{... | collective-permute-start | bytes 1572872 | tf_op jit(solution)/shard_map/ppermute | solution.py:424
  29.5 3.6 %collective-permute-done.3.right_ref = f32[512,256]{1,0:T(8,128)S(1)} collective-permute-done((f32[512,256]{1,0:T(8,128)S(1)}, f32[512,256]{1,0:T(8,128)S(1)}, u32[]{:S(2)}, u32[]{:S(2)}) %collective-permute-start.3) | collective-permute-done | bytes 524320 | tf_op jit(solution)/shard_map/ppermute | solution.py:424
  33.2 3.5 %copy-done.2 = bf16[8192,512]{1,0:T(8,128)(2,1)S(1)} copy-done((bf16[8192,512]{1,0:T(8,128)(2,1)S(1)}, bf16[8192,512]{1,0:T(8,128)(2,1)}, u32[]{:S(2)}) %copy-start.2) | copy-done | bytes 8388632
  36.7 3.5 %copy-done.4 = bf16[512,8192]{1,0:T(8,128)(2,1)S(1)} copy-done((bf16[512,8192]{1,0:T(8,128)(2,1)S(1)}, bf16[512,8192]{1,0:T(8,128)(2,1)}, u32[]{:S(2)}) %copy-start.4) | copy-done | bytes 8388632
  40.2 17.1 %tangent.1 = (f32[8192,256]{1,0:T(8,128)S(1)}, f32[4,40,256]{2,1,0:T(8,128)S(1)}, f32[4,40,256]{2,1,0:T(8,128)S(1)}, f32[4,32,256]{2,1,0:T(8,128)S(1)}, f32[4,32,256]{2,1,0:T(8,128)S(1)}) custom-call(s32[64,4]{1,0:T(8,128)S(1)} %copy.8.pattern_ref, s32[1]{0:T(128)} %bitcast.place_ref, bf16[8192,512]{1,0:T(8,128)(2,1)S(1)} %copy-done.2, ...), custom_call_target="tpu_custom_call" | custom-call | tf_op jit(solution)/shard_map/tangent/pallas_call | solution.py:211
  57.3 7.3 %collective-permute-start.7 = (f32[4,32,256]{2,1,0:T(8,128)S(1)}, f32[4,32,256]{2,1,0:T(8,128)S(1)}, u32[]{:S(2)}, u32[]{:S(2)}) collective-permute-start(f32[4,32,256]{2,1,0:T(8,128)S(1)} %get-tuple-element.28), channel_id=1, source_target_pairs={{0,1},{1,0},{2,3},{3,2},{4,5},{5,4},{6,7},{7,6},{8,9},{9,8},{10,11... | collective-permute-start | bytes 393224 | tf_op jit(solution)/shard_map/ppermute | solution.py:429
  64.7 0.9 collective-permute-done.7
  66.1 3.9 %collective-permute-done.8 = f32[2,32,256]{2,1,0:T(8,128)S(1)} collective-permute-done((f32[2,32,256]{2,1,0:T(8,128)S(1)}, f32[2,32,256]{2,1,0:T(8,128)S(1)}, u32[]{:S(2)}, u32[]{:S(2)}) %collective-permute-start.8) | collective-permute-done | bytes 65568 | tf_op jit(solution)/shard_map/ppermute | solution.py:429
  70.6 1.7 %collective-permute-start.6 = (f32[1,40,256]{2,1,0:T(8,128)S(1)}, f32[1,40,256]{2,1,0:T(8,128)S(1)}, u32[]{:S(2)}, u32[]{:S(2)}) collective-permute-start(f32[1,40,256]{2,1,0:T(8,128)S(1)} %slice.51), channel_id=1, source_target_pairs={{0,4},{4,0},{8,12},{12,8},{16,20},{20,16},{24,28},{28,24},{1,5},{5... | collective-permute-start | bytes 122888 | tf_op jit(solution)/shard_map/ppermute | solution.py:429
  72.4 1.7 %collective-permute-done.9 = f32[1,32,256]{2,1,0:T(8,128)S(1)} collective-permute-done((f32[1,32,256]{2,1,0:T(8,128)S(1)}, f32[1,32,256]{2,1,0:T(8,128)S(1)}, u32[]{:S(2)}, u32[]{:S(2)}) %collective-permute-start.9) | collective-permute-done | bytes 32800 | tf_op jit(solution)/shard_map/ppermute | solution.py:429
  74.0 0.7 collective-permute-done.6
  74.7 1.1 collective-permute-start.10
  75.9 3.3 %collective-permute-done.10 = f32[1,72,256]{2,1,0:T(8,128)S(1)} collective-permute-done((f32[1,72,256]{2,1,0:T(8,128)S(1)}, f32[1,72,256]{2,1,0:T(8,128)S(1)}, u32[]{:S(2)}, u32[]{:S(2)}) %collective-permute-start.10) | collective-permute-done | bytes 73760 | tf_op jit(solution)/shard_map/ppermute | solution.py:429
  79.2 3.7 %collective-permute-start.11 = (f32[1,72,256]{2,1,0:T(8,128)S(1)}, f32[1,72,256]{2,1,0:T(8,128)S(1)}, u32[]{:S(2)}, u32[]{:S(2)}) collective-permute-start(f32[1,72,256]{2,1,0:T(8,128)S(1)} %fusion), channel_id=1, source_target_pairs={{0,16},{4,20},{8,24},{12,28},{16,0},{20,4},{24,8},{28,12},{1,17},{... | collective-permute-start | bytes 221192 | tf_op jit(solution)/shard_map/ppermute | solution.py:429
  82.9 2.3 %collective-permute-done.11 = f32[1,72,256]{2,1,0:T(8,128)S(1)} collective-permute-done((f32[1,72,256]{2,1,0:T(8,128)S(1)}, f32[1,72,256]{2,1,0:T(8,128)S(1)}, u32[]{:S(2)}, u32[]{:S(2)}) %collective-permute-start.11) | collective-permute-done | bytes 73760 | tf_op jit(solution)/shard_map/ppermute | solution.py:429
  85.2 1.0 collective-permute-start.12
  86.2 0.9 collective-permute-start.15
  87.1 2.1 %collective-permute-done.12 = f32[1,40,256]{2,1,0:T(8,128)S(1)} collective-permute-done((f32[1,40,256]{2,1,0:T(8,128)S(1)}, f32[1,40,256]{2,1,0:T(8,128)S(1)}, u32[]{:S(2)}, u32[]{:S(2)}) %collective-permute-start.12) | collective-permute-done | bytes 40992 | tf_op jit(solution)/shard_map/ppermute | solution.py:429
  89.3 0.9 collective-permute-start.13
  90.2 1.1 collective-permute-start.16
  91.2 2.5 %collective-permute-done.13 = f32[2,40,256]{2,1,0:T(8,128)S(1)} collective-permute-done((f32[2,40,256]{2,1,0:T(8,128)S(1)}, f32[2,40,256]{2,1,0:T(8,128)S(1)}, u32[]{:S(2)}, u32[]{:S(2)}) %collective-permute-start.13) | collective-permute-done | bytes 81952 | tf_op jit(solution)/shard_map/ppermute | solution.py:429
  93.8 0.7 collective-permute-done.16
  94.6 1.3 %collective-permute-done.17.refs_3_ = f32[4,32,256]{2,1,0:T(8,128)S(1)} collective-permute-done((f32[4,32,256]{2,1,0:T(8,128)S(1)}, f32[4,32,256]{2,1,0:T(8,128)S(1)}, u32[]{:S(2)}, u32[]{:S(2)}) %collective-permute-start.17) | collective-permute-done | bytes 131104 | tf_op jit(solution)/shard_map/ppermute | solution.py:429
  95.9 20.8 %final.1 = (f32[8192,256]{1,0:T(8,128)}, f32[3,256]{1,0:T(4,128)}, f32[64,128]{1,0:T(8,128)}) custom-call(s32[1]{0:T(128)} %bitcast.place_ref, f32[4,40,256]{2,1,0:T(8,128)S(1)} %pad_maximum_fusion.refs_0_, f32[4,40,256]{2,1,0:T(8,128)S(1)} %collective-permute-done.14.refs_1_, f32[4,32,256]{2,1,0:T(8,128)S(1)} %pad_maximum_fusion.1.refs_2_, ...), custom_call_target="tpu_custom_call" | custom-call | tf_op jit(solution)/shard_map/final/pallas_call | solution.py:391
  (51 shorter events, 1.8 us)
Async XLA Ops:
  0.6 32.5 %copy-start.6 = (f32[8192]{0:T(1024)S(1)}, f32[8192]{0:T(1024)}, u32[]{:S(2)}) copy-start(f32[8192]{0:T(1024)} %param.8) | copy-start | bytes 98308
  0.6 28.5 %copy-start.8 = (s32[64,4]{0,1:T(4,128)S(1)}, s32[64,4]{0,1:T(4,128)}, u32[]{:S(2)}) copy-start(s32[64,4]{0,1:T(4,128)} %param.7) | copy-start | bytes 3076
  2.8 26.5 %collective-permute-start.1 = (f32[512,256]{1,0:T(8,128)S(1)}, f32[512,256]{1,0:T(8,128)S(1)}, u32[]{:S(2)}, u32[]{:S(2)}) collective-permute-start(f32[512,256]{1,0:T(8,128)S(1)} %get-tuple-element.22), channel_id=1, source_target_pairs={{0,28},{4,0},{8,4},{12,8},{16,12},{20,16},{24,20},{28,24},{1,29},{... | collective-permute-start | bytes 1572872 | tf_op jit(solution)/shard_map/ppermute | solution.py:418
  8.8 20.5 %collective-permute-start = (f32[512,256]{1,0:T(8,128)}, f32[512,256]{1,0:T(8,128)S(1)}, u32[]{:S(2)}, u32[]{:S(2)}) collective-permute-start(f32[512,256]{1,0:T(8,128)} %get-tuple-element.21), channel_id=1, source_target_pairs={{0,4},{4,8},{8,12},{12,16},{16,20},{20,24},{24,28},{28,0},{1,5},{5... | collective-permute-start | bytes 1572872 | tf_op jit(solution)/shard_map/ppermute | solution.py:418
  8.8 3.4 %copy-start = (f32[8192,256]{1,0:T(8,128)S(1)}, f32[8192,256]{1,0:T(8,128)}, u32[]{:S(2)}) copy-start(f32[8192,256]{1,0:T(8,128)} %refs_7_.1) | copy-start | bytes 25165828
  12.2 0.8 copy-start.5
  19.7 3.4 %copy-start.1 = (bf16[8192,512]{1,0:T(8,128)(2,1)}, bf16[8192,512]{1,0:T(8,128)(2,1)S(1)}, u32[]{:S(2)}) copy-start(bf16[8192,512]{1,0:T(8,128)(2,1)S(1)} %get-tuple-element.18.field) | copy-start | bytes 25165828
  23.1 3.3 %copy-start.3 = (bf16[512,8192]{1,0:T(8,128)(2,1)}, bf16[512,8192]{1,0:T(8,128)(2,1)S(1)}, u32[]{:S(2)}) copy-start(bf16[512,8192]{1,0:T(8,128)(2,1)S(1)} %get-tuple-element.19.turned) | copy-start | bytes 25165828
  26.4 3.2 %collective-permute-start.2 = (f32[512,256]{1,0:T(8,128)}, f32[512,256]{1,0:T(8,128)S(1)}, u32[]{:S(2)}, u32[]{:S(2)}) collective-permute-start(f32[512,256]{1,0:T(8,128)} %get-tuple-element.21), channel_id=1, source_target_pairs={{0,1},{1,2},{2,3},{4,5},{5,6},{6,7},{8,9},{9,10},{10,11},{12,13},{... | collective-permute-start | bytes 1572872 | tf_op jit(solution)/shard_map/ppermute | solution.py:424
  27.8 5.3 %collective-permute-start.3 = (f32[512,256]{1,0:T(8,128)S(1)}, f32[512,256]{1,0:T(8,128)S(1)}, u32[]{:S(2)}, u32[]{:S(2)}) collective-permute-start(f32[512,256]{1,0:T(8,128)S(1)} %get-tuple-element.22), channel_id=1, source_target_pairs={{1,0},{2,1},{3,2},{5,4},{6,5},{7,6},{9,8},{10,9},{11,10},{13,12},{... | collective-permute-start | bytes 1572872 | tf_op jit(solution)/shard_map/ppermute | solution.py:424
  33.2 62.8 %slice-start = ((s8[8388608]{0:T(1024)(128)(4,1)}), s8[4194304]{0:T(1024)(128)(4,1)S(1)}, s32[]{:S(2)}) async-start(s8[8388608]{0:T(1024)(128)(4,1)} %bitcast.4), calls=%async_computation | async-start | bytes 8388608
  33.2 3.5 %copy-start.2 = (bf16[8192,512]{1,0:T(8,128)(2,1)S(1)}, bf16[8192,512]{1,0:T(8,128)(2,1)}, u32[]{:S(2)}) copy-start(bf16[8192,512]{1,0:T(8,128)(2,1)} %copy-done.1) | copy-start | bytes 25165828
  36.7 3.5 %copy-start.4 = (bf16[512,8192]{1,0:T(8,128)(2,1)S(1)}, bf16[512,8192]{1,0:T(8,128)(2,1)}, u32[]{:S(2)}) copy-start(bf16[512,8192]{1,0:T(8,128)(2,1)} %copy-done.3) | copy-start | bytes 25165828
  40.2 55.7 %slice-start.1 = ((s8[8388608]{0:T(1024)(128)(4,1)}), s8[4194304]{0:T(1024)(128)(4,1)S(1)}, s32[]{:S(2)}) async-start(s8[8388608]{0:T(1024)(128)(4,1)} %bitcast.4), calls=%async_computation.1 | async-start | bytes 8388608
  40.2 55.7 %copy-start.7 = (s32[256]{0:T(256)S(1)}, s32[256]{0:T(256)}, u32[]{:S(2)}) copy-start(s32[256]{0:T(256)} %param.9) | copy-start | bytes 3076
  57.3 8.2 %collective-permute-start.7 = (f32[4,32,256]{2,1,0:T(8,128)S(1)}, f32[4,32,256]{2,1,0:T(8,128)S(1)}, u32[]{:S(2)}, u32[]{:S(2)}) collective-permute-start(f32[4,32,256]{2,1,0:T(8,128)S(1)} %get-tuple-element.28), channel_id=1, source_target_pairs={{0,1},{1,0},{2,3},{3,2},{4,5},{5,4},{6,7},{7,6},{8,9},{9,8},{10,11... | collective-permute-start | bytes 393224 | tf_op jit(solution)/shard_map/ppermute | solution.py:429
  64.6 1.4 %collective-permute-start.4 = (f32[4,40,256]{2,1,0:T(8,128)S(1)}, f32[4,40,256]{2,1,0:T(8,128)S(1)}, u32[]{:S(2)}, u32[]{:S(2)}) collective-permute-start(f32[4,40,256]{2,1,0:T(8,128)S(1)} %get-tuple-element.26), channel_id=1, source_target_pairs={{0,1},{1,0},{2,3},{3,2},{4,5},{5,4},{6,7},{7,6},{8,9},{9,8},{10,11... | collective-permute-start | bytes 491528 | tf_op jit(solution)/shard_map/ppermute | solution.py:429
  65.6 4.4 %collective-permute-start.8 = (f32[2,32,256]{2,1,0:T(8,128)S(1)}, f32[2,32,256]{2,1,0:T(8,128)S(1)}, u32[]{:S(2)}, u32[]{:S(2)}) collective-permute-start(f32[2,32,256]{2,1,0:T(8,128)S(1)} %slice.53), channel_id=1, source_target_pairs={{0,4},{4,0},{8,12},{12,8},{16,20},{20,16},{24,28},{28,24},{1,5},{5... | collective-permute-start | bytes 196616 | tf_op jit(solution)/shard_map/ppermute | solution.py:429
  66.0 4.6 %collective-permute-start.5 = (f32[2,40,256]{2,1,0:T(8,128)S(1)}, f32[2,40,256]{2,1,0:T(8,128)S(1)}, u32[]{:S(2)}, u32[]{:S(2)}) collective-permute-start(f32[2,40,256]{2,1,0:T(8,128)S(1)} %slice.49), channel_id=1, source_target_pairs={{0,2},{1,3},{2,0},{3,1},{4,6},{5,7},{6,4},{7,5},{8,10},{9,11},{10,... | collective-permute-start | bytes 245768 | tf_op jit(solution)/shard_map/ppermute | solution.py:429
  70.1 4.0 %collective-permute-start.9 = (f32[1,32,256]{2,1,0:T(8,128)S(1)}, f32[1,32,256]{2,1,0:T(8,128)S(1)}, u32[]{:S(2)}, u32[]{:S(2)}) collective-permute-start(f32[1,32,256]{2,1,0:T(8,128)S(1)} %slice.55), channel_id=1, source_target_pairs={{0,2},{1,3},{2,0},{3,1},{4,6},{5,7},{6,4},{7,5},{8,10},{9,11},{10,... | collective-permute-start | bytes 98312 | tf_op jit(solution)/shard_map/ppermute | solution.py:429
  70.6 4.1 %collective-permute-start.6 = (f32[1,40,256]{2,1,0:T(8,128)S(1)}, f32[1,40,256]{2,1,0:T(8,128)S(1)}, u32[]{:S(2)}, u32[]{:S(2)}) collective-permute-start(f32[1,40,256]{2,1,0:T(8,128)S(1)} %slice.51), channel_id=1, source_target_pairs={{0,4},{4,0},{8,12},{12,8},{16,20},{20,16},{24,28},{28,24},{1,5},{5... | collective-permute-start | bytes 122888 | tf_op jit(solution)/shard_map/ppermute | solution.py:429
  74.7 4.4 %collective-permute-start.10 = (f32[1,72,256]{2,1,0:T(8,128)S(1)}, f32[1,72,256]{2,1,0:T(8,128)S(1)}, u32[]{:S(2)}, u32[]{:S(2)}) collective-permute-start(f32[1,72,256]{2,1,0:T(8,128)S(1)} %pad_maximum_fusion.3), channel_id=1, source_target_pairs={{0,8},{4,12},{8,0},{12,4},{16,24},{20,28},{24,16},{28,20},{1,9},{5... | collective-permute-start | bytes 221192 | tf_op jit(solution)/shard_map/ppermute | solution.py:429
  79.2 6.0 %collective-permute-start.11 = (f32[1,72,256]{2,1,0:T(8,128)S(1)}, f32[1,72,256]{2,1,0:T(8,128)S(1)}, u32[]{:S(2)}, u32[]{:S(2)}) collective-permute-start(f32[1,72,256]{2,1,0:T(8,128)S(1)} %fusion), channel_id=1, source_target_pairs={{0,16},{4,20},{8,24},{12,28},{16,0},{20,4},{24,8},{28,12},{1,17},{... | collective-permute-start | bytes 221192 | tf_op jit(solution)/shard_map/ppermute | solution.py:429
  85.2 4.1 %collective-permute-start.12 = (f32[1,40,256]{2,1,0:T(8,128)S(1)}, f32[1,40,256]{2,1,0:T(8,128)S(1)}, u32[]{:S(2)}, u32[]{:S(2)}) collective-permute-start(f32[1,40,256]{2,1,0:T(8,128)S(1)} %slice.56), channel_id=1, source_target_pairs={{0,4},{4,0},{8,12},{12,8},{16,20},{20,16},{24,28},{28,24},{1,5},{5... | collective-permute-start | bytes 122888 | tf_op jit(solution)/shard_map/ppermute | solution.py:429
  86.2 3.9 %collective-permute-start.15 = (f32[1,32,256]{2,1,0:T(8,128)S(1)}, f32[1,32,256]{2,1,0:T(8,128)S(1)}, u32[]{:S(2)}, u32[]{:S(2)}) collective-permute-start(f32[1,32,256]{2,1,0:T(8,128)S(1)} %slice.57), channel_id=1, source_target_pairs={{0,2},{1,3},{2,0},{3,1},{4,6},{5,7},{6,4},{7,5},{8,10},{9,11},{10,... | collective-permute-start | bytes 98312 | tf_op jit(solution)/shard_map/ppermute | solution.py:429
  89.3 4.4 %collective-permute-start.13 = (f32[2,40,256]{2,1,0:T(8,128)S(1)}, f32[2,40,256]{2,1,0:T(8,128)S(1)}, u32[]{:S(2)}, u32[]{:S(2)}) collective-permute-start(f32[2,40,256]{2,1,0:T(8,128)S(1)} %pad_maximum_fusion.2), channel_id=1, source_target_pairs={{0,2},{1,3},{2,0},{3,1},{4,6},{5,7},{6,4},{7,5},{8,10},{9,11},{10,... | collective-permute-start | bytes 245768 | tf_op jit(solution)/shard_map/ppermute | solution.py:429
  90.2 4.3 %collective-permute-start.16 = (f32[2,32,256]{2,1,0:T(8,128)S(1)}, f32[2,32,256]{2,1,0:T(8,128)S(1)}, u32[]{:S(2)}, u32[]{:S(2)}) collective-permute-start(f32[2,32,256]{2,1,0:T(8,128)S(1)} %pad_maximum_fusion.4), channel_id=1, source_target_pairs={{0,4},{4,0},{8,12},{12,8},{16,20},{20,16},{24,28},{28,24},{1,5},{5... | collective-permute-start | bytes 196616 | tf_op jit(solution)/shard_map/ppermute | solution.py:429
  93.7 2.2 %collective-permute-start.14 = (f32[4,40,256]{2,1,0:T(8,128)S(1)}, f32[4,40,256]{2,1,0:T(8,128)S(1)}, u32[]{:S(2)}, u32[]{:S(2)}) collective-permute-start(f32[4,40,256]{2,1,0:T(8,128)S(1)} %pad_maximum_fusion.refs_0_), channel_id=1, source_target_pairs={{0,1},{1,0},{2,3},{3,2},{4,5},{5,4},{6,7},{7,6},{8,9},{9,8},{10,11... | collective-permute-start | bytes 491528 | tf_op jit(solution)/shard_map/ppermute | solution.py:429
  94.5 1.4 %collective-permute-start.17 = (f32[4,32,256]{2,1,0:T(8,128)S(1)}, f32[4,32,256]{2,1,0:T(8,128)S(1)}, u32[]{:S(2)}, u32[]{:S(2)}) collective-permute-start(f32[4,32,256]{2,1,0:T(8,128)S(1)} %pad_maximum_fusion.1.refs_2_), channel_id=1, source_target_pairs={{0,1},{1,0},{2,3},{3,2},{4,5},{5,4},{6,7},{7,6},{8,9},{9,8},{10,11... | collective-permute-start | bytes 393224 | tf_op jit(solution)/shard_map/ppermute | solution.py:429

commit v4 on v3

--- a/solution.py
+++ b/solution.py
@@ -11,8 +11,7 @@
 STEPS = 3
 STEP_SIZE = 0.25
 CHUNK = 1024
-LIMIT = 24 * 1024 * 1024
-PARTS = 8
+LIMIT = 56 * 1024 * 1024
 F32 = jnp.float32
 BF16 = jnp.bfloat16
 HIGHEST = lax.Precision.HIGHEST
@@ -34,16 +33,14 @@
     )
 
 
-def first_piece(at):
-    return ((at >> 2) & 1) | (at & 2) | ((at & 1) << 2)
-
-
-def second_piece(at):
-    return ((at >> 2) & 1) | ((at & 1) << 1) | ((at & 2) << 1)
-
-
-def second_place(piece):
-    return ((piece & 1) << 2) | ((piece >> 1) & 1) | ((piece >> 1) & 2)
+def halves(value):
+    half = value.shape[1] // 2
+    return jnp.concatenate([value[:, :half], value[:, half:]], 0)
+
+
+def whole(value):
+    half = value.shape[0] // 2
+    return jnp.concatenate([value[:half], value[half:]], 1)
 
 
 def force_product(panel, force):
@@ -110,46 +107,54 @@
 
 def tangent_kernel(
     pattern_ref,
-    place_ref,
-    field,
-    turned,
-    prev_ref,
-    next_ref,
-    left_ref,
-    right_ref,
+    field_any,
+    prev_any,
+    next_any,
+    left_any,
+    right_any,
+    turned_ref,
     tangent_ref,
     force_ref,
     gram_ref,
     load_ref,
     image_ref,
-    keep_first,
-    send_first,
-    keep_second,
-    send_second,
+    pack_ref,
+    field,
+    edges,
     mixed,
     rest,
     load,
-    packed,
-    halo,
+    sems,
 ):
-    rows, snaps = image_ref.shape
+    step = pl.program_id(0)
+    chunks = pl.num_programs(0) - 1
+    rows = chunks * CHUNK
+    snaps = image_ref.shape[1]
     block_count, coupled = pattern_ref.shape
     block = rows // block_count
     edge = HALO * block
-    chunks = rows // CHUNK
     per_chunk = CHUNK // block
-    for i, ref in enumerate((prev_ref, next_ref, left_ref, right_ref)):
-        high, low = split(ref[...])
-        at = pl.ds(i * edge, edge)
-        halo[at, :snaps] = high
-        halo[at, snaps:] = low
-    mixed[...] = jnp.zeros_like(mixed)
-    rest[...] = jnp.zeros_like(rest)
-    load[...] = load_ref[...]
-
-    @pl.loop(0, chunks)
-    def _(step):
-        start = pl.multiple_of(step * CHUNK, CHUNK)
+
+    @pl.when(step == 0)
+    def _():
+        copies = [pltpu.make_async_copy(field_any, field.at[pl.ds(0, rows), :], sems.at[4])]
+        for i, ref in enumerate((prev_any, next_any, left_any, right_any)):
+            copies.append(pltpu.make_async_copy(ref, edges.at[pl.ds(i * edge, edge), :], sems.at[i]))
+        for copy in reversed(copies):
+            copy.start()
+        for i in range(4):
+            copies[1 + i].wait()
+            high, low = split(edges[i * edge : (i + 1) * edge, :])
+            at = pl.ds(rows + i * edge, edge)
+            field[at, :snaps] = high
+            field[at, snaps:] = low
+        mixed[...] = jnp.zeros_like(mixed)
+        rest[...] = jnp.zeros_like(rest)
+        load[...] = load_ref[...]
+        copies[0].wait()
+
+    @pl.when(step < chunks)
+    def _():
         images = []
         for k in range(per_chunk):
             g = step * per_chunk + k
@@ -158,77 +163,85 @@
                 code = pattern_ref[g, e]
                 source = lax.div(code, block_count)
                 pick = lax.rem(code, block_count)
-                here = source == 0
                 tail = (source == 1) | (source == 3)
-                beyond = (source - 1) * HALO + jnp.where(tail, pick - (block_count - HALO), pick)
-                beyond = jnp.where(here, 0, beyond)
-                inner = field[pl.ds(pl.multiple_of(pick * block, block), block), :]
-                outer = halo[pl.ds(pl.multiple_of(beyond * block, block), block), :]
-                picked.append(lax.select(here, inner, outer))
-            own = pl.ds(pl.multiple_of(start + k * block, block), block)
+                base = jnp.where(source == 0, 0, block_count + (source - 1) * HALO)
+                place = base + jnp.where(tail, pick - (block_count - HALO), pick)
+                picked.append(field[pl.ds(pl.multiple_of(place * block, block), block), :])
+            own = slice(k * block, (k + 1) * block)
             both = matmul(tangent_ref[own, :], jnp.concatenate(picked, 0))
             image = STEP_SIZE * (both[:, :snaps] + both[:, snaps:])
             image_ref[own, :] = image
             images.append(image)
         image = jnp.concatenate(images, 0)
-        load[...] += force_product(image, force_ref[pl.ds(pl.multiple_of(step * per_chunk, per_chunk), per_chunk), :])
+        load[...] += force_product(image, force_ref[...])
         high, low = split(image)
         high_turned = high.T
-        panels = turned[:, pl.ds(start, CHUNK)]
+        panels = turned_ref[...]
         mixed[...] += matmul(jnp.concatenate([panels, high_turned], 0), high)
         rest[...] += matmul(jnp.concatenate([panels[:snaps], high_turned], 0), low)
 
-    gram = gram_ref[:, :snaps] + gram_ref[:, snaps:] + gram_ref[:, snaps:].T
-    cross = mixed[:snaps] + mixed[snaps : 2 * snaps] + rest[:snaps]
-    square = mixed[2 * snaps :] + rest[snaps:] + rest[snaps:].T
-    row = lax.broadcasted_iota(jnp.int32, (snaps, snaps), 0)
-    column = lax.broadcasted_iota(jnp.int32, (snaps, snaps), 1)
-    diagonal = jnp.sum(jnp.where(row == column, square, 0.0), 0, keepdims=True)
-    packed[0] = jnp.where(row <= column, gram, square)
-    packed[1] = cross
-    extra_row = lax.broadcasted_iota(jnp.int32, (8, snaps), 0)
-    extra = jnp.where(extra_row == 0, load[...], jnp.where(extra_row == 1, diagonal, 0.0))
-    share = snaps // PARTS
-    for at in range(PARTS):
-        first = keep_first if at < PARTS // 2 else send_first
-        second = keep_second if at < PARTS // 2 else send_second
-        slot = at % (PARTS // 2)
-        begin = pl.multiple_of((place_ref[0] ^ first_piece(at)) * share, 8)
-        first[slot, :share, :] = packed[0, pl.ds(begin, share), :]
-        first[slot, share:, :] = extra
-        begin = pl.multiple_of((place_ref[0] ^ second_piece(at)) * share, 8)
-        second[slot] = packed[1, pl.ds(begin, share), :]
-
-
-def tangent_call(field, turned, halos, tangent, pattern, force, gram, load, place):
+    @pl.when(step == chunks)
+    def _():
+        gram = gram_ref[:, :snaps] + gram_ref[:, snaps:] + gram_ref[:, snaps:].T
+        cross = mixed[:snaps] + mixed[snaps : 2 * snaps] + rest[:snaps]
+        square = mixed[2 * snaps :] + rest[snaps:] + rest[snaps:].T
+        row = lax.broadcasted_iota(jnp.int32, (snaps, snaps), 0)
+        column = lax.broadcasted_iota(jnp.int32, (snaps, snaps), 1)
+        diagonal = jnp.sum(jnp.where(row == column, square, 0.0), 0, keepdims=True)
+        first = halves(jnp.where(row <= column, gram, square))
+        second = halves(cross)
+        vectors = jnp.concatenate([halves(load[...]), halves(diagonal), jnp.zeros((4, snaps // 2), F32)], 0)
+        share = 2 * snaps // pack_ref.shape[0]
+        for k in range(pack_ref.shape[0]):
+            own = slice(k * share, (k + 1) * share)
+            pack_ref[k, :share, :] = first[own]
+            pack_ref[k, share : 2 * share, :] = second[own]
+            pack_ref[k, 2 * share :, :] = vectors
+
+
+def tangent_call(field, turned, halos, tangent, pattern, force, gram, load, devices):
     rows = tangent.shape[0]
     snaps = gram.shape[0]
-    share = snaps // PARTS
-    vmem = pl.BlockSpec(memory_space=pltpu.VMEM)
-    smem = pl.BlockSpec(memory_space=pltpu.SMEM)
-    first = jax.ShapeDtypeStruct((PARTS // 2, share + 8, snaps), F32)
-    second = jax.ShapeDtypeStruct((PARTS // 2, share, snaps), F32)
+    block = force.shape[1]
+    chunks = rows // CHUNK
+    share = 2 * snaps // devices
+    hbm = pl.BlockSpec(memory_space=pl.ANY)
+    last = lambda i: jnp.minimum(i, chunks - 1)
+    piece = (devices, 2 * share + 8, snaps // 2)
     return pl.pallas_call(
         tangent_kernel,
-        out_shape=(
-            jax.ShapeDtypeStruct((rows, snaps), F32),
-            first,
-            first,
-            second,
-            second,
+        out_shape=(jax.ShapeDtypeStruct((rows, snaps), F32), jax.ShapeDtypeStruct(piece, F32)),
+        grid_spec=pltpu.PrefetchScalarGridSpec(
+            num_scalar_prefetch=1,
+            grid=(chunks + 1,),
+            in_specs=[
+                hbm,
+                hbm,
+                hbm,
+                hbm,
+                hbm,
+                pl.BlockSpec((2 * snaps, CHUNK), lambda i, _: (0, last(i))),
+                pl.BlockSpec((CHUNK, tangent.shape[1]), lambda i, _: (last(i), 0)),
+                pl.BlockSpec((CHUNK // block, block), lambda i, _: (last(i), 0)),
+                pl.BlockSpec((snaps, 2 * snaps), lambda i, _: (0, 0)),
+                pl.BlockSpec((1, snaps), lambda i, _: (0, 0)),
+            ],
+            out_specs=[
+                pl.BlockSpec((CHUNK, snaps), lambda i, _: (last(i), 0)),
+                pl.BlockSpec(piece, lambda i, _: (0, 0, 0)),
+            ],
+            scratch_shapes=[
+                pltpu.VMEM((rows + 4 * HALO * block, 2 * snaps), BF16),
+                pltpu.VMEM((4 * HALO * block, snaps), F32),
+                pltpu.VMEM((3 * snaps, snaps), F32),
+                pltpu.VMEM((2 * snaps, snaps), F32),
+                pltpu.VMEM((1, snaps), F32),
+                pltpu.SemaphoreType.DMA((5,)),
+            ],
         ),
-        in_specs=[smem, smem] + [vmem] * 10,
-        out_specs=[vmem] * 5,
-        scratch_shapes=[
-            pltpu.VMEM((3 * snaps, snaps), F32),
-            pltpu.VMEM((2 * snaps, snaps), F32),
-            pltpu.VMEM((1, snaps), F32),
-            pltpu.VMEM((2, snaps, snaps), F32),
-            pltpu.VMEM((4 * halos[0].shape[0], 2 * snaps), BF16),
-        ],
         compiler_params=pltpu.CompilerParams(vmem_limit_bytes=LIMIT),
         name="tangent",
-    )(pattern, place, field, turned, *halos, tangent, force, gram, load)
+    )(pattern, field, *halos, turned, tangent, force, gram, load)
 
 
 def inverse_factors(blocks):
@@ -281,16 +294,15 @@
     )
 
 
-def reduced_system(inverse_count, place, first, second, index):
-    snaps = first.shape[2]
-    share = snaps // PARTS
-    half = snaps // 2
-    order = [first_piece(place ^ c) for c in range(PARTS)]
-    packed = jnp.concatenate([first[at, :share, :] for at in order], 0) * inverse_count
-    load = first[0, share : share + 1, :] * inverse_count
-    diagonal = first[0, share + 1 : share + 2, :] * inverse_count
-    order = [second_place(place ^ c) for c in range(PARTS)]
-    cross = jnp.concatenate([second[at] for at in order], 0) * inverse_count
+def reduced_system(inverse_count, pack, index):
+    pieces, depth, half = pack.shape
+    snaps = 2 * half
+    share = 2 * snaps // pieces
+    packed = whole(jnp.concatenate([pack[k, :share, :] for k in range(pieces)], 0)) * inverse_count
+    cross = whole(jnp.concatenate([pack[k, share : 2 * share, :] for k in range(pieces)], 0)) * inverse_count
+    vectors = pack[0, 2 * share :, :] * inverse_count
+    load = whole(vectors[0:2])
+    diagonal = whole(vectors[2:4])
     row = lax.broadcasted_iota(jnp.int32, (snaps, snaps), 0)
     column = lax.broadcasted_iota(jnp.int32, (snaps, snaps), 1)
     turned = packed.T
@@ -332,20 +344,35 @@
     return root, history, state - old, state
 
 
-def final_kernel(inverse_count, place_ref, *refs):
-    pieces = refs[:4]
-    index_ref, force_ref, image, snap_any, basis_any, coeff_ref, residual_ref = refs[4:11]
-    snap, first, second, root_ref, change_ref, state_ref, tile, sems = refs[11:]
+def final_kernel(
+    inverse_count,
+    pack_ref,
+    index_ref,
+    force_ref,
+    snap_any,
+    image_any,
+    basis_any,
+    coeff_ref,
+    residual_ref,
+    snap,
+    image,
+    root_ref,
+    change_ref,
+    state_ref,
+    tile,
+    sems,
+):
     rows, snaps = snap.shape
     block = force_ref.shape[1]
     chunks = rows // CHUNK
     per_chunk = CHUNK // block
-    copy = pltpu.make_async_copy(snap_any, snap, sems.at[chunks])
-    copy.start()
-    for i, pack in enumerate((first, second)):
-        pack[: PARTS // 2] = pieces[2 * i][...]
-        pack[PARTS // 2 :] = pieces[2 * i + 1][...]
-    root, history, change, state = reduced_system(inverse_count, place_ref[0], first, second, index_ref[...])
+    copies = [
+        pltpu.make_async_copy(snap_any, snap, sems.at[chunks]),
+        pltpu.make_async_copy(image_any, image, sems.at[chunks + 1]),
+    ]
+    for copy in copies:
+        copy.start()
+    root, history, change, state = reduced_system(inverse_count, pack_ref, index_ref[...])
     high, low = split(root)
     root_ref[:, :snaps] = high
     root_ref[:, snaps:] = low
@@ -353,7 +380,8 @@
         coeff_ref[n : n + 1, :] = history[n]
     change_ref[...] = change
     state_ref[...] = state
-    copy.wait()
+    for copy in copies:
+        copy.wait()
     tile[...] = jnp.zeros_like(tile)
     lane = lax.broadcasted_iota(jnp.int32, (block, block), 1)
 
@@ -382,10 +410,9 @@
         out_copy(i).wait()
 
 
-def final_call(pieces, step_index, place, snapshots, image, force, inverse_count):
+def final_call(pack, step_index, snapshots, image, force, inverse_count):
     rows, snaps = snapshots.shape
     block = force.shape[1]
-    share = snaps // PARTS
     vmem = pl.BlockSpec(memory_space=pltpu.VMEM)
     hbm = pl.BlockSpec(memory_space=pl.ANY)
     return pl.pallas_call(
@@ -395,21 +422,20 @@
             jax.ShapeDtypeStruct((STEPS, snaps), F32),
             jax.ShapeDtypeStruct(force.shape, F32),
         ),
-        in_specs=[pl.BlockSpec(memory_space=pltpu.SMEM)] + [vmem] * 7 + [hbm],
+        in_specs=[vmem, vmem, vmem, hbm, hbm],
         out_specs=[hbm, vmem, vmem],
         scratch_shapes=[
             pltpu.VMEM((rows, snaps), F32),
-            pltpu.VMEM((PARTS, share + 8, snaps), F32),
-            pltpu.VMEM((PARTS, share, snaps), F32),
+            pltpu.VMEM((rows, snaps), F32),
             pltpu.VMEM((snaps, 2 * snaps), BF16),
             pltpu.VMEM((1, snaps), F32),
             pltpu.VMEM((1, snaps), F32),
             pltpu.VMEM((block, block), F32),
-            pltpu.SemaphoreType.DMA((rows // CHUNK + 1,)),
+            pltpu.SemaphoreType.DMA((rows // CHUNK + 2,)),
         ],
         compiler_params=pltpu.CompilerParams(vmem_limit_bytes=LIMIT),
         name="final",
-    )(place, *pieces, step_index, force, image, snapshots)
+    )(pack, step_index, force, snapshots, image)
 
 
 def shifted(value, axis, steps):
@@ -424,31 +450,18 @@
     return lax.ppermute(shard, axis, pairs)
 
 
-def partner(value, axis, bit):
-    count = lax.axis_size(axis)
-    return lax.ppermute(value, axis, [(i, i ^ bit) for i in range(count)])
-
-
-def reduce_packed(keep_first, send_first, keep_second, send_second):
-    core, x, y = ("zone", 1), ("zone", 2), ("rows", 1)
-    first = keep_first + partner(send_first, *core)
-    second = keep_second + partner(send_second, *core)
-    for way_first, way_second in ((x, y), (y, x)):
-        half = first.shape[0] // 2
-        first = first[:half] + partner(first[half:], *way_first)
-        second = second[:half] + partner(second[half:], *way_second)
-    edge = first.shape[1]
-    value = jnp.concatenate([first, second], 1)
-    for axis, least in (("rows", 2), ("zone", 4)):
-        bit = least
-        while bit < lax.axis_size(axis):
-            value = value + partner(value, axis, bit)
-            bit *= 2
-    first, second = value[:, :edge], value[:, edge:]
-    for way_first, way_second in ((y, x), (x, y)):
-        first = jnp.concatenate([first, partner(first, *way_first)], 0)
-        second = jnp.concatenate([second, partner(second, *way_second)], 0)
-    return first, partner(first, *core), second, partner(second, *core)
+def exchange(value, axis):
+    return lax.all_to_all(value, axis, 0, 0, tiled=True)
+
+
+def reduce_pieces(pack):
+    zones, lines = lax.axis_size("zone"), lax.axis_size("rows")
+    value = pack.reshape((zones, lines) + pack.shape[1:])
+    value = exchange(value, "zone").sum(0)
+    value = exchange(value, "rows").sum(0)
+    value = exchange(jnp.broadcast_to(value, (lines,) + value.shape), "rows")
+    value = exchange(jnp.broadcast_to(value, (zones,) + value.shape), "zone")
+    return value.reshape(pack.shape)
 
 
 def shards(snapshots, tangent, pattern, forcing, step_index):
@@ -456,9 +469,8 @@
     blocks = pattern.shape[0]
     block = rows // blocks
     edge = HALO * block
-    inverse_count = 1.0 / (rows * lax.axis_size("rows") * lax.axis_size("zone"))
-    place = (lax.axis_index("zone") & 3) | ((lax.axis_index("rows") & 1) << 2)
-    place = jnp.reshape(place, (1,)).astype(jnp.int32)
+    devices = lax.axis_size("rows") * lax.axis_size("zone")
+    inverse_count = 1.0 / (rows * devices)
     force = forcing.reshape(blocks, block)
     head, tail = snapshots[:edge], snapshots[rows - edge :]
     rows_prev = shifted(tail, "rows", 1)
@@ -466,10 +478,9 @@
     field, turned, gram, load = gram_call(snapshots, force)
     head, tail, load = lax.optimization_barrier((head, tail, load))
     halos = (rows_prev, rows_next, from_behind(tail, "zone", 1), from_behind(head, "zone", -1))
-    image, *packed = tangent_call(field, turned, halos, tangent, pattern, force, gram, load, place)
-    pieces = reduce_packed(*packed)
+    image, pack = tangent_call(field, turned, halos, tangent, pattern, force, gram, load, devices)
     basis, coefficients, residual = final_call(
-        pieces, step_index.reshape(1, snaps), place, snapshots, image, force, inverse_count
+        reduce_pieces(pack), step_index.reshape(1, snaps), snapshots, image, force, inverse_count
     )
     return basis, coefficients, residual.reshape(rows)
 

time: 117 us -> 133 us (1.14)
  blocking collectives: 0 us -> 54.7 us
  waiting for transfers between devices: 24.1 us -> 3.7 us
  starting transfers between devices: 26.9 us -> 8.85 us
  local copies, waits for them, and re-layouts: 20.1 us -> 3.19 us
  Pallas kernels: 44.6 us -> 60.3 us
    all_to_all x0 -> x4, blocking collectives: none -> 54.7 us  [exchange(): return lax.all_to_all(value, axis, 0, 0, tiled=True)]
    ppermute x14 -> x0, waiting for transfers between devices: 20.2 us -> none  [partner(): return lax.ppermute(value, axis, [(i, i ^ bit) for i in range(count)])]
    ppermute x14 -> x0, starting transfers between devices: 18.1 us -> none  [partner(): return lax.ppermute(value, axis, [(i, i ^ bit) for i in range(count)])]
    unnamed x23 -> x11, local copies, waits for them, and re-layouts: 17.9 us -> 1.86 us
    pallas_call x1, Pallas kernels: 6.74 us -> 13.1 us  [gram_call(): pl.pallas_call(gram_kernel, out_shape=(jax.ShapeDtypeStruct((rows, 2 * sn...]
    pallas_call x1, Pallas kernels: 17.1 us -> 22.1 us  [tangent_call(): pl.pallas_call(tangent_kernel, out_shape=(jax.ShapeDtypeStruct((rows, sna...]
    pallas_call x1, Pallas kernels: 20.8 us -> 25.1 us  [final_call(): pl.pallas_call(functools.partial(final_kernel, inverse_count), out_shape=...]
    ppermute x2, waiting for transfers between devices: 3.91 us -> 0.01 us  [from_behind(): return lax.ppermute(shard, axis, pairs)]
  transfers between devices with their start and end apart: 18 -> 4, of which waited for: 14 -> 2; matrix products, arithmetic and copies ran while one was open for 0% -> 1% of each run, Pallas kernels for 6% -> 10%
where the time goes in v4:
time: 133 us; the launch traced here: 132 us
  Pallas kernels  60.3 us (45%)
  blocking collectives  54.7 us (41%)
  starting transfers between devices  8.85 us (7%)
  waiting for transfers between devices  3.7 us (3%)
  local copies, waits for them, and re-layouts  3.19 us (2%)
    all_to_all x4, blocking collectives, exchange(): return lax.all_to_all(value, axis, 0, 0, tiled=True)  54.7 us
    pallas_call x1, Pallas kernels, final_call(): pl.pallas_call(functools.partial(final_kernel, inverse_count), out_shape=...  25.1 us
    pallas_call x1, Pallas kernels, tangent_call(): pl.pallas_call(tangent_kernel, out_shape=(jax.ShapeDtypeStruct((rows, sna...  22.1 us
    pallas_call x1, Pallas kernels, gram_call(): pl.pallas_call(gram_kernel, out_shape=(jax.ShapeDtypeStruct((rows, 2 * sn...  13.1 us
    ppermute x2, starting transfers between devices, shifted(): return lax.ppermute(value, axis, pairs)  6.06 us
    ppermute x2, waiting for transfers between devices, shifted(): return lax.ppermute(value, axis, pairs)  3.7 us
    ppermute x2, starting transfers between devices, from_behind(): return lax.ppermute(shard, axis, pairs)  2.79 us
  transfers between devices with their start and end apart: 4, of which 2 were waited for; matrix products, arithmetic and copies ran while one was open for 1% of the time, Pallas kernels for 10%

profile of v4, /device:TPU:0, one launch (start us, length us, event | category | flops | bytes accessed | tf_op | source)
XLA Modules:
  0.0 131.6 jit_solution(12394022964599695498)
XLA Ops:
  0.6 0.0 copy-start.4
  0.6 1.3 fusion
  1.9 6.1 %collective-permute-start.1 = (f32[512,256]{1,0:T(8,128)S(1)}, f32[512,256]{1,0:T(8,128)S(1)}, u32[]{:S(2)}, u32[]{:S(2)}) collective-permute-start(f32[512,256]{1,0:T(8,128)S(1)} %get-tuple-element.18), channel_id=1, source_target_pairs={{0,28},{4,0},{8,4},{12,8},{16,12},{20,16},{24,20},{28,24},{1,29},{... | collective-permute-start | bytes 1572872 | tf_op jit(solution)/shard_map/ppermute | solution.py:444
  8.0 0.0 collective-permute-start
  8.0 13.1 %gram.1 = (bf16[8192,512]{1,0:T(8,128)(2,1)}, bf16[512,8192]{1,0:T(8,128)(2,1)}, f32[256,512]{1,0:T(8,128)}, f32[1,256]{1,0:T(1,128)}) custom-call(f32[8192,256]{1,0:T(8,128)} %snap_any.1, f32[64,128]{1,0:T(8,128)} %bitcast.7), custom_call_target="tpu_custom_call" | custom-call | flops 2147483648 | bytes 25165824 | tf_op jit(solution)/shard_map/gram/pallas_call | solution.py:81
  21.0 1.5 %collective-permute-start.2 = (f32[512,256]{1,0:T(8,128)S(1)}, f32[512,256]{1,0:T(8,128)S(1)}, u32[]{:S(2)}, u32[]{:S(2)}) collective-permute-start(f32[512,256]{1,0:T(8,128)S(1)} %get-tuple-element.17), channel_id=1, source_target_pairs={{0,1},{1,2},{2,3},{4,5},{5,6},{6,7},{8,9},{9,10},{10,11},{12,13},{... | collective-permute-start | bytes 1572872 | tf_op jit(solution)/shard_map/ppermute | solution.py:450
  22.5 1.3 collective-permute-start.3
  23.8 0.0 copy-done.4
  23.8 0.7 copy.9.pattern_ref
  24.6 3.5 %collective-permute-done.1.next_any = f32[512,256]{1,0:T(8,128)S(1)} collective-permute-done((f32[512,256]{1,0:T(8,128)S(1)}, f32[512,256]{1,0:T(8,128)S(1)}, u32[]{:S(2)}, u32[]{:S(2)}) %collective-permute-start.1) | collective-permute-done | bytes 524320 | tf_op jit(solution)/shard_map/ppermute | solution.py:444
  28.1 0.0 copy-start
  28.1 0.2 collective-permute-done.prev_any
  28.3 0.0 copy-start.1
  28.3 0.0 collective-permute-done.2.left_any
  28.3 0.0 copy-start.2
  28.3 0.0 collective-permute-done.3.right_any
  28.3 0.0 copy-start.3
  28.3 0.6 copy-done
  28.9 0.2 copy-done.1
  29.1 0.2 copy-done.2
  29.3 0.2 copy-done.3
  29.4 22.1 %tangent.1 = (f32[8192,256]{1,0:T(8,128)}, f32[32,40,128]{2,1,0:T(8,128)}) custom-call(s32[64,4]{1,0:T(8,128)} %copy.9.pattern_ref, bf16[8192,512]{1,0:T(8,128)(2,1)} %get-tuple-element.15.field_any, f32[512,256]{1,0:T(8,128)} %copy-done.1, f32[512,256]{1,0:T(8,128)} %copy-done, f32[512,256]{1,0:T(8,128)} %copy-done.2, f32[512,256]{1,0:T(8,128)} %copy-done.3, ...), custom_call_target="tpu_custom_call" | custom-call | tf_op jit(solution)/shard_map/tangent/pallas_call | solution.py:211
  51.6 18.0 %all_to_all.20 = f32[4,8,40,128]{3,2,1,0:T(8,128)S(1)} all-to-all(f32[4,8,40,128]{3,2,1,0:T(8,128)} %bitcast.6), channel_id=1, replica_groups=mesh['rows'=8,'zone'=4] {'zone'}, dimensions={0} | all-to-all | bytes 1310720 | tf_op jit(solution)/shard_map/all_to_all | solution.py:454
  69.6 13.4 %all_to_all.21 = f32[8,40,128]{2,1,0:T(8,128)S(1)} all-to-all(f32[8,40,128]{2,1,0:T(8,128)S(1)} %reduce_sum.18), channel_id=1, replica_groups=mesh['rows'=8,'zone'=4] {'rows'}, dimensions={0} | all-to-all | bytes 327680 | tf_op jit(solution)/shard_map/all_to_all | solution.py:454
  83.0 10.0 %all_to_all.22 = f32[8,40,128]{2,1,0:T(8,128)S(1)} all-to-all(f32[8,40,128]{2,1,0:T(8,128)S(1)} %broadcast_in_dim.6), channel_id=1, replica_groups=mesh['rows'=8,'zone'=4] {'rows'}, dimensions={0} | all-to-all | bytes 327680 | tf_op jit(solution)/shard_map/all_to_all | solution.py:454
  93.0 13.4 %all_to_all.23 = f32[4,8,40,128]{3,2,1,0:T(8,128)} all-to-all(f32[4,8,40,128]{3,2,1,0:T(8,128)S(1)} %broadcast_in_dim.7), channel_id=1, replica_groups=mesh['rows'=8,'zone'=4] {'zone'}, dimensions={0} | all-to-all | bytes 1310720 | tf_op jit(solution)/shard_map/all_to_all | solution.py:454
  106.4 25.1 %final.1 = (f32[8192,256]{1,0:T(8,128)}, f32[3,256]{1,0:T(4,128)}, f32[64,128]{1,0:T(8,128)}) custom-call(f32[32,40,128]{2,1,0:T(8,128)} %bitcast.5, s32[1,256]{1,0:T(1,128)} %bitcast.10, f32[64,128]{1,0:T(8,128)} %bitcast.9, f32[8192,256]{1,0:T(8,128)} %snap_any.1, f32[8192,256]{1,0:T(8,128)} %get-tuple-element.23.image_any), custom_call_target="tpu_custom_call" | custom-call | tf_op jit(solution)/shard_map/final/pallas_call | solution.py:418
  (4 shorter events, 0.1 us)
Async XLA Ops:
  0.6 23.2 %copy-start.4 = (s32[64,4]{0,1:T(4,128)S(1)}, s32[64,4]{0,1:T(4,128)}, u32[]{:S(2)}) copy-start(s32[64,4]{0,1:T(4,128)} %param.7) | copy-start | bytes 3076
  1.9 26.2 %collective-permute-start.1 = (f32[512,256]{1,0:T(8,128)S(1)}, f32[512,256]{1,0:T(8,128)S(1)}, u32[]{:S(2)}, u32[]{:S(2)}) collective-permute-start(f32[512,256]{1,0:T(8,128)S(1)} %get-tuple-element.18), channel_id=1, source_target_pairs={{0,28},{4,0},{8,4},{12,8},{16,12},{20,16},{24,20},{28,24},{1,29},{... | collective-permute-start | bytes 1572872 | tf_op jit(solution)/shard_map/ppermute | solution.py:444
  8.0 20.3 %collective-permute-start = (f32[512,256]{1,0:T(8,128)S(1)}, f32[512,256]{1,0:T(8,128)S(1)}, u32[]{:S(2)}, u32[]{:S(2)}) collective-permute-start(f32[512,256]{1,0:T(8,128)S(1)} %get-tuple-element.17), channel_id=1, source_target_pairs={{0,4},{4,8},{8,12},{12,16},{16,20},{20,24},{24,28},{28,0},{1,5},{5... | collective-permute-start | bytes 1572872 | tf_op jit(solution)/shard_map/ppermute | solution.py:444
  21.0 7.2 %collective-permute-start.2 = (f32[512,256]{1,0:T(8,128)S(1)}, f32[512,256]{1,0:T(8,128)S(1)}, u32[]{:S(2)}, u32[]{:S(2)}) collective-permute-start(f32[512,256]{1,0:T(8,128)S(1)} %get-tuple-element.17), channel_id=1, source_target_pairs={{0,1},{1,2},{2,3},{4,5},{5,6},{6,7},{8,9},{9,10},{10,11},{12,13},{... | collective-permute-start | bytes 1572872 | tf_op jit(solution)/shard_map/ppermute | solution.py:450
  22.5 5.7 %collective-permute-start.3 = (f32[512,256]{1,0:T(8,128)S(1)}, f32[512,256]{1,0:T(8,128)S(1)}, u32[]{:S(2)}, u32[]{:S(2)}) collective-permute-start(f32[512,256]{1,0:T(8,128)S(1)} %get-tuple-element.18), channel_id=1, source_target_pairs={{1,0},{2,1},{3,2},{5,4},{6,5},{7,6},{9,8},{10,9},{11,10},{13,12},{... | collective-permute-start | bytes 1572872 | tf_op jit(solution)/shard_map/ppermute | solution.py:450
  28.1 0.8 copy-start
  28.3 0.8 copy-start.1
  28.3 1.0 copy-start.2
  28.3 1.2 copy-start.3

commit v5 on v3

--- a/solution.py
+++ b/solution.py
@@ -11,7 +11,7 @@
 STEPS = 3
 STEP_SIZE = 0.25
 CHUNK = 1024
-LIMIT = 24 * 1024 * 1024
+LIMIT = 56 * 1024 * 1024
 PARTS = 8
 F32 = jnp.float32
 BF16 = jnp.bfloat16
@@ -111,45 +111,84 @@
 def tangent_kernel(
     pattern_ref,
     place_ref,
-    field,
-    turned,
-    prev_ref,
-    next_ref,
-    left_ref,
-    right_ref,
-    tangent_ref,
+    field_any,
+    left_any,
+    right_any,
+    prev_any,
+    next_any,
+    turned_any,
+    tangent_any,
     force_ref,
     gram_ref,
     load_ref,
-    image_ref,
+    image_any,
     keep_first,
     send_first,
     keep_second,
     send_second,
+    field,
+    edges,
+    turned,
+    tangent,
+    image,
     mixed,
     rest,
     load,
     packed,
-    halo,
+    field_sems,
+    edge_sems,
+    turned_sems,
+    tangent_sems,
+    image_sems,
 ):
-    rows, snaps = image_ref.shape
+    rows, snaps = image.shape
     block_count, coupled = pattern_ref.shape
     block = rows // block_count
     edge = HALO * block
     chunks = rows // CHUNK
     per_chunk = CHUNK // block
-    for i, ref in enumerate((prev_ref, next_ref, left_ref, right_ref)):
-        high, low = split(ref[...])
-        at = pl.ds(i * edge, edge)
-        halo[at, :snaps] = high
-        halo[at, snaps:] = low
+
+    def chunk(i):
+        return pl.ds(pl.multiple_of(i * CHUNK, CHUNK), CHUNK)
+
+    def field_copy(i):
+        return pltpu.make_async_copy(field_any.at[chunk(i), :], field.at[chunk(i), :], field_sems.at[i])
+
+    def turned_copy(i):
+        return pltpu.make_async_copy(turned_any.at[:, chunk(i)], turned.at[i], turned_sems.at[i])
+
+    def tangent_copy(i):
+        return pltpu.make_async_copy(tangent_any.at[chunk(i), :], tangent.at[chunk(i), :], tangent_sems.at[i])
+
+    def image_copy(i):
+        return pltpu.make_async_copy(image.at[chunk(i), :], image_any.at[chunk(i), :], image_sems.at[i])
+
+    edge_copies = []
+    for i, ref in enumerate((left_any, right_any, prev_any, next_any)):
+        edge_copies.append(pltpu.make_async_copy(ref, edges.at[pl.ds(i * edge, edge), :], edge_sems.at[i]))
+        edge_copies[-1].start()
+    for i in range(chunks):
+        field_copy(i).start()
+    for i in range(chunks):
+        tangent_copy(i).start()
+        turned_copy(i).start()
+    for i in range(4):
+        edge_copies[i].wait()
+        high, low = split(edges[i * edge : (i + 1) * edge, :])
+        at = pl.ds(rows + i * edge, edge)
+        field[at, :snaps] = high
+        field[at, snaps:] = low
     mixed[...] = jnp.zeros_like(mixed)
     rest[...] = jnp.zeros_like(rest)
     load[...] = load_ref[...]
+    for i in range(chunks):
+        field_copy(i).wait()
 
     @pl.loop(0, chunks)
     def _(step):
         start = pl.multiple_of(step * CHUNK, CHUNK)
+        tangent_copy(step).wait()
+        turned_copy(step).wait()
         images = []
         for k in range(per_chunk):
             g = step * per_chunk + k
@@ -158,23 +197,22 @@
                 code = pattern_ref[g, e]
                 source = lax.div(code, block_count)
                 pick = lax.rem(code, block_count)
-                here = source == 0
                 tail = (source == 1) | (source == 3)
-                beyond = (source - 1) * HALO + jnp.where(tail, pick - (block_count - HALO), pick)
-                beyond = jnp.where(here, 0, beyond)
-                inner = field[pl.ds(pl.multiple_of(pick * block, block), block), :]
-                outer = halo[pl.ds(pl.multiple_of(beyond * block, block), block), :]
-                picked.append(lax.select(here, inner, outer))
+                base = jnp.where(source == 0, 0, block_count + ((source + 1) & 3) * HALO)
+                at = base + jnp.where(tail, pick - (block_count - HALO), pick)
+                picked.append(field[pl.ds(pl.multiple_of(at * block, block), block), :])
             own = pl.ds(pl.multiple_of(start + k * block, block), block)
-            both = matmul(tangent_ref[own, :], jnp.concatenate(picked, 0))
-            image = STEP_SIZE * (both[:, :snaps] + both[:, snaps:])
-            image_ref[own, :] = image
-            images.append(image)
-        image = jnp.concatenate(images, 0)
-        load[...] += force_product(image, force_ref[pl.ds(pl.multiple_of(step * per_chunk, per_chunk), per_chunk), :])
-        high, low = split(image)
+            both = matmul(tangent[own, :], jnp.concatenate(picked, 0))
+            part = STEP_SIZE * (both[:, :snaps] + both[:, snaps:])
+            image[own, :] = part
+            images.append(part)
+        image_copy(step).start()
+        panel = jnp.concatenate(images, 0)
+        line = pl.ds(pl.multiple_of(step * per_chunk, per_chunk), per_chunk)
+        load[...] += force_product(panel, force_ref[line, :])
+        high, low = split(panel)
         high_turned = high.T
-        panels = turned[:, pl.ds(start, CHUNK)]
+        panels = turned[step]
         mixed[...] += matmul(jnp.concatenate([panels, high_turned], 0), high)
         rest[...] += matmul(jnp.concatenate([panels[:snaps], high_turned], 0), low)
 
@@ -199,36 +237,46 @@
         begin = pl.multiple_of((place_ref[0] ^ second_piece(at)) * share, 8)
         second[slot] = packed[1, pl.ds(begin, share), :]
 
+    @pl.loop(0, chunks)
+    def _(step):
+        image_copy(step).wait()
+
 
 def tangent_call(field, turned, halos, tangent, pattern, force, gram, load, place):
-    rows = tangent.shape[0]
+    rows, width = tangent.shape
     snaps = gram.shape[0]
     share = snaps // PARTS
+    chunks = rows // CHUNK
+    edge = halos[0].shape[0]
     vmem = pl.BlockSpec(memory_space=pltpu.VMEM)
     smem = pl.BlockSpec(memory_space=pltpu.SMEM)
+    hbm = pl.BlockSpec(memory_space=pl.ANY)
     first = jax.ShapeDtypeStruct((PARTS // 2, share + 8, snaps), F32)
     second = jax.ShapeDtypeStruct((PARTS // 2, share, snaps), F32)
     return pl.pallas_call(
         tangent_kernel,
-        out_shape=(
-            jax.ShapeDtypeStruct((rows, snaps), F32),
-            first,
-            first,
-            second,
-            second,
-        ),
-        in_specs=[smem, smem] + [vmem] * 10,
-        out_specs=[vmem] * 5,
+        out_shape=(jax.ShapeDtypeStruct((rows, snaps), F32), first, first, second, second),
+        in_specs=[smem, smem] + [hbm] * 7 + [vmem] * 3,
+        out_specs=[hbm] + [vmem] * 4,
         scratch_shapes=[
+            pltpu.VMEM((rows + 4 * edge, 2 * snaps), BF16),
+            pltpu.VMEM((4 * edge, snaps), F32),
+            pltpu.VMEM((chunks, 2 * snaps, CHUNK), BF16),
+            pltpu.VMEM((rows, width), BF16),
+            pltpu.VMEM((rows, snaps), F32),
             pltpu.VMEM((3 * snaps, snaps), F32),
             pltpu.VMEM((2 * snaps, snaps), F32),
             pltpu.VMEM((1, snaps), F32),
             pltpu.VMEM((2, snaps, snaps), F32),
-            pltpu.VMEM((4 * halos[0].shape[0], 2 * snaps), BF16),
+            pltpu.SemaphoreType.DMA((chunks,)),
+            pltpu.SemaphoreType.DMA((4,)),
+            pltpu.SemaphoreType.DMA((chunks,)),
+            pltpu.SemaphoreType.DMA((chunks,)),
+            pltpu.SemaphoreType.DMA((chunks,)),
         ],
         compiler_params=pltpu.CompilerParams(vmem_limit_bytes=LIMIT),
         name="tangent",
-    )(pattern, place, field, turned, *halos, tangent, force, gram, load)
+    )(pattern, place, field, *halos, turned, tangent, force, gram, load)
 
 
 def inverse_factors(blocks):
@@ -332,19 +380,56 @@
     return root, history, state - old, state
 
 
-def final_kernel(inverse_count, place_ref, *refs):
-    pieces = refs[:4]
-    index_ref, force_ref, image, snap_any, basis_any, coeff_ref, residual_ref = refs[4:11]
-    snap, first, second, root_ref, change_ref, state_ref, tile, sems = refs[11:]
+def final_kernel(
+    inverse_count,
+    place_ref,
+    first_low,
+    first_high,
+    second_low,
+    second_high,
+    index_ref,
+    force_ref,
+    snap_any,
+    image_any,
+    basis_any,
+    coeff_ref,
+    residual_ref,
+    snap,
+    image,
+    first,
+    second,
+    root_ref,
+    change_ref,
+    state_ref,
+    tile,
+    snap_sems,
+    image_sems,
+    basis_sems,
+):
     rows, snaps = snap.shape
     block = force_ref.shape[1]
     chunks = rows // CHUNK
     per_chunk = CHUNK // block
-    copy = pltpu.make_async_copy(snap_any, snap, sems.at[chunks])
-    copy.start()
-    for i, pack in enumerate((first, second)):
-        pack[: PARTS // 2] = pieces[2 * i][...]
-        pack[PARTS // 2 :] = pieces[2 * i + 1][...]
+
+    def chunk(i):
+        return pl.ds(pl.multiple_of(i * CHUNK, CHUNK), CHUNK)
+
+    def snap_copy(i):
+        return pltpu.make_async_copy(snap_any.at[chunk(i), :], snap.at[chunk(i), :], snap_sems.at[i])
+
+    def image_copy(i):
+        return pltpu.make_async_copy(image_any.at[chunk(i), :], image.at[chunk(i), :], image_sems.at[i])
+
+    def out_copy(i):
+        return pltpu.make_async_copy(snap.at[chunk(i), :], basis_any.at[chunk(i), :], basis_sems.at[i])
+
+    for i in range(chunks):
+        snap_copy(i).start()
+        image_copy(i).start()
+    first[: PARTS // 2] = first_low[...]
+    first[PARTS // 2 :] = first_high[...]
+    second[: PARTS // 2] = second_low[...]
+    second[PARTS // 2 :] = second_high[...]
     root, history, change, state = reduced_system(inverse_count, place_ref[0], first, second, index_ref[...])
     high, low = split(root)
     root_ref[:, :snaps] = high
@@ -353,17 +438,14 @@
         coeff_ref[n : n + 1, :] = history[n]
     change_ref[...] = change
     state_ref[...] = state
-    copy.wait()
     tile[...] = jnp.zeros_like(tile)
     lane = lax.broadcasted_iota(jnp.int32, (block, block), 1)
 
-    def out_copy(i):
-        at = pl.ds(pl.multiple_of(i * CHUNK, CHUNK), CHUNK)
-        return pltpu.make_async_copy(snap.at[at, :], basis_any.at[at, :], sems.at[i])
-
     @pl.loop(0, chunks)
     def _(i):
-        at = pl.ds(pl.multiple_of(i * CHUNK, CHUNK), CHUNK)
+        snap_copy(i).wait()
+        image_copy(i).wait()
+        at = chunk(i)
         panel = snap[at, :]
         sums = jnp.sum(panel * change_ref[...] + image[at, :] * state_ref[...], 1, keepdims=True)
         gathered = tile[...]
@@ -386,6 +468,7 @@
     rows, snaps = snapshots.shape
     block = force.shape[1]
     share = snaps // PARTS
+    chunks = rows // CHUNK
     vmem = pl.BlockSpec(memory_space=pltpu.VMEM)
     hbm = pl.BlockSpec(memory_space=pl.ANY)
     return pl.pallas_call(
@@ -395,9 +478,10 @@
             jax.ShapeDtypeStruct((STEPS, snaps), F32),
             jax.ShapeDtypeStruct(force.shape, F32),
         ),
-        in_specs=[pl.BlockSpec(memory_space=pltpu.SMEM)] + [vmem] * 7 + [hbm],
+        in_specs=[pl.BlockSpec(memory_space=pltpu.SMEM)] + [vmem] * 6 + [hbm, hbm],
         out_specs=[hbm, vmem, vmem],
         scratch_shapes=[
+            pltpu.VMEM((rows, snaps), F32),
             pltpu.VMEM((rows, snaps), F32),
             pltpu.VMEM((PARTS, share + 8, snaps), F32),
             pltpu.VMEM((PARTS, share, snaps), F32),
@@ -405,11 +489,13 @@
             pltpu.VMEM((1, snaps), F32),
             pltpu.VMEM((1, snaps), F32),
             pltpu.VMEM((block, block), F32),
-            pltpu.SemaphoreType.DMA((rows // CHUNK + 1,)),
+            pltpu.SemaphoreType.DMA((chunks,)),
+            pltpu.SemaphoreType.DMA((chunks,)),
+            pltpu.SemaphoreType.DMA((chunks,)),
         ],
         compiler_params=pltpu.CompilerParams(vmem_limit_bytes=LIMIT),
         name="final",
-    )(place, *pieces, step_index, force, image, snapshots)
+    )(place, *pieces, step_index, force, snapshots, image)
 
 
 def shifted(value, axis, steps):
@@ -464,8 +550,7 @@
     rows_prev = shifted(tail, "rows", 1)
     rows_next = shifted(head, "rows", -1)
     field, turned, gram, load = gram_call(snapshots, force)
-    head, tail, load = lax.optimization_barrier((head, tail, load))
-    halos = (rows_prev, rows_next, from_behind(tail, "zone", 1), from_behind(head, "zone", -1))
+    halos = (from_behind(tail, "zone", 1), from_behind(head, "zone", -1), rows_prev, rows_next)
     image, *packed = tangent_call(field, turned, halos, tangent, pattern, force, gram, load, place)
     pieces = reduce_packed(*packed)
     basis, coefficients, residual = final_call(

time: 117 us -> 115 us (0.983)
  local copies, waits for them, and re-layouts: 20.1 us -> 4.62 us
  Pallas kernels: 44.6 us -> 59.4 us
  waiting for transfers between devices: 24.1 us -> 20.7 us
  other arithmetic: 0.14 us -> 1.96 us
    unnamed x23 -> x17, local copies, waits for them, and re-layouts: 17.9 us -> 3.32 us
    pallas_call x1, Pallas kernels: 6.74 us -> 13.1 us  [gram_call(): pl.pallas_call(gram_kernel, out_shape=(jax.ShapeDtypeStruct((rows, 2 * sn...]
    pallas_call x1, Pallas kernels: 17.1 us -> 23.2 us  [tangent_call(): pl.pallas_call(tangent_kernel, out_shape=(jax.ShapeDtypeStruct((rows, sna...]
    ppermute x2, waiting for transfers between devices: 3.91 us -> 0.01 us  [from_behind(): return lax.ppermute(shard, axis, pairs)]
    pallas_call x1, Pallas kernels: 20.8 us -> 23.1 us  [final_call(): pl.pallas_call(functools.partial(final_kernel, inverse_count), out_shape=...]
    ppermute x14, starting transfers between devices: 18.1 us -> 16.1 us  [partner(): return lax.ppermute(value, axis, [(i, i ^ bit) for i in range(count)])]
    ppermute x2, starting transfers between devices: 2.76 us -> 4.34 us  [from_behind(): return lax.ppermute(shard, axis, pairs)]
    ppermute x2, waiting for transfers between devices: 0.01 us -> 1.35 us  [shifted(): return lax.ppermute(value, axis, pairs)]
  transfers between devices with their start and end apart: 18 -> 18, of which waited for: 14 -> 12; matrix products, arithmetic and copies ran while one was open for 0% -> 3% of each run, Pallas kernels for 6% -> 11%
where the time goes in v5:
time: 115 us; the launch traced here: 114 us
  Pallas kernels  59.4 us (52%)
  starting transfers between devices  26.6 us (23%)
  waiting for transfers between devices  20.7 us (18%)
  local copies, waits for them, and re-layouts  4.62 us (4%)
  other arithmetic  1.96 us (2%)
    pallas_call x1, Pallas kernels, tangent_call(): pl.pallas_call(tangent_kernel, out_shape=(jax.ShapeDtypeStruct((rows, sna...  23.2 us
    pallas_call x1, Pallas kernels, final_call(): pl.pallas_call(functools.partial(final_kernel, inverse_count), out_shape=...  23.1 us
    ppermute x14, waiting for transfers between devices, partner(): return lax.ppermute(value, axis, [(i, i ^ bit) for i in range(count)])  19.3 us
    ppermute x14, starting transfers between devices, partner(): return lax.ppermute(value, axis, [(i, i ^ bit) for i in range(count)])  16.1 us
    pallas_call x1, Pallas kernels, gram_call(): pl.pallas_call(gram_kernel, out_shape=(jax.ShapeDtypeStruct((rows, 2 * sn...  13.1 us
    ppermute x2, starting transfers between devices, shifted(): return lax.ppermute(value, axis, pairs)  6.12 us
    ppermute x2, starting transfers between devices, from_behind(): return lax.ppermute(shard, axis, pairs)  4.34 us
    unnamed x17, local copies, waits for them, and re-layouts  3.32 us
  transfers between devices with their start and end apart: 18, of which 12 were waited for; matrix products, arithmetic and copies ran while one was open for 3% of the time, Pallas kernels for 11%

profile of v5, /device:TPU:0, one launch (start us, length us, event | category | flops | bytes accessed | tf_op | source)
XLA Modules:
  0.0 114.3 jit_solution(14365638064066868646)
XLA Ops:
  0.6 1.3 %fusion.1 = (f32[512,256]{1,0:T(8,128)S(1)}, f32[512,256]{1,0:T(8,128)S(1)}) fusion(f32[8192,256]{1,0:T(8,128)} %snap_any.1), kind=kLoop, calls=%fused_computation.10 | loop fusion | bytes 2097152 | tf_op jit(solution)/shard_map/slice | solution.py:549
  1.9 6.1 %collective-permute-start.3 = (f32[512,256]{1,0:T(8,128)S(1)}, f32[512,256]{1,0:T(8,128)S(1)}, u32[]{:S(2)}, u32[]{:S(2)}) collective-permute-start(f32[512,256]{1,0:T(8,128)S(1)} %get-tuple-element.27), channel_id=1, source_target_pairs={{0,28},{4,0},{8,4},{12,8},{16,12},{20,16},{24,20},{28,24},{1,29},{... | collective-permute-start | bytes 1572872 | tf_op jit(solution)/shard_map/ppermute | solution.py:504
  8.0 1.3 %collective-permute-start.1 = (f32[512,256]{1,0:T(8,128)S(1)}, f32[512,256]{1,0:T(8,128)S(1)}, u32[]{:S(2)}, u32[]{:S(2)}) collective-permute-start(f32[512,256]{1,0:T(8,128)S(1)} %get-tuple-element.27), channel_id=1, source_target_pairs={{1,0},{2,1},{3,2},{5,4},{6,5},{7,6},{9,8},{10,9},{11,10},{13,12},{... | collective-permute-start | bytes 1572872 | tf_op jit(solution)/shard_map/ppermute | solution.py:510
  9.3 3.1 %collective-permute-start = (f32[512,256]{1,0:T(8,128)S(1)}, f32[512,256]{1,0:T(8,128)S(1)}, u32[]{:S(2)}, u32[]{:S(2)}) collective-permute-start(f32[512,256]{1,0:T(8,128)S(1)} %get-tuple-element.28), channel_id=1, source_target_pairs={{0,1},{1,2},{2,3},{4,5},{5,6},{6,7},{8,9},{9,10},{10,11},{12,13},{... | collective-permute-start | bytes 1572872 | tf_op jit(solution)/shard_map/ppermute | solution.py:510
  12.4 1.4 %copy.8.pattern_ref = s32[64,4]{1,0:T(8,128)} copy(s32[64,4]{0,1:T(4,128)} %param.7) | data formatting | bytes 2048 | tf_op args[2]
  13.8 13.1 %gram.1 = (bf16[8192,512]{1,0:T(8,128)(2,1)}, bf16[512,8192]{1,0:T(8,128)(2,1)}, f32[256,512]{1,0:T(8,128)}, f32[1,256]{1,0:T(1,128)}) custom-call(f32[8192,256]{1,0:T(8,128)} %snap_any.1, f32[64,128]{1,0:T(8,128)} %bitcast.4), custom_call_target="tpu_custom_call" | custom-call | flops 2147483648 | bytes 25165824 | tf_op jit(solution)/shard_map/gram/pallas_call | solution.py:84
  26.8 1.2 %collective-permute-done.3.next_any = f32[512,256]{1,0:T(8,128)S(1)} collective-permute-done((f32[512,256]{1,0:T(8,128)S(1)}, f32[512,256]{1,0:T(8,128)S(1)}, u32[]{:S(2)}, u32[]{:S(2)}) %collective-permute-start.3) | collective-permute-done | bytes 524320 | tf_op jit(solution)/shard_map/ppermute | solution.py:504
  28.2 0.7 copy-done.1
  29.4 23.2 %tangent.1 = (f32[8192,256]{1,0:T(8,128)}, f32[4,40,256]{2,1,0:T(8,128)}, f32[4,40,256]{2,1,0:T(8,128)}, f32[4,32,256]{2,1,0:T(8,128)}, f32[4,32,256]{2,1,0:T(8,128)}) custom-call(s32[64,4]{1,0:T(8,128)} %copy.8.pattern_ref, s32[1]{0:T(128)} %bitcast.place_ref, bf16[8192,512]{1,0:T(8,128)(2,1)} %get-tuple-element.15.field_any, f32[512,256]{1,0:T(8,128)} %copy-done.4, ...), custom_call_target="tpu_custom_call" | custom-call | tf_op jit(solution)/shard_map/tangent/pallas_call | solution.py:256
  52.8 0.5 collective-permute-start.4
  53.3 1.0 collective-permute-done.7
  54.3 0.9 add.27
  55.2 2.3 %collective-permute-start.8 = (f32[2,32,256]{2,1,0:T(8,128)S(1)}, f32[2,32,256]{2,1,0:T(8,128)S(1)}, u32[]{:S(2)}, u32[]{:S(2)}) collective-permute-start(f32[2,32,256]{2,1,0:T(8,128)S(1)} %slice.53), channel_id=1, source_target_pairs={{0,4},{4,0},{8,12},{12,8},{16,20},{20,16},{24,28},{28,24},{1,5},{5... | collective-permute-start | bytes 196616 | tf_op jit(solution)/shard_map/ppermute | solution.py:515
  57.6 0.9 add.24
  58.5 1.6 %collective-permute-start.5 = (f32[2,40,256]{2,1,0:T(8,128)S(1)}, f32[2,40,256]{2,1,0:T(8,128)S(1)}, u32[]{:S(2)}, u32[]{:S(2)}) collective-permute-start(f32[2,40,256]{2,1,0:T(8,128)S(1)} %slice.49), channel_id=1, source_target_pairs={{0,2},{1,3},{2,0},{3,1},{4,6},{5,7},{6,4},{7,5},{8,10},{9,11},{10,... | collective-permute-start | bytes 245768 | tf_op jit(solution)/shard_map/ppermute | solution.py:515
  60.2 1.4 %collective-permute-start.9 = (f32[1,32,256]{2,1,0:T(8,128)S(1)}, f32[1,32,256]{2,1,0:T(8,128)S(1)}, u32[]{:S(2)}, u32[]{:S(2)}) collective-permute-start(f32[1,32,256]{2,1,0:T(8,128)S(1)} %slice.55), channel_id=1, source_target_pairs={{0,2},{1,3},{2,0},{3,1},{4,6},{5,7},{6,4},{7,5},{8,10},{9,11},{10,... | collective-permute-start | bytes 98312 | tf_op jit(solution)/shard_map/ppermute | solution.py:515
  61.6 1.8 %collective-permute-done.5 = f32[2,40,256]{2,1,0:T(8,128)S(1)} collective-permute-done((f32[2,40,256]{2,1,0:T(8,128)S(1)}, f32[2,40,256]{2,1,0:T(8,128)S(1)}, u32[]{:S(2)}, u32[]{:S(2)}) %collective-permute-start.5) | collective-permute-done | bytes 81952 | tf_op jit(solution)/shard_map/ppermute | solution.py:515
  63.6 0.6 collective-permute-done.9
  64.2 3.3 %collective-permute-done.6 = f32[1,40,256]{2,1,0:T(8,128)S(1)} collective-permute-done((f32[1,40,256]{2,1,0:T(8,128)S(1)}, f32[1,40,256]{2,1,0:T(8,128)S(1)}, u32[]{:S(2)}, u32[]{:S(2)}) %collective-permute-start.6) | collective-permute-done | bytes 40992 | tf_op jit(solution)/shard_map/ppermute | solution.py:515
  67.5 1.7 %collective-permute-start.10 = (f32[1,72,256]{2,1,0:T(8,128)S(1)}, f32[1,72,256]{2,1,0:T(8,128)S(1)}, u32[]{:S(2)}, u32[]{:S(2)}) collective-permute-start(f32[1,72,256]{2,1,0:T(8,128)S(1)} %pad_maximum_fusion.3), channel_id=1, source_target_pairs={{0,8},{4,12},{8,0},{12,4},{16,24},{20,28},{24,16},{28,20},{1,9},{5... | collective-permute-start | bytes 221192 | tf_op jit(solution)/shard_map/ppermute | solution.py:515
  69.2 2.8 %collective-permute-done.10 = f32[1,72,256]{2,1,0:T(8,128)S(1)} collective-permute-done((f32[1,72,256]{2,1,0:T(8,128)S(1)}, f32[1,72,256]{2,1,0:T(8,128)S(1)}, u32[]{:S(2)}, u32[]{:S(2)}) %collective-permute-start.10) | collective-permute-done | bytes 73760 | tf_op jit(solution)/shard_map/ppermute | solution.py:515
  71.9 4.6 %collective-permute-start.11 = (f32[1,72,256]{2,1,0:T(8,128)S(1)}, f32[1,72,256]{2,1,0:T(8,128)S(1)}, u32[]{:S(2)}, u32[]{:S(2)}) collective-permute-start(f32[1,72,256]{2,1,0:T(8,128)S(1)} %fusion), channel_id=1, source_target_pairs={{0,16},{4,20},{8,24},{12,28},{16,0},{20,4},{24,8},{28,12},{1,17},{... | collective-permute-start | bytes 221192 | tf_op jit(solution)/shard_map/ppermute | solution.py:515
  76.6 2.3 %collective-permute-done.11 = f32[1,72,256]{2,1,0:T(8,128)S(1)} collective-permute-done((f32[1,72,256]{2,1,0:T(8,128)S(1)}, f32[1,72,256]{2,1,0:T(8,128)S(1)}, u32[]{:S(2)}, u32[]{:S(2)}) %collective-permute-start.11) | collective-permute-done | bytes 73760 | tf_op jit(solution)/shard_map/ppermute | solution.py:515
  79.0 1.6 %collective-permute-start.15 = (f32[1,32,256]{2,1,0:T(8,128)S(1)}, f32[1,32,256]{2,1,0:T(8,128)S(1)}, u32[]{:S(2)}, u32[]{:S(2)}) collective-permute-start(f32[1,32,256]{2,1,0:T(8,128)S(1)} %slice.57), channel_id=1, source_target_pairs={{0,2},{1,3},{2,0},{3,1},{4,6},{5,7},{6,4},{7,5},{8,10},{9,11},{10,... | collective-permute-start | bytes 98312 | tf_op jit(solution)/shard_map/ppermute | solution.py:515
  80.6 2.4 %collective-permute-done.12 = f32[1,40,256]{2,1,0:T(8,128)S(1)} collective-permute-done((f32[1,40,256]{2,1,0:T(8,128)S(1)}, f32[1,40,256]{2,1,0:T(8,128)S(1)}, u32[]{:S(2)}, u32[]{:S(2)}) %collective-permute-start.12) | collective-permute-done | bytes 40992 | tf_op jit(solution)/shard_map/ppermute | solution.py:515
  83.0 1.5 %collective-permute-start.13 = (f32[2,40,256]{2,1,0:T(8,128)S(1)}, f32[2,40,256]{2,1,0:T(8,128)S(1)}, u32[]{:S(2)}, u32[]{:S(2)}) collective-permute-start(f32[2,40,256]{2,1,0:T(8,128)S(1)} %pad_maximum_fusion.2), channel_id=1, source_target_pairs={{0,2},{1,3},{2,0},{3,1},{4,6},{5,7},{6,4},{7,5},{8,10},{9,11},{10,... | collective-permute-start | bytes 245768 | tf_op jit(solution)/shard_map/ppermute | solution.py:515
  84.5 0.4 collective-permute-start.16
  84.9 2.5 %collective-permute-done.13 = f32[2,40,256]{2,1,0:T(8,128)S(1)} collective-permute-done((f32[2,40,256]{2,1,0:T(8,128)S(1)}, f32[2,40,256]{2,1,0:T(8,128)S(1)}, u32[]{:S(2)}, u32[]{:S(2)}) %collective-permute-start.13) | collective-permute-done | bytes 81952 | tf_op jit(solution)/shard_map/ppermute | solution.py:515
  87.5 1.3 %collective-permute-done.16 = f32[2,32,256]{2,1,0:T(8,128)S(1)} collective-permute-done((f32[2,32,256]{2,1,0:T(8,128)S(1)}, f32[2,32,256]{2,1,0:T(8,128)S(1)}, u32[]{:S(2)}, u32[]{:S(2)}) %collective-permute-start.16) | collective-permute-done | bytes 65568 | tf_op jit(solution)/shard_map/ppermute | solution.py:515
  88.9 1.3 %collective-permute-done.17.second_high = f32[4,32,256]{2,1,0:T(8,128)S(1)} collective-permute-done((f32[4,32,256]{2,1,0:T(8,128)S(1)}, f32[4,32,256]{2,1,0:T(8,128)S(1)}, u32[]{:S(2)}, u32[]{:S(2)}) %collective-permute-start.17) | collective-permute-done | bytes 131104 | tf_op jit(solution)/shard_map/ppermute | solution.py:515
  90.3 0.6 copy-done.7
  91.0 23.1 %final.1 = (f32[8192,256]{1,0:T(8,128)}, f32[3,256]{1,0:T(4,128)}, f32[64,128]{1,0:T(8,128)}) custom-call(s32[1]{0:T(128)} %bitcast.place_ref, f32[4,40,256]{2,1,0:T(8,128)} %copy-done, f32[4,40,256]{2,1,0:T(8,128)} %copy-done.6, f32[4,32,256]{2,1,0:T(8,128)} %copy-done.5, f32[4,32,256]{2,1,0:T(8,128)} %copy-done.7, s32[1,256]{1,0:T(1,128)} %bitcast.7, ...), custom_call_target="tpu_custom_call" | custom-call | tf_op jit(solution)/shard_map/final/pallas_call | solution.py:474
  (44 shorter events, 1.4 us)
Async XLA Ops:
  1.9 26.2 %collective-permute-start.3 = (f32[512,256]{1,0:T(8,128)S(1)}, f32[512,256]{1,0:T(8,128)S(1)}, u32[]{:S(2)}, u32[]{:S(2)}) collective-permute-start(f32[512,256]{1,0:T(8,128)S(1)} %get-tuple-element.27), channel_id=1, source_target_pairs={{0,28},{4,0},{8,4},{12,8},{16,12},{20,16},{24,20},{28,24},{1,29},{... | collective-permute-start | bytes 1572872 | tf_op jit(solution)/shard_map/ppermute | solution.py:504
  8.0 20.1 %collective-permute-start.1 = (f32[512,256]{1,0:T(8,128)S(1)}, f32[512,256]{1,0:T(8,128)S(1)}, u32[]{:S(2)}, u32[]{:S(2)}) collective-permute-start(f32[512,256]{1,0:T(8,128)S(1)} %get-tuple-element.27), channel_id=1, source_target_pairs={{1,0},{2,1},{3,2},{5,4},{6,5},{7,6},{9,8},{10,9},{11,10},{13,12},{... | collective-permute-start | bytes 1572872 | tf_op jit(solution)/shard_map/ppermute | solution.py:510
  9.2 19.0 %collective-permute-start.2 = (f32[512,256]{1,0:T(8,128)S(1)}, f32[512,256]{1,0:T(8,128)S(1)}, u32[]{:S(2)}, u32[]{:S(2)}) collective-permute-start(f32[512,256]{1,0:T(8,128)S(1)} %get-tuple-element.28), channel_id=1, source_target_pairs={{0,4},{4,8},{8,12},{12,16},{16,20},{20,24},{24,28},{28,0},{1,5},{5... | collective-permute-start | bytes 1572872 | tf_op jit(solution)/shard_map/ppermute | solution.py:504
  9.3 18.9 %collective-permute-start = (f32[512,256]{1,0:T(8,128)S(1)}, f32[512,256]{1,0:T(8,128)S(1)}, u32[]{:S(2)}, u32[]{:S(2)}) collective-permute-start(f32[512,256]{1,0:T(8,128)S(1)} %get-tuple-element.28), channel_id=1, source_target_pairs={{0,1},{1,2},{2,3},{4,5},{5,6},{6,7},{8,9},{9,10},{10,11},{12,13},{... | collective-permute-start | bytes 1572872 | tf_op jit(solution)/shard_map/ppermute | solution.py:510
  28.1 0.8 copy-start.1
  28.1 1.0 copy-start.2
  28.2 1.0 copy-start.3
  28.2 1.2 %copy-start.4 = (f32[512,256]{1,0:T(8,128)}, f32[512,256]{1,0:T(8,128)S(1)}, u32[]{:S(2)}) copy-start(f32[512,256]{1,0:T(8,128)S(1)} %collective-permute-done.left_any) | copy-start | bytes 1572868
  52.7 1.6 %collective-permute-start.7 = (f32[4,32,256]{2,1,0:T(8,128)}, f32[4,32,256]{2,1,0:T(8,128)S(1)}, u32[]{:S(2)}, u32[]{:S(2)}) collective-permute-start(f32[4,32,256]{2,1,0:T(8,128)} %get-tuple-element.22), channel_id=1, source_target_pairs={{0,1},{1,0},{2,3},{3,2},{4,5},{5,4},{6,7},{7,6},{8,9},{9,8},{10,11... | collective-permute-start | bytes 393224 | tf_op jit(solution)/shard_map/ppermute | solution.py:515
  52.8 4.8 %collective-permute-start.4 = (f32[4,40,256]{2,1,0:T(8,128)}, f32[4,40,256]{2,1,0:T(8,128)S(1)}, u32[]{:S(2)}, u32[]{:S(2)}) collective-permute-start(f32[4,40,256]{2,1,0:T(8,128)} %get-tuple-element.20), channel_id=1, source_target_pairs={{0,1},{1,0},{2,3},{3,2},{4,5},{5,4},{6,7},{7,6},{8,9},{9,8},{10,11... | collective-permute-start | bytes 491528 | tf_op jit(solution)/shard_map/ppermute | solution.py:515
  55.2 4.9 %collective-permute-start.8 = (f32[2,32,256]{2,1,0:T(8,128)S(1)}, f32[2,32,256]{2,1,0:T(8,128)S(1)}, u32[]{:S(2)}, u32[]{:S(2)}) collective-permute-start(f32[2,32,256]{2,1,0:T(8,128)S(1)} %slice.53), channel_id=1, source_target_pairs={{0,4},{4,0},{8,12},{12,8},{16,20},{20,16},{24,28},{28,24},{1,5},{5... | collective-permute-start | bytes 196616 | tf_op jit(solution)/shard_map/ppermute | solution.py:515
  58.5 4.9 %collective-permute-start.5 = (f32[2,40,256]{2,1,0:T(8,128)S(1)}, f32[2,40,256]{2,1,0:T(8,128)S(1)}, u32[]{:S(2)}, u32[]{:S(2)}) collective-permute-start(f32[2,40,256]{2,1,0:T(8,128)S(1)} %slice.49), channel_id=1, source_target_pairs={{0,2},{1,3},{2,0},{3,1},{4,6},{5,7},{6,4},{7,5},{8,10},{9,11},{10,... | collective-permute-start | bytes 245768 | tf_op jit(solution)/shard_map/ppermute | solution.py:515
  60.2 4.0 %collective-permute-start.9 = (f32[1,32,256]{2,1,0:T(8,128)S(1)}, f32[1,32,256]{2,1,0:T(8,128)S(1)}, u32[]{:S(2)}, u32[]{:S(2)}) collective-permute-start(f32[1,32,256]{2,1,0:T(8,128)S(1)} %slice.55), channel_id=1, source_target_pairs={{0,2},{1,3},{2,0},{3,1},{4,6},{5,7},{6,4},{7,5},{8,10},{9,11},{10,... | collective-permute-start | bytes 98312 | tf_op jit(solution)/shard_map/ppermute | solution.py:515
  63.4 4.1 %collective-permute-start.6 = (f32[1,40,256]{2,1,0:T(8,128)S(1)}, f32[1,40,256]{2,1,0:T(8,128)S(1)}, u32[]{:S(2)}, u32[]{:S(2)}) collective-permute-start(f32[1,40,256]{2,1,0:T(8,128)S(1)} %slice.51), channel_id=1, source_target_pairs={{0,4},{4,0},{8,12},{12,8},{16,20},{20,16},{24,28},{28,24},{1,5},{5... | collective-permute-start | bytes 122888 | tf_op jit(solution)/shard_map/ppermute | solution.py:515
  67.5 4.4 %collective-permute-start.10 = (f32[1,72,256]{2,1,0:T(8,128)S(1)}, f32[1,72,256]{2,1,0:T(8,128)S(1)}, u32[]{:S(2)}, u32[]{:S(2)}) collective-permute-start(f32[1,72,256]{2,1,0:T(8,128)S(1)} %pad_maximum_fusion.3), channel_id=1, source_target_pairs={{0,8},{4,12},{8,0},{12,4},{16,24},{20,28},{24,16},{28,20},{1,9},{5... | collective-permute-start | bytes 221192 | tf_op jit(solution)/shard_map/ppermute | solution.py:515
  71.9 7.0 %collective-permute-start.11 = (f32[1,72,256]{2,1,0:T(8,128)S(1)}, f32[1,72,256]{2,1,0:T(8,128)S(1)}, u32[]{:S(2)}, u32[]{:S(2)}) collective-permute-start(f32[1,72,256]{2,1,0:T(8,128)S(1)} %fusion), channel_id=1, source_target_pairs={{0,16},{4,20},{8,24},{12,28},{16,0},{20,4},{24,8},{28,12},{1,17},{... | collective-permute-start | bytes 221192 | tf_op jit(solution)/shard_map/ppermute | solution.py:515
  78.9 4.1 %collective-permute-start.12 = (f32[1,40,256]{2,1,0:T(8,128)S(1)}, f32[1,40,256]{2,1,0:T(8,128)S(1)}, u32[]{:S(2)}, u32[]{:S(2)}) collective-permute-start(f32[1,40,256]{2,1,0:T(8,128)S(1)} %slice.56), channel_id=1, source_target_pairs={{0,4},{4,0},{8,12},{12,8},{16,20},{20,16},{24,28},{28,24},{1,5},{5... | collective-permute-start | bytes 122888 | tf_op jit(solution)/shard_map/ppermute | solution.py:515
  79.0 5.5 %collective-permute-start.15 = (f32[1,32,256]{2,1,0:T(8,128)S(1)}, f32[1,32,256]{2,1,0:T(8,128)S(1)}, u32[]{:S(2)}, u32[]{:S(2)}) collective-permute-start(f32[1,32,256]{2,1,0:T(8,128)S(1)} %slice.57), channel_id=1, source_target_pairs={{0,2},{1,3},{2,0},{3,1},{4,6},{5,7},{6,4},{7,5},{8,10},{9,11},{10,... | collective-permute-start | bytes 98312 | tf_op jit(solution)/shard_map/ppermute | solution.py:515
  83.0 4.4 %collective-permute-start.13 = (f32[2,40,256]{2,1,0:T(8,128)S(1)}, f32[2,40,256]{2,1,0:T(8,128)S(1)}, u32[]{:S(2)}, u32[]{:S(2)}) collective-permute-start(f32[2,40,256]{2,1,0:T(8,128)S(1)} %pad_maximum_fusion.2), channel_id=1, source_target_pairs={{0,2},{1,3},{2,0},{3,1},{4,6},{5,7},{6,4},{7,5},{8,10},{9,11},{10,... | collective-permute-start | bytes 245768 | tf_op jit(solution)/shard_map/ppermute | solution.py:515
  84.5 4.3 %collective-permute-start.16 = (f32[2,32,256]{2,1,0:T(8,128)S(1)}, f32[2,32,256]{2,1,0:T(8,128)S(1)}, u32[]{:S(2)}, u32[]{:S(2)}) collective-permute-start(f32[2,32,256]{2,1,0:T(8,128)S(1)} %pad_maximum_fusion.4), channel_id=1, source_target_pairs={{0,4},{4,0},{8,12},{12,8},{16,20},{20,16},{24,28},{28,24},{1,5},{5... | collective-permute-start | bytes 196616 | tf_op jit(solution)/shard_map/ppermute | solution.py:515
  87.5 2.8 %copy-start = (f32[4,40,256]{2,1,0:T(8,128)}, f32[4,40,256]{2,1,0:T(8,128)S(1)}, u32[]{:S(2)}) copy-start(f32[4,40,256]{2,1,0:T(8,128)S(1)} %pad_maximum_fusion.first_low) | copy-start | bytes 491524
  87.5 2.8 %collective-permute-start.14 = (f32[4,40,256]{2,1,0:T(8,128)S(1)}, f32[4,40,256]{2,1,0:T(8,128)S(1)}, u32[]{:S(2)}, u32[]{:S(2)}) collective-permute-start(f32[4,40,256]{2,1,0:T(8,128)S(1)} %pad_maximum_fusion.first_low), channel_id=1, source_target_pairs={{0,1},{1,0},{2,3},{3,2},{4,5},{5,4},{6,7},{7,6},{8,9},{9,8},{10,11... | collective-permute-start | bytes 491528 | tf_op jit(solution)/shard_map/ppermute | solution.py:515
  88.9 1.4 %copy-start.5 = (f32[4,32,256]{2,1,0:T(8,128)}, f32[4,32,256]{2,1,0:T(8,128)S(1)}, u32[]{:S(2)}) copy-start(f32[4,32,256]{2,1,0:T(8,128)S(1)} %pad_maximum_fusion.1.second_low) | copy-start | bytes 393220
  88.9 1.4 %collective-permute-start.17 = (f32[4,32,256]{2,1,0:T(8,128)S(1)}, f32[4,32,256]{2,1,0:T(8,128)S(1)}, u32[]{:S(2)}, u32[]{:S(2)}) collective-permute-start(f32[4,32,256]{2,1,0:T(8,128)S(1)} %pad_maximum_fusion.1.second_low), channel_id=1, source_target_pairs={{0,1},{1,0},{2,3},{3,2},{4,5},{5,4},{6,7},{7,6},{8,9},{9,8},{10,11... | collective-permute-start | bytes 393224 | tf_op jit(solution)/shard_map/ppermute | solution.py:515
  90.3 0.6 copy-start.7
  90.3 0.7 copy-start.6

commit v6 on v5

--- a/solution.py
+++ b/solution.py
@@ -11,7 +11,7 @@
 STEPS = 3
 STEP_SIZE = 0.25
 CHUNK = 1024
-LIMIT = 56 * 1024 * 1024
+MIB = 1024 * 1024
 PARTS = 8
 F32 = jnp.float32
 BF16 = jnp.bfloat16
@@ -55,54 +55,35 @@
     return total
 
 
-def gram_kernel(snap_ref, force_ref, field_ref, turned_ref, gram_ref, load_ref):
-    panel = snap_ref[...]
-    snaps = panel.shape[1]
-    high, low = split(panel)
-    turned = high.T
-    field_ref[:, :snaps] = high
-    field_ref[:, snaps:] = low
-    turned_ref[:snaps, :] = turned
-    turned_ref[snaps:, :] = low.T
-    gram = matmul(turned, jnp.concatenate([high, low], 1))
-    load = force_product(panel, force_ref[...])
-
-    @pl.when(pl.program_id(0) == 0)
-    def _():
-        gram_ref[...] = gram
-        load_ref[...] = load
-
-    @pl.when(pl.program_id(0) > 0)
-    def _():
-        gram_ref[...] += gram
-        load_ref[...] += load
+def gram_kernel(snap_ref, force_ref, gram_ref, load_ref):
+    rows = snap_ref.shape[0]
+    per_chunk = CHUNK // force_ref.shape[1]
+    gram_ref[...] = jnp.zeros_like(gram_ref)
+    load_ref[...] = jnp.zeros_like(load_ref)
+
+    @pl.loop(0, rows // CHUNK)
+    def _(i):
+        panel = snap_ref[pl.ds(pl.multiple_of(i * CHUNK, CHUNK), CHUNK), :]
+        high, low = split(panel)
+        gram_ref[...] += matmul(high.T, jnp.concatenate([high, low], 1))
+        line = pl.ds(pl.multiple_of(i * per_chunk, per_chunk), per_chunk)
+        load_ref[...] += force_product(panel, force_ref[line, :])
 
 
 def gram_call(snapshots, force):
     rows, snaps = snapshots.shape
-    block = force.shape[1]
+    vmem = pl.BlockSpec(memory_space=pltpu.VMEM)
     return pl.pallas_call(
         gram_kernel,
         out_shape=(
-            jax.ShapeDtypeStruct((rows, 2 * snaps), BF16),
-            jax.ShapeDtypeStruct((2 * snaps, rows), BF16),
             jax.ShapeDtypeStruct((snaps, 2 * snaps), F32),
             jax.ShapeDtypeStruct((1, snaps), F32),
         ),
-        grid=(rows // CHUNK,),
-        in_specs=[
-            pl.BlockSpec((CHUNK, snaps), lambda i: (i, 0)),
-            pl.BlockSpec((CHUNK // block, block), lambda i: (i, 0)),
-        ],
-        out_specs=[
-            pl.BlockSpec((CHUNK, 2 * snaps), lambda i: (i, 0)),
-            pl.BlockSpec((2 * snaps, CHUNK), lambda i: (0, i)),
-            pl.BlockSpec((snaps, 2 * snaps), lambda i: (0, 0)),
-            pl.BlockSpec((1, snaps), lambda i: (0, 0)),
-        ],
-        compiler_params=pltpu.CompilerParams(vmem_limit_bytes=LIMIT),
+        in_specs=[vmem, vmem],
+        out_specs=[vmem, vmem],
+        compiler_params=pltpu.CompilerParams(vmem_limit_bytes=10 * MIB),
         cost_estimate=pl.CostEstimate(
-            flops=4 * rows * snaps * snaps, bytes_accessed=12 * rows * snaps, transcendentals=0
+            flops=4 * rows * snaps * snaps, bytes_accessed=4 * rows * snaps, transcendentals=0
         ),
         name="gram",
     )(snapshots, force)
@@ -111,35 +92,27 @@
 def tangent_kernel(
     pattern_ref,
     place_ref,
-    field_any,
-    left_any,
-    right_any,
-    prev_any,
-    next_any,
-    turned_any,
+    snap,
+    left_ref,
+    right_ref,
+    prev_ref,
+    next_ref,
     tangent_any,
     force_ref,
     gram_ref,
     load_ref,
-    image_any,
+    image,
     keep_first,
     send_first,
     keep_second,
     send_second,
     field,
-    edges,
-    turned,
-    tangent,
-    image,
     mixed,
     rest,
     load,
     packed,
-    field_sems,
-    edge_sems,
-    turned_sems,
-    tangent_sems,
-    image_sems,
+    tangent,
+    sems,
 ):
     rows, snaps = image.shape
     block_count, coupled = pattern_ref.shape
@@ -148,47 +121,35 @@
     chunks = rows // CHUNK
     per_chunk = CHUNK // block
 
-    def chunk(i):
-        return pl.ds(pl.multiple_of(i * CHUNK, CHUNK), CHUNK)
-
-    def field_copy(i):
-        return pltpu.make_async_copy(field_any.at[chunk(i), :], field.at[chunk(i), :], field_sems.at[i])
-
-    def turned_copy(i):
-        return pltpu.make_async_copy(turned_any.at[:, chunk(i)], turned.at[i], turned_sems.at[i])
-
     def tangent_copy(i):
-        return pltpu.make_async_copy(tangent_any.at[chunk(i), :], tangent.at[chunk(i), :], tangent_sems.at[i])
-
-    def image_copy(i):
-        return pltpu.make_async_copy(image.at[chunk(i), :], image_any.at[chunk(i), :], image_sems.at[i])
-
-    edge_copies = []
-    for i, ref in enumerate((left_any, right_any, prev_any, next_any)):
-        edge_copies.append(pltpu.make_async_copy(ref, edges.at[pl.ds(i * edge, edge), :], edge_sems.at[i]))
-        edge_copies[-1].start()
-    for i in range(chunks):
-        field_copy(i).start()
+        at = pl.ds(pl.multiple_of(i * CHUNK, CHUNK), CHUNK)
+        return pltpu.make_async_copy(tangent_any.at[at, :], tangent.at[at, :], sems.at[i])
+
     for i in range(chunks):
         tangent_copy(i).start()
-        turned_copy(i).start()
-    for i in range(4):
-        edge_copies[i].wait()
-        high, low = split(edges[i * edge : (i + 1) * edge, :])
-        at = pl.ds(rows + i * edge, edge)
+
+    def enter(at, value):
+        high, low = split(value)
         field[at, :snaps] = high
         field[at, snaps:] = low
+
+    @pl.loop(0, chunks)
+    def _(i):
+        at = pl.ds(pl.multiple_of(i * CHUNK, CHUNK), CHUNK)
+        enter(at, snap[at, :])
+
+    for i, ref in enumerate((left_ref, right_ref, prev_ref, next_ref)):
+        enter(pl.ds(rows + i * edge, edge), ref[...])
     mixed[...] = jnp.zeros_like(mixed)
     rest[...] = jnp.zeros_like(rest)
     load[...] = load_ref[...]
-    for i in range(chunks):
-        field_copy(i).wait()
 
     @pl.loop(0, chunks)
     def _(step):
         start = pl.multiple_of(step * CHUNK, CHUNK)
+        here = field[pl.ds(start, CHUNK), :]
+        panels = [here[:, :snaps].T, here[:, snaps:].T]
         tangent_copy(step).wait()
-        turned_copy(step).wait()
         images = []
         for k in range(per_chunk):
             g = step * per_chunk + k
@@ -206,15 +167,13 @@
             part = STEP_SIZE * (both[:, :snaps] + both[:, snaps:])
             image[own, :] = part
             images.append(part)
-        image_copy(step).start()
         panel = jnp.concatenate(images, 0)
         line = pl.ds(pl.multiple_of(step * per_chunk, per_chunk), per_chunk)
         load[...] += force_product(panel, force_ref[line, :])
         high, low = split(panel)
         high_turned = high.T
-        panels = turned[step]
-        mixed[...] += matmul(jnp.concatenate([panels, high_turned], 0), high)
-        rest[...] += matmul(jnp.concatenate([panels[:snaps], high_turned], 0), low)
+        mixed[...] += matmul(jnp.concatenate([*panels, high_turned], 0), high)
+        rest[...] += matmul(jnp.concatenate([panels[0], high_turned], 0), low)
 
     gram = gram_ref[:, :snaps] + gram_ref[:, snaps:] + gram_ref[:, snaps:].T
     cross = mixed[:snaps] + mixed[snaps : 2 * snaps] + rest[:snaps]
@@ -237,46 +196,32 @@
         begin = pl.multiple_of((place_ref[0] ^ second_piece(at)) * share, 8)
         second[slot] = packed[1, pl.ds(begin, share), :]
 
-    @pl.loop(0, chunks)
-    def _(step):
-        image_copy(step).wait()
-
-
-def tangent_call(field, turned, halos, tangent, pattern, force, gram, load, place):
-    rows, width = tangent.shape
-    snaps = gram.shape[0]
+
+def tangent_call(snapshots, halos, tangent, pattern, force, gram, load, place):
+    rows, snaps = snapshots.shape
     share = snaps // PARTS
-    chunks = rows // CHUNK
     edge = halos[0].shape[0]
     vmem = pl.BlockSpec(memory_space=pltpu.VMEM)
     smem = pl.BlockSpec(memory_space=pltpu.SMEM)
-    hbm = pl.BlockSpec(memory_space=pl.ANY)
     first = jax.ShapeDtypeStruct((PARTS // 2, share + 8, snaps), F32)
     second = jax.ShapeDtypeStruct((PARTS // 2, share, snaps), F32)
     return pl.pallas_call(
         tangent_kernel,
         out_shape=(jax.ShapeDtypeStruct((rows, snaps), F32), first, first, second, second),
-        in_specs=[smem, smem] + [hbm] * 7 + [vmem] * 3,
-        out_specs=[hbm] + [vmem] * 4,
+        in_specs=[smem, smem] + [vmem] * 5 + [pl.BlockSpec(memory_space=pl.ANY)] + [vmem] * 3,
+        out_specs=[vmem] * 5,
         scratch_shapes=[
             pltpu.VMEM((rows + 4 * edge, 2 * snaps), BF16),
-            pltpu.VMEM((4 * edge, snaps), F32),
-            pltpu.VMEM((chunks, 2 * snaps, CHUNK), BF16),
-            pltpu.VMEM((rows, width), BF16),
-            pltpu.VMEM((rows, snaps), F32),
             pltpu.VMEM((3 * snaps, snaps), F32),
             pltpu.VMEM((2 * snaps, snaps), F32),
             pltpu.VMEM((1, snaps), F32),
             pltpu.VMEM((2, snaps, snaps), F32),
-            pltpu.SemaphoreType.DMA((chunks,)),
-            pltpu.SemaphoreType.DMA((4,)),
-            pltpu.SemaphoreType.DMA((chunks,)),
-            pltpu.SemaphoreType.DMA((chunks,)),
-            pltpu.SemaphoreType.DMA((chunks,)),
+            pltpu.VMEM(tangent.shape, BF16),
+            pltpu.SemaphoreType.DMA((rows // CHUNK,)),
         ],
-        compiler_params=pltpu.CompilerParams(vmem_limit_bytes=LIMIT),
+        compiler_params=pltpu.CompilerParams(vmem_limit_bytes=40 * MIB),
         name="tangent",
-    )(pattern, place, field, *halos, turned, tangent, force, gram, load)
+    )(pattern, place, snapshots, *halos, tangent, force, gram, load)
 
 
 def inverse_factors(blocks):
@@ -389,22 +334,19 @@
     second_high,
     index_ref,
     force_ref,
-    snap_any,
-    image_any,
+    snap,
+    image,
     basis_any,
     coeff_ref,
     residual_ref,
-    snap,
-    image,
     first,
     second,
     root_ref,
     change_ref,
     state_ref,
     tile,
-    snap_sems,
-    image_sems,
-    basis_sems,
+    basis,
+    sems,
 ):
     rows, snaps = snap.shape
     block = force_ref.shape[1]
@@ -414,18 +356,9 @@
     def chunk(i):
         return pl.ds(pl.multiple_of(i * CHUNK, CHUNK), CHUNK)
 
-    def snap_copy(i):
-        return pltpu.make_async_copy(snap_any.at[chunk(i), :], snap.at[chunk(i), :], snap_sems.at[i])
-
-    def image_copy(i):
-        return pltpu.make_async_copy(image_any.at[chunk(i), :], image.at[chunk(i), :], image_sems.at[i])
-
     def out_copy(i):
-        return pltpu.make_async_copy(snap.at[chunk(i), :], basis_any.at[chunk(i), :], basis_sems.at[i])
-
-    for i in range(chunks):
-        snap_copy(i).start()
-        image_copy(i).start()
+        return pltpu.make_async_copy(basis.at[i % 2], basis_any.at[chunk(i), :], sems.at[i % 2])
+
     first[: PARTS // 2] = first_low[...]
     first[PARTS // 2 :] = first_high[...]
     second[: PARTS // 2] = second_low[...]
@@ -443,8 +376,6 @@
 
     @pl.loop(0, chunks)
     def _(i):
-        snap_copy(i).wait()
-        image_copy(i).wait()
         at = chunk(i)
         panel = snap[at, :]
         sums = jnp.sum(panel * change_ref[...] + image[at, :] * state_ref[...], 1, keepdims=True)
@@ -454,13 +385,17 @@
         tile[...] = gathered
         panel_high, panel_low = split(panel)
         both = matmul(panel_high, root_ref[...])
-        snap[at, :] = both[:, :snaps] + both[:, snaps:] + matmul(panel_low, root_ref[:, :snaps])
+
+        @pl.when(i >= 2)
+        def _():
+            out_copy(i - 2).wait()
+
+        basis[i % 2] = both[:, :snaps] + both[:, snaps:] + matmul(panel_low, root_ref[:, :snaps])
         out_copy(i).start()
 
     residual_ref[...] = tile[...].T[: rows // block] - STEP_SIZE * force_ref[...]
 
-    @pl.loop(0, chunks)
-    def _(i):
+    for i in range(chunks - 2, chunks):
         out_copy(i).wait()
 
 
@@ -468,7 +403,6 @@
     rows, snaps = snapshots.shape
     block = force.shape[1]
     share = snaps // PARTS
-    chunks = rows // CHUNK
     vmem = pl.BlockSpec(memory_space=pltpu.VMEM)
     hbm = pl.BlockSpec(memory_space=pl.ANY)
     return pl.pallas_call(
@@ -478,22 +412,19 @@
             jax.ShapeDtypeStruct((STEPS, snaps), F32),
             jax.ShapeDtypeStruct(force.shape, F32),
         ),
-        in_specs=[pl.BlockSpec(memory_space=pltpu.SMEM)] + [vmem] * 6 + [hbm, hbm],
+        in_specs=[pl.BlockSpec(memory_space=pltpu.SMEM)] + [vmem] * 8,
         out_specs=[hbm, vmem, vmem],
         scratch_shapes=[
-            pltpu.VMEM((rows, snaps), F32),
-            pltpu.VMEM((rows, snaps), F32),
             pltpu.VMEM((PARTS, share + 8, snaps), F32),
             pltpu.VMEM((PARTS, share, snaps), F32),
             pltpu.VMEM((snaps, 2 * snaps), BF16),
             pltpu.VMEM((1, snaps), F32),
             pltpu.VMEM((1, snaps), F32),
             pltpu.VMEM((block, block), F32),
-            pltpu.SemaphoreType.DMA((chunks,)),
-            pltpu.SemaphoreType.DMA((chunks,)),
-            pltpu.SemaphoreType.DMA((chunks,)),
+            pltpu.VMEM((2, CHUNK, snaps), F32),
+            pltpu.SemaphoreType.DMA((2,)),
         ],
-        compiler_params=pltpu.CompilerParams(vmem_limit_bytes=LIMIT),
+        compiler_params=pltpu.CompilerParams(vmem_limit_bytes=12 * MIB),
         name="final",
     )(place, *pieces, step_index, force, snapshots, image)
 
@@ -549,9 +480,9 @@
     head, tail = snapshots[:edge], snapshots[rows - edge :]
     rows_prev = shifted(tail, "rows", 1)
     rows_next = shifted(head, "rows", -1)
-    field, turned, gram, load = gram_call(snapshots, force)
+    gram, load = gram_call(snapshots, force)
     halos = (from_behind(tail, "zone", 1), from_behind(head, "zone", -1), rows_prev, rows_next)
-    image, *packed = tangent_call(field, turned, halos, tangent, pattern, force, gram, load, place)
+    image, *packed = tangent_call(snapshots, halos, tangent, pattern, force, gram, load, place)
     pieces = reduce_packed(*packed)
     basis, coefficients, residual = final_call(
         pieces, step_index.reshape(1, snaps), place, snapshots, image, force, inverse_count

time: 115 us -> 107 us (0.930)
  Pallas kernels: 59.4 us -> 47.4 us
  waiting for transfers between devices: 20.7 us -> 23.8 us
  other arithmetic: 1.96 us -> 0.14 us
  local copies, waits for them, and re-layouts: 4.62 us -> 6.24 us
  starting transfers between devices: 26.6 us -> 28 us
    pallas_call x1, Pallas kernels: 13.1 us -> 4.5 us  [gram_call(): pl.pallas_call(gram_kernel, out_shape=(jax.ShapeDtypeStruct((snaps, 2 * s...]
    ppermute x2, waiting for transfers between devices: 1.35 us -> 6.39 us  [shifted(): return lax.ppermute(value, axis, pairs)]
    pallas_call x1, Pallas kernels: 23.2 us -> 20.4 us  [tangent_call(): pl.pallas_call(tangent_kernel, out_shape=(jax.ShapeDtypeStruct((rows, sna...]
    ppermute x14, waiting for transfers between devices: 19.3 us -> 17.4 us  [partner(): return lax.ppermute(value, axis, [(i, i ^ bit) for i in range(count)])]
    unnamed x17 -> x13, local copies, waits for them, and re-layouts: 3.32 us -> 4.93 us
    ppermute x14, starting transfers between devices: 16.1 us -> 17.6 us  [partner(): return lax.ppermute(value, axis, [(i, i ^ bit) for i in range(count)])]
  transfers between devices with their start and end apart: 18 -> 18, of which waited for: 12 -> 13; matrix products, arithmetic and copies ran while one was open for 3% -> 1% of each run, Pallas kernels for 11% -> 4%
where the time goes in v6:
time: 107 us
  Pallas kernels  47.4 us (44%)
  starting transfers between devices  28 us (26%)
  waiting for transfers between devices  23.8 us (22%)
  local copies, waits for them, and re-layouts  6.24 us (6%)
    pallas_call x1, Pallas kernels, final_call(): pl.pallas_call(functools.partial(final_kernel, inverse_count), out_shape=...  22.5 us
    pallas_call x1, Pallas kernels, tangent_call(): pl.pallas_call(tangent_kernel, out_shape=(jax.ShapeDtypeStruct((rows, sna...  20.4 us
    ppermute x14, starting transfers between devices, partner(): return lax.ppermute(value, axis, [(i, i ^ bit) for i in range(count)])  17.6 us
    ppermute x14, waiting for transfers between devices, partner(): return lax.ppermute(value, axis, [(i, i ^ bit) for i in range(count)])  17.4 us
    ppermute x2, waiting for transfers between devices, shifted(): return lax.ppermute(value, axis, pairs)  6.39 us
    ppermute x2, starting transfers between devices, shifted(): return lax.ppermute(value, axis, pairs)  6.12 us
    unnamed x13, local copies, waits for them, and re-layouts  4.93 us
    pallas_call x1, Pallas kernels, gram_call(): pl.pallas_call(gram_kernel, out_shape=(jax.ShapeDtypeStruct((snaps, 2 * s...  4.5 us
  transfers between devices with their start and end apart: 18, of which 13 were waited for; matrix products, arithmetic and copies ran while one was open for 1% of the time, Pallas kernels for 4%

profile of v6, /device:TPU:0, one launch (start us, length us, event | category | flops | bytes accessed | tf_op | source)
XLA Modules:
  0.0 106.6 jit_solution(6442269899401953894)
XLA Ops:
  0.6 1.3 %fusion.1 = (f32[512,256]{1,0:T(8,128)S(1)}, f32[512,256]{1,0:T(8,128)S(1)}) fusion(f32[8192,256]{1,0:T(8,128)} %snap.3), kind=kLoop, calls=%fused_computation.10 | loop fusion | bytes 2097152 | tf_op jit(solution)/shard_map/slice | solution.py:480
  1.9 6.1 %collective-permute-start.3 = (f32[512,256]{1,0:T(8,128)S(1)}, f32[512,256]{1,0:T(8,128)S(1)}, u32[]{:S(2)}, u32[]{:S(2)}) collective-permute-start(f32[512,256]{1,0:T(8,128)S(1)} %get-tuple-element.23), channel_id=1, source_target_pairs={{0,28},{4,0},{8,4},{12,8},{16,12},{20,16},{24,20},{28,24},{1,29},{... | collective-permute-start | bytes 1572872 | tf_op jit(solution)/shard_map/ppermute | solution.py:435
  8.0 1.3 %collective-permute-start.1 = (f32[512,256]{1,0:T(8,128)S(1)}, f32[512,256]{1,0:T(8,128)S(1)}, u32[]{:S(2)}, u32[]{:S(2)}) collective-permute-start(f32[512,256]{1,0:T(8,128)S(1)} %get-tuple-element.23), channel_id=1, source_target_pairs={{1,0},{2,1},{3,2},{5,4},{6,5},{7,6},{9,8},{10,9},{11,10},{13,12},{... | collective-permute-start | bytes 1572872 | tf_op jit(solution)/shard_map/ppermute | solution.py:441
  9.3 3.1 %collective-permute-start = (f32[512,256]{1,0:T(8,128)S(1)}, f32[512,256]{1,0:T(8,128)S(1)}, u32[]{:S(2)}, u32[]{:S(2)}) collective-permute-start(f32[512,256]{1,0:T(8,128)S(1)} %get-tuple-element.24), channel_id=1, source_target_pairs={{0,1},{1,2},{2,3},{4,5},{5,6},{6,7},{8,9},{9,10},{10,11},{12,13},{... | collective-permute-start | bytes 1572872 | tf_op jit(solution)/shard_map/ppermute | solution.py:441
  12.4 0.8 copy.8.pattern_ref
  13.2 3.4 %copy-done = f32[8192,256]{1,0:T(8,128)S(1)} copy-done((f32[8192,256]{1,0:T(8,128)S(1)}, f32[8192,256]{1,0:T(8,128)}, u32[]{:S(2)}) %copy-start) | copy-done | bytes 8388632
  16.6 0.8 copy-done.1
  17.3 4.5 %gram.1 = (f32[256,512]{1,0:T(8,128)S(1)}, f32[1,256]{1,0:T(1,128)S(1)}) custom-call(f32[8192,256]{1,0:T(8,128)S(1)} %copy-done, f32[64,128]{1,0:T(8,128)S(1)} %bitcast.6), custom_call_target="tpu_custom_call" | custom-call | flops 2147483648 | bytes 8388608 | tf_op jit(solution)/shard_map/gram/pallas_call | solution.py:76
  21.8 6.3 %collective-permute-done.3.next_ref = f32[512,256]{1,0:T(8,128)S(1)} collective-permute-done((f32[512,256]{1,0:T(8,128)S(1)}, f32[512,256]{1,0:T(8,128)S(1)}, u32[]{:S(2)}, u32[]{:S(2)}) %collective-permute-start.3) | collective-permute-done | bytes 524320 | tf_op jit(solution)/shard_map/ppermute | solution.py:435
  28.2 20.4 %tangent.1 = (f32[8192,256]{1,0:T(8,128)S(1)}, f32[4,40,256]{2,1,0:T(8,128)S(1)}, f32[4,40,256]{2,1,0:T(8,128)S(1)}, f32[4,32,256]{2,1,0:T(8,128)S(1)}, f32[4,32,256]{2,1,0:T(8,128)S(1)}) custom-call(s32[64,4]{1,0:T(8,128)S(1)} %copy.8.pattern_ref, s32[1]{0:T(128)} %bitcast.place_ref, f32[8192,256]{1,0:T(8,128)} %snap.3, ...), custom_call_target="tpu_custom_call" | custom-call | tf_op jit(solution)/shard_map/tangent/pallas_call | solution.py:208
  48.9 0.3 collective-permute-start.4
  49.2 0.8 collective-permute-done.7
  50.1 2.5 %collective-permute-start.8 = (f32[2,32,256]{2,1,0:T(8,128)S(1)}, f32[2,32,256]{2,1,0:T(8,128)S(1)}, u32[]{:S(2)}, u32[]{:S(2)}) collective-permute-start(f32[2,32,256]{2,1,0:T(8,128)S(1)} %slice.53), channel_id=1, source_target_pairs={{0,4},{4,0},{8,12},{12,8},{16,20},{20,16},{24,28},{28,24},{1,5},{5... | collective-permute-start | bytes 196616 | tf_op jit(solution)/shard_map/ppermute | solution.py:446
  52.7 1.6 %collective-permute-start.5 = (f32[2,40,256]{2,1,0:T(8,128)S(1)}, f32[2,40,256]{2,1,0:T(8,128)S(1)}, u32[]{:S(2)}, u32[]{:S(2)}) collective-permute-start(f32[2,40,256]{2,1,0:T(8,128)S(1)} %slice.49), channel_id=1, source_target_pairs={{0,2},{1,3},{2,0},{3,1},{4,6},{5,7},{6,4},{7,5},{8,10},{9,11},{10,... | collective-permute-start | bytes 245768 | tf_op jit(solution)/shard_map/ppermute | solution.py:446
  54.3 0.8 collective-permute-done.8
  55.1 1.6 %collective-permute-start.9 = (f32[1,32,256]{2,1,0:T(8,128)S(1)}, f32[1,32,256]{2,1,0:T(8,128)S(1)}, u32[]{:S(2)}, u32[]{:S(2)}) collective-permute-start(f32[1,32,256]{2,1,0:T(8,128)S(1)} %slice.55), channel_id=1, source_target_pairs={{0,2},{1,3},{2,0},{3,1},{4,6},{5,7},{6,4},{7,5},{8,10},{9,11},{10,... | collective-permute-start | bytes 98312 | tf_op jit(solution)/shard_map/ppermute | solution.py:446
  56.7 0.5 collective-permute-done.5
  57.2 1.4 %collective-permute-start.6 = (f32[1,40,256]{2,1,0:T(8,128)S(1)}, f32[1,40,256]{2,1,0:T(8,128)S(1)}, u32[]{:S(2)}, u32[]{:S(2)}) collective-permute-start(f32[1,40,256]{2,1,0:T(8,128)S(1)} %slice.51), channel_id=1, source_target_pairs={{0,4},{4,0},{8,12},{12,8},{16,20},{20,16},{24,28},{28,24},{1,5},{5... | collective-permute-start | bytes 122888 | tf_op jit(solution)/shard_map/ppermute | solution.py:446
  58.6 0.4 collective-permute-done.9
  59.1 2.2 %collective-permute-done.6 = f32[1,40,256]{2,1,0:T(8,128)S(1)} collective-permute-done((f32[1,40,256]{2,1,0:T(8,128)S(1)}, f32[1,40,256]{2,1,0:T(8,128)S(1)}, u32[]{:S(2)}, u32[]{:S(2)}) %collective-permute-start.6) | collective-permute-done | bytes 40992 | tf_op jit(solution)/shard_map/ppermute | solution.py:446
  61.3 1.7 %collective-permute-start.10 = (f32[1,72,256]{2,1,0:T(8,128)S(1)}, f32[1,72,256]{2,1,0:T(8,128)S(1)}, u32[]{:S(2)}, u32[]{:S(2)}) collective-permute-start(f32[1,72,256]{2,1,0:T(8,128)S(1)} %pad_maximum_fusion.3), channel_id=1, source_target_pairs={{0,8},{4,12},{8,0},{12,4},{16,24},{20,28},{24,16},{28,20},{1,9},{5... | collective-permute-start | bytes 221192 | tf_op jit(solution)/shard_map/ppermute | solution.py:446
  63.0 2.8 %collective-permute-done.10 = f32[1,72,256]{2,1,0:T(8,128)S(1)} collective-permute-done((f32[1,72,256]{2,1,0:T(8,128)S(1)}, f32[1,72,256]{2,1,0:T(8,128)S(1)}, u32[]{:S(2)}, u32[]{:S(2)}) %collective-permute-start.10) | collective-permute-done | bytes 73760 | tf_op jit(solution)/shard_map/ppermute | solution.py:446
  65.7 4.4 %collective-permute-start.11 = (f32[1,72,256]{2,1,0:T(8,128)S(1)}, f32[1,72,256]{2,1,0:T(8,128)S(1)}, u32[]{:S(2)}, u32[]{:S(2)}) collective-permute-start(f32[1,72,256]{2,1,0:T(8,128)S(1)} %fusion), channel_id=1, source_target_pairs={{0,16},{4,20},{8,24},{12,28},{16,0},{20,4},{24,8},{28,12},{1,17},{... | collective-permute-start | bytes 221192 | tf_op jit(solution)/shard_map/ppermute | solution.py:446
  70.2 2.3 %collective-permute-done.11 = f32[1,72,256]{2,1,0:T(8,128)S(1)} collective-permute-done((f32[1,72,256]{2,1,0:T(8,128)S(1)}, f32[1,72,256]{2,1,0:T(8,128)S(1)}, u32[]{:S(2)}, u32[]{:S(2)}) %collective-permute-start.11) | collective-permute-done | bytes 73760 | tf_op jit(solution)/shard_map/ppermute | solution.py:446
  72.5 1.6 %collective-permute-start.12 = (f32[1,40,256]{2,1,0:T(8,128)S(1)}, f32[1,40,256]{2,1,0:T(8,128)S(1)}, u32[]{:S(2)}, u32[]{:S(2)}) collective-permute-start(f32[1,40,256]{2,1,0:T(8,128)S(1)} %slice.56), channel_id=1, source_target_pairs={{0,4},{4,0},{8,12},{12,8},{16,20},{20,16},{24,28},{28,24},{1,5},{5... | collective-permute-start | bytes 122888 | tf_op jit(solution)/shard_map/ppermute | solution.py:446
  74.2 2.4 %collective-permute-done.12 = f32[1,40,256]{2,1,0:T(8,128)S(1)} collective-permute-done((f32[1,40,256]{2,1,0:T(8,128)S(1)}, f32[1,40,256]{2,1,0:T(8,128)S(1)}, u32[]{:S(2)}, u32[]{:S(2)}) %collective-permute-start.12) | collective-permute-done | bytes 40992 | tf_op jit(solution)/shard_map/ppermute | solution.py:446
  76.6 1.5 %collective-permute-start.13 = (f32[2,40,256]{2,1,0:T(8,128)S(1)}, f32[2,40,256]{2,1,0:T(8,128)S(1)}, u32[]{:S(2)}, u32[]{:S(2)}) collective-permute-start(f32[2,40,256]{2,1,0:T(8,128)S(1)} %pad_maximum_fusion.2), channel_id=1, source_target_pairs={{0,2},{1,3},{2,0},{3,1},{4,6},{5,7},{6,4},{7,5},{8,10},{9,11},{10,... | collective-permute-start | bytes 245768 | tf_op jit(solution)/shard_map/ppermute | solution.py:446
  78.1 0.4 collective-permute-start.16
  78.6 2.5 %collective-permute-done.13 = f32[2,40,256]{2,1,0:T(8,128)S(1)} collective-permute-done((f32[2,40,256]{2,1,0:T(8,128)S(1)}, f32[2,40,256]{2,1,0:T(8,128)S(1)}, u32[]{:S(2)}, u32[]{:S(2)}) %collective-permute-start.13) | collective-permute-done | bytes 81952 | tf_op jit(solution)/shard_map/ppermute | solution.py:446
  81.1 1.3 %collective-permute-done.16 = f32[2,32,256]{2,1,0:T(8,128)S(1)} collective-permute-done((f32[2,32,256]{2,1,0:T(8,128)S(1)}, f32[2,32,256]{2,1,0:T(8,128)S(1)}, u32[]{:S(2)}, u32[]{:S(2)}) %collective-permute-start.16) | collective-permute-done | bytes 65568 | tf_op jit(solution)/shard_map/ppermute | solution.py:446
  82.6 1.3 %collective-permute-done.17.second_high = f32[4,32,256]{2,1,0:T(8,128)S(1)} collective-permute-done((f32[4,32,256]{2,1,0:T(8,128)S(1)}, f32[4,32,256]{2,1,0:T(8,128)S(1)}, u32[]{:S(2)}, u32[]{:S(2)}) %collective-permute-start.17) | collective-permute-done | bytes 131104 | tf_op jit(solution)/shard_map/ppermute | solution.py:446
  83.9 22.5 %final.1 = (f32[8192,256]{1,0:T(8,128)}, f32[3,256]{1,0:T(4,128)}, f32[64,128]{1,0:T(8,128)}) custom-call(s32[1]{0:T(128)} %bitcast.place_ref, f32[4,40,256]{2,1,0:T(8,128)S(1)} %pad_maximum_fusion.first_low, f32[4,40,256]{2,1,0:T(8,128)S(1)} %collective-permute-done.14.first_high, f32[4,32,256]{2,1,0:T(8,128)S(1)} %pad_maximum_fusion.1.second_low, ...), custom_call_target="tpu_custom_call" | custom-call | tf_op jit(solution)/shard_map/final/pallas_call | solution.py:408
  (41 shorter events, 0.8 us)
Async XLA Ops:
  0.6 27.6 %copy-start.2 = (f32[8192]{0:T(1024)S(1)}, f32[8192]{0:T(1024)}, u32[]{:S(2)}) copy-start(f32[8192]{0:T(1024)} %param.8) | copy-start | bytes 98308
  1.9 26.2 %collective-permute-start.3 = (f32[512,256]{1,0:T(8,128)S(1)}, f32[512,256]{1,0:T(8,128)S(1)}, u32[]{:S(2)}, u32[]{:S(2)}) collective-permute-start(f32[512,256]{1,0:T(8,128)S(1)} %get-tuple-element.23), channel_id=1, source_target_pairs={{0,28},{4,0},{8,4},{12,8},{16,12},{20,16},{24,20},{28,24},{1,29},{... | collective-permute-start | bytes 1572872 | tf_op jit(solution)/shard_map/ppermute | solution.py:435
  8.0 20.1 %collective-permute-start.1 = (f32[512,256]{1,0:T(8,128)S(1)}, f32[512,256]{1,0:T(8,128)S(1)}, u32[]{:S(2)}, u32[]{:S(2)}) collective-permute-start(f32[512,256]{1,0:T(8,128)S(1)} %get-tuple-element.23), channel_id=1, source_target_pairs={{1,0},{2,1},{3,2},{5,4},{6,5},{7,6},{9,8},{10,9},{11,10},{13,12},{... | collective-permute-start | bytes 1572872 | tf_op jit(solution)/shard_map/ppermute | solution.py:441
  9.3 19.0 %collective-permute-start.2 = (f32[512,256]{1,0:T(8,128)S(1)}, f32[512,256]{1,0:T(8,128)S(1)}, u32[]{:S(2)}, u32[]{:S(2)}) collective-permute-start(f32[512,256]{1,0:T(8,128)S(1)} %get-tuple-element.24), channel_id=1, source_target_pairs={{0,4},{4,8},{8,12},{12,16},{16,20},{20,24},{24,28},{28,0},{1,5},{5... | collective-permute-start | bytes 1572872 | tf_op jit(solution)/shard_map/ppermute | solution.py:435
  9.3 18.9 %collective-permute-start = (f32[512,256]{1,0:T(8,128)S(1)}, f32[512,256]{1,0:T(8,128)S(1)}, u32[]{:S(2)}, u32[]{:S(2)}) collective-permute-start(f32[512,256]{1,0:T(8,128)S(1)} %get-tuple-element.24), channel_id=1, source_target_pairs={{0,1},{1,2},{2,3},{4,5},{5,6},{6,7},{8,9},{9,10},{10,11},{12,13},{... | collective-permute-start | bytes 1572872 | tf_op jit(solution)/shard_map/ppermute | solution.py:441
  13.2 3.4 %copy-start = (f32[8192,256]{1,0:T(8,128)S(1)}, f32[8192,256]{1,0:T(8,128)}, u32[]{:S(2)}) copy-start(f32[8192,256]{1,0:T(8,128)} %snap.3) | copy-start | bytes 25165828
  16.6 0.8 copy-start.1
  28.2 55.7 %slice-start = ((s8[8388608]{0:T(1024)(128)(4,1)}), s8[4194304]{0:T(1024)(128)(4,1)S(1)}, s32[]{:S(2)}) async-start(s8[8388608]{0:T(1024)(128)(4,1)} %bitcast.4), calls=%async_computation | async-start | bytes 8388608
  28.2 55.7 %slice-start.1 = ((s8[8388608]{0:T(1024)(128)(4,1)}), s8[4194304]{0:T(1024)(128)(4,1)S(1)}, s32[]{:S(2)}) async-start(s8[8388608]{0:T(1024)(128)(4,1)} %bitcast.4), calls=%async_computation.1 | async-start | bytes 8388608
  28.2 55.7 %copy-start.3 = (s32[256]{0:T(256)S(1)}, s32[256]{0:T(256)}, u32[]{:S(2)}) copy-start(s32[256]{0:T(256)} %param.9) | copy-start | bytes 3076
  48.6 1.4 %collective-permute-start.7 = (f32[4,32,256]{2,1,0:T(8,128)S(1)}, f32[4,32,256]{2,1,0:T(8,128)S(1)}, u32[]{:S(2)}, u32[]{:S(2)}) collective-permute-start(f32[4,32,256]{2,1,0:T(8,128)S(1)} %get-tuple-element.18), channel_id=1, source_target_pairs={{0,1},{1,0},{2,3},{3,2},{4,5},{5,4},{6,7},{7,6},{8,9},{9,8},{10,11... | collective-permute-start | bytes 393224 | tf_op jit(solution)/shard_map/ppermute | solution.py:446
  48.9 3.7 %collective-permute-start.4 = (f32[4,40,256]{2,1,0:T(8,128)S(1)}, f32[4,40,256]{2,1,0:T(8,128)S(1)}, u32[]{:S(2)}, u32[]{:S(2)}) collective-permute-start(f32[4,40,256]{2,1,0:T(8,128)S(1)} %get-tuple-element.16), channel_id=1, source_target_pairs={{0,1},{1,0},{2,3},{3,2},{4,5},{5,4},{6,7},{7,6},{8,9},{9,8},{10,11... | collective-permute-start | bytes 491528 | tf_op jit(solution)/shard_map/ppermute | solution.py:446
  50.1 4.9 %collective-permute-start.8 = (f32[2,32,256]{2,1,0:T(8,128)S(1)}, f32[2,32,256]{2,1,0:T(8,128)S(1)}, u32[]{:S(2)}, u32[]{:S(2)}) collective-permute-start(f32[2,32,256]{2,1,0:T(8,128)S(1)} %slice.53), channel_id=1, source_target_pairs={{0,4},{4,0},{8,12},{12,8},{16,20},{20,16},{24,28},{28,24},{1,5},{5... | collective-permute-start | bytes 196616 | tf_op jit(solution)/shard_map/ppermute | solution.py:446
  52.7 4.5 %collective-permute-start.5 = (f32[2,40,256]{2,1,0:T(8,128)S(1)}, f32[2,40,256]{2,1,0:T(8,128)S(1)}, u32[]{:S(2)}, u32[]{:S(2)}) collective-permute-start(f32[2,40,256]{2,1,0:T(8,128)S(1)} %slice.49), channel_id=1, source_target_pairs={{0,2},{1,3},{2,0},{3,1},{4,6},{5,7},{6,4},{7,5},{8,10},{9,11},{10,... | collective-permute-start | bytes 245768 | tf_op jit(solution)/shard_map/ppermute | solution.py:446
  55.1 4.0 %collective-permute-start.9 = (f32[1,32,256]{2,1,0:T(8,128)S(1)}, f32[1,32,256]{2,1,0:T(8,128)S(1)}, u32[]{:S(2)}, u32[]{:S(2)}) collective-permute-start(f32[1,32,256]{2,1,0:T(8,128)S(1)} %slice.55), channel_id=1, source_target_pairs={{0,2},{1,3},{2,0},{3,1},{4,6},{5,7},{6,4},{7,5},{8,10},{9,11},{10,... | collective-permute-start | bytes 98312 | tf_op jit(solution)/shard_map/ppermute | solution.py:446
  57.2 4.1 %collective-permute-start.6 = (f32[1,40,256]{2,1,0:T(8,128)S(1)}, f32[1,40,256]{2,1,0:T(8,128)S(1)}, u32[]{:S(2)}, u32[]{:S(2)}) collective-permute-start(f32[1,40,256]{2,1,0:T(8,128)S(1)} %slice.51), channel_id=1, source_target_pairs={{0,4},{4,0},{8,12},{12,8},{16,20},{20,16},{24,28},{28,24},{1,5},{5... | collective-permute-start | bytes 122888 | tf_op jit(solution)/shard_map/ppermute | solution.py:446
  61.3 4.4 %collective-permute-start.10 = (f32[1,72,256]{2,1,0:T(8,128)S(1)}, f32[1,72,256]{2,1,0:T(8,128)S(1)}, u32[]{:S(2)}, u32[]{:S(2)}) collective-permute-start(f32[1,72,256]{2,1,0:T(8,128)S(1)} %pad_maximum_fusion.3), channel_id=1, source_target_pairs={{0,8},{4,12},{8,0},{12,4},{16,24},{20,28},{24,16},{28,20},{1,9},{5... | collective-permute-start | bytes 221192 | tf_op jit(solution)/shard_map/ppermute | solution.py:446
  65.7 6.8 %collective-permute-start.11 = (f32[1,72,256]{2,1,0:T(8,128)S(1)}, f32[1,72,256]{2,1,0:T(8,128)S(1)}, u32[]{:S(2)}, u32[]{:S(2)}) collective-permute-start(f32[1,72,256]{2,1,0:T(8,128)S(1)} %fusion), channel_id=1, source_target_pairs={{0,16},{4,20},{8,24},{12,28},{16,0},{20,4},{24,8},{28,12},{1,17},{... | collective-permute-start | bytes 221192 | tf_op jit(solution)/shard_map/ppermute | solution.py:446
  72.5 4.1 %collective-permute-start.12 = (f32[1,40,256]{2,1,0:T(8,128)S(1)}, f32[1,40,256]{2,1,0:T(8,128)S(1)}, u32[]{:S(2)}, u32[]{:S(2)}) collective-permute-start(f32[1,40,256]{2,1,0:T(8,128)S(1)} %slice.56), channel_id=1, source_target_pairs={{0,4},{4,0},{8,12},{12,8},{16,20},{20,16},{24,28},{28,24},{1,5},{5... | collective-permute-start | bytes 122888 | tf_op jit(solution)/shard_map/ppermute | solution.py:446
  74.1 4.0 %collective-permute-start.15 = (f32[1,32,256]{2,1,0:T(8,128)S(1)}, f32[1,32,256]{2,1,0:T(8,128)S(1)}, u32[]{:S(2)}, u32[]{:S(2)}) collective-permute-start(f32[1,32,256]{2,1,0:T(8,128)S(1)} %slice.57), channel_id=1, source_target_pairs={{0,2},{1,3},{2,0},{3,1},{4,6},{5,7},{6,4},{7,5},{8,10},{9,11},{10,... | collective-permute-start | bytes 98312 | tf_op jit(solution)/shard_map/ppermute | solution.py:446
  76.6 4.4 %collective-permute-start.13 = (f32[2,40,256]{2,1,0:T(8,128)S(1)}, f32[2,40,256]{2,1,0:T(8,128)S(1)}, u32[]{:S(2)}, u32[]{:S(2)}) collective-permute-start(f32[2,40,256]{2,1,0:T(8,128)S(1)} %pad_maximum_fusion.2), channel_id=1, source_target_pairs={{0,2},{1,3},{2,0},{3,1},{4,6},{5,7},{6,4},{7,5},{8,10},{9,11},{10,... | collective-permute-start | bytes 245768 | tf_op jit(solution)/shard_map/ppermute | solution.py:446
  78.1 4.3 %collective-permute-start.16 = (f32[2,32,256]{2,1,0:T(8,128)S(1)}, f32[2,32,256]{2,1,0:T(8,128)S(1)}, u32[]{:S(2)}, u32[]{:S(2)}) collective-permute-start(f32[2,32,256]{2,1,0:T(8,128)S(1)} %pad_maximum_fusion.4), channel_id=1, source_target_pairs={{0,4},{4,0},{8,12},{12,8},{16,20},{20,16},{24,28},{28,24},{1,5},{5... | collective-permute-start | bytes 196616 | tf_op jit(solution)/shard_map/ppermute | solution.py:446
  81.1 2.8 %collective-permute-start.14 = (f32[4,40,256]{2,1,0:T(8,128)S(1)}, f32[4,40,256]{2,1,0:T(8,128)S(1)}, u32[]{:S(2)}, u32[]{:S(2)}) collective-permute-start(f32[4,40,256]{2,1,0:T(8,128)S(1)} %pad_maximum_fusion.first_low), channel_id=1, source_target_pairs={{0,1},{1,0},{2,3},{3,2},{4,5},{5,4},{6,7},{7,6},{8,9},{9,8},{10,11... | collective-permute-start | bytes 491528 | tf_op jit(solution)/shard_map/ppermute | solution.py:446
  82.5 1.4 %collective-permute-start.17 = (f32[4,32,256]{2,1,0:T(8,128)S(1)}, f32[4,32,256]{2,1,0:T(8,128)S(1)}, u32[]{:S(2)}, u32[]{:S(2)}) collective-permute-start(f32[4,32,256]{2,1,0:T(8,128)S(1)} %pad_maximum_fusion.1.second_low), channel_id=1, source_target_pairs={{0,1},{1,0},{2,3},{3,2},{4,5},{5,4},{6,7},{7,6},{8,9},{9,8},{10,11... | collective-permute-start | bytes 393224 | tf_op jit(solution)/shard_map/ppermute | solution.py:446

commit v7 on v6

--- a/solution.py
+++ b/solution.py
@@ -34,16 +34,8 @@
     )
 
 
-def first_piece(at):
-    return ((at >> 2) & 1) | (at & 2) | ((at & 1) << 2)
-
-
-def second_piece(at):
-    return ((at >> 2) & 1) | ((at & 1) << 1) | ((at & 2) << 1)
-
-
-def second_place(piece):
-    return ((piece & 1) << 2) | ((piece >> 1) & 1) | ((piece >> 1) & 2)
+def piece_at(position):
+    return ((position >> 2) & 1) | (position & 2) | ((position & 1) << 2)
 
 
 def force_product(panel, force):
@@ -55,7 +47,7 @@
     return total
 
 
-def gram_kernel(snap_ref, force_ref, gram_ref, load_ref):
+def gram_kernel(snap_ref, force_ref, field_ref, turned_ref, gram_ref, load_ref):
     rows = snap_ref.shape[0]
     per_chunk = CHUNK // force_ref.shape[1]
     gram_ref[...] = jnp.zeros_like(gram_ref)
@@ -63,9 +55,16 @@
 
     @pl.loop(0, rows // CHUNK)
     def _(i):
-        panel = snap_ref[pl.ds(pl.multiple_of(i * CHUNK, CHUNK), CHUNK), :]
+        at = pl.ds(pl.multiple_of(i * CHUNK, CHUNK), CHUNK)
+        panel = snap_ref[at, :]
+        snaps = panel.shape[1]
         high, low = split(panel)
-        gram_ref[...] += matmul(high.T, jnp.concatenate([high, low], 1))
+        turned = high.T
+        field_ref[at, :snaps] = high
+        field_ref[at, snaps:] = low
+        turned_ref[i, :snaps, :] = turned
+        turned_ref[i, snaps:, :] = low.T
+        gram_ref[...] += matmul(turned, jnp.concatenate([high, low], 1))
         line = pl.ds(pl.multiple_of(i * per_chunk, per_chunk), per_chunk)
         load_ref[...] += force_product(panel, force_ref[line, :])
 
@@ -76,11 +75,13 @@
     return pl.pallas_call(
         gram_kernel,
         out_shape=(
+            jax.ShapeDtypeStruct((rows, 2 * snaps), BF16),
+            jax.ShapeDtypeStruct((rows // CHUNK, 2 * snaps, CHUNK), BF16),
             jax.ShapeDtypeStruct((snaps, 2 * snaps), F32),
             jax.ShapeDtypeStruct((1, snaps), F32),
         ),
         in_specs=[vmem, vmem],
-        out_specs=[vmem, vmem],
+        out_specs=[vmem] * 4,
         compiler_params=pltpu.CompilerParams(vmem_limit_bytes=10 * MIB),
         cost_estimate=pl.CostEstimate(
             flops=4 * rows * snaps * snaps, bytes_accessed=4 * rows * snaps, transcendentals=0
@@ -92,7 +93,8 @@
 def tangent_kernel(
     pattern_ref,
     place_ref,
-    snap,
+    field,
+    turned,
     left_ref,
     right_ref,
     prev_ref,
@@ -102,11 +104,9 @@
     gram_ref,
     load_ref,
     image,
-    keep_first,
-    send_first,
-    keep_second,
-    send_second,
-    field,
+    keep_ref,
+    send_ref,
+    halo,
     mixed,
     rest,
     load,
@@ -128,18 +128,11 @@
     for i in range(chunks):
         tangent_copy(i).start()
 
-    def enter(at, value):
-        high, low = split(value)
-        field[at, :snaps] = high
-        field[at, snaps:] = low
-
-    @pl.loop(0, chunks)
-    def _(i):
-        at = pl.ds(pl.multiple_of(i * CHUNK, CHUNK), CHUNK)
-        enter(at, snap[at, :])
-
     for i, ref in enumerate((left_ref, right_ref, prev_ref, next_ref)):
-        enter(pl.ds(rows + i * edge, edge), ref[...])
+        high, low = split(ref[...])
+        at = pl.ds(i * edge, edge)
+        halo[at, :snaps] = high
+        halo[at, snaps:] = low
     mixed[...] = jnp.zeros_like(mixed)
     rest[...] = jnp.zeros_like(rest)
     load[...] = load_ref[...]
@@ -147,8 +140,6 @@
     @pl.loop(0, chunks)
     def _(step):
         start = pl.multiple_of(step * CHUNK, CHUNK)
-        here = field[pl.ds(start, CHUNK), :]
-        panels = [here[:, :snaps].T, here[:, snaps:].T]
         tangent_copy(step).wait()
         images = []
         for k in range(per_chunk):
@@ -158,10 +149,13 @@
                 code = pattern_ref[g, e]
                 source = lax.div(code, block_count)
                 pick = lax.rem(code, block_count)
+                here = source == 0
                 tail = (source == 1) | (source == 3)
-                base = jnp.where(source == 0, 0, block_count + ((source + 1) & 3) * HALO)
-                at = base + jnp.where(tail, pick - (block_count - HALO), pick)
-                picked.append(field[pl.ds(pl.multiple_of(at * block, block), block), :])
+                beyond = ((source + 1) & 3) * HALO + jnp.where(tail, pick - (block_count - HALO), pick)
+                beyond = jnp.where(here, 0, beyond)
+                inner = field[pl.ds(pl.multiple_of(pick * block, block), block), :]
+                outer = halo[pl.ds(pl.multiple_of(beyond * block, block), block), :]
+                picked.append(lax.select(here, inner, outer))
             own = pl.ds(pl.multiple_of(start + k * block, block), block)
             both = matmul(tangent[own, :], jnp.concatenate(picked, 0))
             part = STEP_SIZE * (both[:, :snaps] + both[:, snaps:])
@@ -172,8 +166,9 @@
         load[...] += force_product(panel, force_ref[line, :])
         high, low = split(panel)
         high_turned = high.T
-        mixed[...] += matmul(jnp.concatenate([*panels, high_turned], 0), high)
-        rest[...] += matmul(jnp.concatenate([panels[0], high_turned], 0), low)
+        panels = turned[step]
+        mixed[...] += matmul(jnp.concatenate([panels, high_turned], 0), high)
+        rest[...] += matmul(jnp.concatenate([panels[:snaps], high_turned], 0), low)
 
     gram = gram_ref[:, :snaps] + gram_ref[:, snaps:] + gram_ref[:, snaps:].T
     cross = mixed[:snaps] + mixed[snaps : 2 * snaps] + rest[:snaps]
@@ -187,31 +182,29 @@
     extra = jnp.where(extra_row == 0, load[...], jnp.where(extra_row == 1, diagonal, 0.0))
     share = snaps // PARTS
     for at in range(PARTS):
-        first = keep_first if at < PARTS // 2 else send_first
-        second = keep_second if at < PARTS // 2 else send_second
+        out = keep_ref if at < PARTS // 2 else send_ref
         slot = at % (PARTS // 2)
-        begin = pl.multiple_of((place_ref[0] ^ first_piece(at)) * share, 8)
-        first[slot, :share, :] = packed[0, pl.ds(begin, share), :]
-        first[slot, share:, :] = extra
-        begin = pl.multiple_of((place_ref[0] ^ second_piece(at)) * share, 8)
-        second[slot] = packed[1, pl.ds(begin, share), :]
-
-
-def tangent_call(snapshots, halos, tangent, pattern, force, gram, load, place):
-    rows, snaps = snapshots.shape
+        begin = pl.multiple_of((place_ref[0] ^ piece_at(at)) * share, 8)
+        out[slot, :share, :] = packed[0, pl.ds(begin, share), :]
+        out[slot, share : 2 * share, :] = packed[1, pl.ds(begin, share), :]
+        out[slot, 2 * share :, :] = extra
+
+
+def tangent_call(field, turned, halos, tangent, pattern, force, gram, load, place):
+    rows = tangent.shape[0]
+    snaps = gram.shape[0]
     share = snaps // PARTS
     edge = halos[0].shape[0]
     vmem = pl.BlockSpec(memory_space=pltpu.VMEM)
     smem = pl.BlockSpec(memory_space=pltpu.SMEM)
-    first = jax.ShapeDtypeStruct((PARTS // 2, share + 8, snaps), F32)
-    second = jax.ShapeDtypeStruct((PARTS // 2, share, snaps), F32)
+    packed = jax.ShapeDtypeStruct((PARTS // 2, 2 * share + 8, snaps), F32)
     return pl.pallas_call(
         tangent_kernel,
-        out_shape=(jax.ShapeDtypeStruct((rows, snaps), F32), first, first, second, second),
-        in_specs=[smem, smem] + [vmem] * 5 + [pl.BlockSpec(memory_space=pl.ANY)] + [vmem] * 3,
-        out_specs=[vmem] * 5,
+        out_shape=(jax.ShapeDtypeStruct((rows, snaps), F32), packed, packed),
+        in_specs=[smem, smem] + [vmem] * 6 + [pl.BlockSpec(memory_space=pl.ANY)] + [vmem] * 3,
+        out_specs=[vmem] * 3,
         scratch_shapes=[
-            pltpu.VMEM((rows + 4 * edge, 2 * snaps), BF16),
+            pltpu.VMEM((4 * edge, 2 * snaps), BF16),
             pltpu.VMEM((3 * snaps, snaps), F32),
             pltpu.VMEM((2 * snaps, snaps), F32),
             pltpu.VMEM((1, snaps), F32),
@@ -219,9 +212,9 @@
             pltpu.VMEM(tangent.shape, BF16),
             pltpu.SemaphoreType.DMA((rows // CHUNK,)),
         ],
-        compiler_params=pltpu.CompilerParams(vmem_limit_bytes=40 * MIB),
+        compiler_params=pltpu.CompilerParams(vmem_limit_bytes=18 * MIB),
         name="tangent",
-    )(pattern, place, snapshots, *halos, tangent, force, gram, load)
+    )(pattern, place, field, turned, *halos, tangent, force, gram, load)
 
 
 def inverse_factors(blocks):
@@ -274,16 +267,15 @@
     )
 
 
-def reduced_system(inverse_count, place, first, second, index):
-    snaps = first.shape[2]
+def reduced_system(inverse_count, place, pack, index):
+    snaps = pack.shape[2]
     share = snaps // PARTS
     half = snaps // 2
-    order = [first_piece(place ^ c) for c in range(PARTS)]
-    packed = jnp.concatenate([first[at, :share, :] for at in order], 0) * inverse_count
-    load = first[0, share : share + 1, :] * inverse_count
-    diagonal = first[0, share + 1 : share + 2, :] * inverse_count
-    order = [second_place(place ^ c) for c in range(PARTS)]
-    cross = jnp.concatenate([second[at] for at in order], 0) * inverse_count
+    order = [piece_at(place ^ c) for c in range(PARTS)]
+    packed = jnp.concatenate([pack[at, :share, :] for at in order], 0) * inverse_count
+    cross = jnp.concatenate([pack[at, share : 2 * share, :] for at in order], 0) * inverse_count
+    load = pack[0, 2 * share : 2 * share + 1, :] * inverse_count
+    diagonal = pack[0, 2 * share + 1 : 2 * share + 2, :] * inverse_count
     row = lax.broadcasted_iota(jnp.int32, (snaps, snaps), 0)
     column = lax.broadcasted_iota(jnp.int32, (snaps, snaps), 1)
     turned = packed.T
@@ -328,10 +320,8 @@
 def final_kernel(
     inverse_count,
     place_ref,
-    first_low,
-    first_high,
-    second_low,
-    second_high,
+    low_ref,
+    high_ref,
     index_ref,
     force_ref,
     snap,
@@ -339,8 +329,7 @@
     basis_any,
     coeff_ref,
     residual_ref,
-    first,
-    second,
+    pack,
     root_ref,
     change_ref,
     state_ref,
@@ -357,13 +346,11 @@
         return pl.ds(pl.multiple_of(i * CHUNK, CHUNK), CHUNK)
 
     def out_copy(i):
-        return pltpu.make_async_copy(basis.at[i % 2], basis_any.at[chunk(i), :], sems.at[i % 2])
-
-    first[: PARTS // 2] = first_low[...]
-    first[PARTS // 2 :] = first_high[...]
-    second[: PARTS // 2] = second_low[...]
-    second[PARTS // 2 :] = second_high[...]
-    root, history, change, state = reduced_system(inverse_count, place_ref[0], first, second, index_ref[...])
+        return pltpu.make_async_copy(basis.at[chunk(i), :], basis_any.at[chunk(i), :], sems.at[i])
+
+    pack[: PARTS // 2] = low_ref[...]
+    pack[PARTS // 2 :] = high_ref[...]
+    root, history, change, state = reduced_system(inverse_count, place_ref[0], pack, index_ref[...])
     high, low = split(root)
     root_ref[:, :snaps] = high
     root_ref[:, snaps:] = low
@@ -385,17 +372,13 @@
         tile[...] = gathered
         panel_high, panel_low = split(panel)
         both = matmul(panel_high, root_ref[...])
-
-        @pl.when(i >= 2)
-        def _():
-            out_copy(i - 2).wait()
-
-        basis[i % 2] = both[:, :snaps] + both[:, snaps:] + matmul(panel_low, root_ref[:, :snaps])
+        basis[at, :] = both[:, :snaps] + both[:, snaps:] + matmul(panel_low, root_ref[:, :snaps])
         out_copy(i).start()
 
     residual_ref[...] = tile[...].T[: rows // block] - STEP_SIZE * force_ref[...]
 
-    for i in range(chunks - 2, chunks):
+    @pl.loop(0, chunks)
+    def _(i):
         out_copy(i).wait()
 
 
@@ -412,19 +395,18 @@
             jax.ShapeDtypeStruct((STEPS, snaps), F32),
             jax.ShapeDtypeStruct(force.shape, F32),
         ),
-        in_specs=[pl.BlockSpec(memory_space=pltpu.SMEM)] + [vmem] * 8,
+        in_specs=[pl.BlockSpec(memory_space=pltpu.SMEM)] + [vmem] * 6,
         out_specs=[hbm, vmem, vmem],
         scratch_shapes=[
-            pltpu.VMEM((PARTS, share + 8, snaps), F32),
-            pltpu.VMEM((PARTS, share, snaps), F32),
+            pltpu.VMEM((PARTS, 2 * share + 8, snaps), F32),
             pltpu.VMEM((snaps, 2 * snaps), BF16),
             pltpu.VMEM((1, snaps), F32),
             pltpu.VMEM((1, snaps), F32),
             pltpu.VMEM((block, block), F32),
-            pltpu.VMEM((2, CHUNK, snaps), F32),
-            pltpu.SemaphoreType.DMA((2,)),
+            pltpu.VMEM((rows, snaps), F32),
+            pltpu.SemaphoreType.DMA((rows // CHUNK,)),
         ],
-        compiler_params=pltpu.CompilerParams(vmem_limit_bytes=12 * MIB),
+        compiler_params=pltpu.CompilerParams(vmem_limit_bytes=18 * MIB),
         name="final",
     )(place, *pieces, step_index, force, snapshots, image)
 
@@ -446,26 +428,19 @@
     return lax.ppermute(value, axis, [(i, i ^ bit) for i in range(count)])
 
 
-def reduce_packed(keep_first, send_first, keep_second, send_second):
+def reduce_packed(keep, send):
     core, x, y = ("zone", 1), ("zone", 2), ("rows", 1)
-    first = keep_first + partner(send_first, *core)
-    second = keep_second + partner(send_second, *core)
-    for way_first, way_second in ((x, y), (y, x)):
-        half = first.shape[0] // 2
-        first = first[:half] + partner(first[half:], *way_first)
-        second = second[:half] + partner(second[half:], *way_second)
-    edge = first.shape[1]
-    value = jnp.concatenate([first, second], 1)
-    for axis, least in (("rows", 2), ("zone", 4)):
-        bit = least
+    value = keep + partner(send, *core)
+    for way in (x, y):
+        half = value.shape[0] // 2
+        value = value[:half] + partner(value[half:], *way)
+    for axis, bit in (("rows", 2), ("zone", 4)):
         while bit < lax.axis_size(axis):
             value = value + partner(value, axis, bit)
             bit *= 2
-    first, second = value[:, :edge], value[:, edge:]
-    for way_first, way_second in ((y, x), (x, y)):
-        first = jnp.concatenate([first, partner(first, *way_first)], 0)
-        second = jnp.concatenate([second, partner(second, *way_second)], 0)
-    return first, partner(first, *core), second, partner(second, *core)
+    for way in (y, x):
+        value = jnp.concatenate([value, partner(value, *way)], 0)
+    return value, partner(value, *core)
 
 
 def shards(snapshots, tangent, pattern, forcing, step_index):
@@ -480,9 +455,9 @@
     head, tail = snapshots[:edge], snapshots[rows - edge :]
     rows_prev = shifted(tail, "rows", 1)
     rows_next = shifted(head, "rows", -1)
-    gram, load = gram_call(snapshots, force)
+    field, turned, gram, load = gram_call(snapshots, force)
     halos = (from_behind(tail, "zone", 1), from_behind(head, "zone", -1), rows_prev, rows_next)
-    image, *packed = tangent_call(snapshots, halos, tangent, pattern, force, gram, load, place)
+    image, *packed = tangent_call(field, turned, halos, tangent, pattern, force, gram, load, place)
     pieces = reduce_packed(*packed)
     basis, coefficients, residual = final_call(
         pieces, step_index.reshape(1, snaps), place, snapshots, image, force, inverse_count

time: 107 us -> 99.5 us (0.930)
  Pallas kernels: 47.4 us -> 41.4 us
  starting transfers between devices: 28 us -> 24.4 us
  waiting for transfers between devices: 23.8 us -> 25.8 us
    pallas_call x1, Pallas kernels: 20.4 us -> 15.3 us  [tangent_call(): pl.pallas_call(tangent_kernel, out_shape=(jax.ShapeDtypeStruct((rows, sna...]
    ppermute x14 -> x8, starting transfers between devices: 17.6 us -> 13.9 us  [partner(): return lax.ppermute(value, axis, [(i, i ^ bit) for i in range(count)])]
    ppermute x14 -> x8, waiting for transfers between devices: 17.4 us -> 20.7 us  [partner(): return lax.ppermute(value, axis, [(i, i ^ bit) for i in range(count)])]
    pallas_call x1, Pallas kernels: 22.5 us -> 20.3 us  [final_call(): pl.pallas_call(functools.partial(final_kernel, inverse_count), out_shape=...]
    ppermute x2, waiting for transfers between devices: 6.39 us -> 5.1 us  [shifted(): return lax.ppermute(value, axis, pairs)]
    pallas_call x1, Pallas kernels: 4.5 us -> 5.78 us  [gram_call(): pl.pallas_call(gram_kernel, out_shape=(jax.ShapeDtypeStruct((rows, 2 * sn...]
  transfers between devices with their start and end apart: 18 -> 12, of which waited for: 13 -> 10; matrix products, arithmetic and copies ran while one was open for 1% -> 1% of each run, Pallas kernels for 4% -> 6%
where the time goes in v7:
time: 99.5 us; the launch traced here: 98.9 us
  Pallas kernels  41.4 us (42%)
  waiting for transfers between devices  25.8 us (26%)
  starting transfers between devices  24.4 us (25%)
  local copies, waits for them, and re-layouts  6.22 us (6%)
    ppermute x8, waiting for transfers between devices, partner(): return lax.ppermute(value, axis, [(i, i ^ bit) for i in range(count)])  20.7 us
    pallas_call x1, Pallas kernels, final_call(): pl.pallas_call(functools.partial(final_kernel, inverse_count), out_shape=...  20.3 us
    pallas_call x1, Pallas kernels, tangent_call(): pl.pallas_call(tangent_kernel, out_shape=(jax.ShapeDtypeStruct((rows, sna...  15.3 us
    ppermute x8, starting transfers between devices, partner(): return lax.ppermute(value, axis, [(i, i ^ bit) for i in range(count)])  13.9 us
    ppermute x2, starting transfers between devices, shifted(): return lax.ppermute(value, axis, pairs)  6.12 us
    pallas_call x1, Pallas kernels, gram_call(): pl.pallas_call(gram_kernel, out_shape=(jax.ShapeDtypeStruct((rows, 2 * sn...  5.78 us
    ppermute x2, waiting for transfers between devices, shifted(): return lax.ppermute(value, axis, pairs)  5.1 us
    unnamed x13, local copies, waits for them, and re-layouts  4.93 us
  transfers between devices with their start and end apart: 12, of which 10 were waited for; matrix products, arithmetic and copies ran while one was open for 1% of the time, Pallas kernels for 6%

profile of v7, /device:TPU:0, one launch (start us, length us, event | category | flops | bytes accessed | tf_op | source)
XLA Modules:
  0.0 98.9 jit_solution(15729833495524159962)
XLA Ops:
  0.6 1.3 %fusion = (f32[512,256]{1,0:T(8,128)S(1)}, f32[512,256]{1,0:T(8,128)S(1)}) fusion(f32[8192,256]{1,0:T(8,128)} %snap.1), kind=kLoop, calls=%fused_computation.4 | loop fusion | bytes 2097152 | tf_op jit(solution)/shard_map/slice | solution.py:455
  1.9 6.1 %collective-permute-start.3 = (f32[512,256]{1,0:T(8,128)S(1)}, f32[512,256]{1,0:T(8,128)S(1)}, u32[]{:S(2)}, u32[]{:S(2)}) collective-permute-start(f32[512,256]{1,0:T(8,128)S(1)} %get-tuple-element.23), channel_id=1, source_target_pairs={{0,28},{4,0},{8,4},{12,8},{16,12},{20,16},{24,20},{28,24},{1,29},{... | collective-permute-start | bytes 1572872 | tf_op jit(solution)/shard_map/ppermute | solution.py:417
  8.0 1.3 %collective-permute-start.1 = (f32[512,256]{1,0:T(8,128)S(1)}, f32[512,256]{1,0:T(8,128)S(1)}, u32[]{:S(2)}, u32[]{:S(2)}) collective-permute-start(f32[512,256]{1,0:T(8,128)S(1)} %get-tuple-element.23), channel_id=1, source_target_pairs={{1,0},{2,1},{3,2},{5,4},{6,5},{7,6},{9,8},{10,9},{11,10},{13,12},{... | collective-permute-start | bytes 1572872 | tf_op jit(solution)/shard_map/ppermute | solution.py:423
  9.2 0.1 collective-permute-start.2
  9.3 3.1 %collective-permute-start = (f32[512,256]{1,0:T(8,128)S(1)}, f32[512,256]{1,0:T(8,128)S(1)}, u32[]{:S(2)}, u32[]{:S(2)}) collective-permute-start(f32[512,256]{1,0:T(8,128)S(1)} %get-tuple-element.24), channel_id=1, source_target_pairs={{0,1},{1,2},{2,3},{4,5},{5,6},{6,7},{8,9},{9,10},{10,11},{12,13},{... | collective-permute-start | bytes 1572872 | tf_op jit(solution)/shard_map/ppermute | solution.py:423
  12.4 0.8 copy.8.pattern_ref
  13.2 3.4 %copy-done = f32[8192,256]{1,0:T(8,128)S(1)} copy-done((f32[8192,256]{1,0:T(8,128)S(1)}, f32[8192,256]{1,0:T(8,128)}, u32[]{:S(2)}) %copy-start) | copy-done | bytes 8388632
  16.5 0.8 copy-done.2
  17.3 5.8 %gram.1 = (bf16[8192,512]{1,0:T(8,128)(2,1)S(1)}, bf16[8,512,1024]{2,1,0:T(8,128)(2,1)S(1)}, f32[256,512]{1,0:T(8,128)S(1)}, f32[1,256]{1,0:T(1,128)S(1)}) custom-call(f32[8192,256]{1,0:T(8,128)S(1)} %copy-done, f32[64,128]{1,0:T(8,128)S(1)} %bitcast.6), custom_call_target="tpu_custom_call" | custom-call | flops 2147483648 | bytes 8388608 | tf_op jit(solution)/shard_map/gram/pallas_call | solution.py:75
  23.1 5.0 %collective-permute-done.3.next_ref = f32[512,256]{1,0:T(8,128)S(1)} collective-permute-done((f32[512,256]{1,0:T(8,128)S(1)}, f32[512,256]{1,0:T(8,128)S(1)}, u32[]{:S(2)}, u32[]{:S(2)}) %collective-permute-start.3) | collective-permute-done | bytes 524320 | tf_op jit(solution)/shard_map/ppermute | solution.py:417
  28.1 0.0 collective-permute-done.1.right_ref
  28.1 0.1 collective-permute-done.2.prev_ref
  28.2 0.0 collective-permute-done.left_ref
  28.2 0.0 copy-start.3
  28.2 15.3 %tangent.1 = (f32[8192,256]{1,0:T(8,128)S(1)}, f32[4,72,256]{2,1,0:T(8,128)S(1)}, f32[4,72,256]{2,1,0:T(8,128)S(1)}) custom-call(s32[64,4]{1,0:T(8,128)S(1)} %copy.8.pattern_ref, s32[1]{0:T(128)} %bitcast.place_ref, bf16[8192,512]{1,0:T(8,128)(2,1)S(1)} %get-tuple-element.13.field, bf16[8,512,1024]{2,1,0:T(8,128)(2,1)S(1)} %get-tuple-element.14.turned, ...), custom_call_target="tpu_custom_call" | custom-call | tf_op jit(solution)/shard_map/tangent/pallas_call | solution.py:201
  43.5 0.3 collective-permute-start.4
  43.8 1.4 %collective-permute-done.4 = f32[4,72,256]{2,1,0:T(8,128)S(1)} collective-permute-done((f32[4,72,256]{2,1,0:T(8,128)S(1)}, f32[4,72,256]{2,1,0:T(8,128)S(1)}, u32[]{:S(2)}, u32[]{:S(2)}) %collective-permute-start.4) | collective-permute-done | bytes 294944 | tf_op jit(solution)/shard_map/ppermute | solution.py:428
  45.3 1.7 %collective-permute-start.5 = (f32[2,72,256]{2,1,0:T(8,128)S(1)}, f32[2,72,256]{2,1,0:T(8,128)S(1)}, u32[]{:S(2)}, u32[]{:S(2)}) collective-permute-start(f32[2,72,256]{2,1,0:T(8,128)S(1)} %slice.25), channel_id=1, source_target_pairs={{0,2},{1,3},{2,0},{3,1},{4,6},{5,7},{6,4},{7,5},{8,10},{9,11},{10,... | collective-permute-start | bytes 442376 | tf_op jit(solution)/shard_map/ppermute | solution.py:428
  46.9 4.3 %collective-permute-done.5 = f32[2,72,256]{2,1,0:T(8,128)S(1)} collective-permute-done((f32[2,72,256]{2,1,0:T(8,128)S(1)}, f32[2,72,256]{2,1,0:T(8,128)S(1)}, u32[]{:S(2)}, u32[]{:S(2)}) %collective-permute-start.5) | collective-permute-done | bytes 147488 | tf_op jit(solution)/shard_map/ppermute | solution.py:428
  51.3 2.5 %collective-permute-start.6 = (f32[1,72,256]{2,1,0:T(8,128)S(1)}, f32[1,72,256]{2,1,0:T(8,128)S(1)}, u32[]{:S(2)}, u32[]{:S(2)}) collective-permute-start(f32[1,72,256]{2,1,0:T(8,128)S(1)} %slice.27), channel_id=1, source_target_pairs={{0,4},{4,0},{8,12},{12,8},{16,20},{20,16},{24,28},{28,24},{1,5},{5... | collective-permute-start | bytes 221192 | tf_op jit(solution)/shard_map/ppermute | solution.py:428
  53.8 2.3 %collective-permute-done.6 = f32[1,72,256]{2,1,0:T(8,128)S(1)} collective-permute-done((f32[1,72,256]{2,1,0:T(8,128)S(1)}, f32[1,72,256]{2,1,0:T(8,128)S(1)}, u32[]{:S(2)}, u32[]{:S(2)}) %collective-permute-start.6) | collective-permute-done | bytes 73760 | tf_op jit(solution)/shard_map/ppermute | solution.py:428
  56.1 1.7 %collective-permute-start.7 = (f32[1,72,256]{2,1,0:T(8,128)S(1)}, f32[1,72,256]{2,1,0:T(8,128)S(1)}, u32[]{:S(2)}, u32[]{:S(2)}) collective-permute-start(f32[1,72,256]{2,1,0:T(8,128)S(1)} %slice_add_fusion.1), channel_id=1, source_target_pairs={{0,8},{4,12},{8,0},{12,4},{16,24},{20,28},{24,16},{28,20},{1,9},{5... | collective-permute-start | bytes 221192 | tf_op jit(solution)/shard_map/ppermute | solution.py:428
  57.8 2.7 %collective-permute-done.7 = f32[1,72,256]{2,1,0:T(8,128)S(1)} collective-permute-done((f32[1,72,256]{2,1,0:T(8,128)S(1)}, f32[1,72,256]{2,1,0:T(8,128)S(1)}, u32[]{:S(2)}, u32[]{:S(2)}) %collective-permute-start.7) | collective-permute-done | bytes 73760 | tf_op jit(solution)/shard_map/ppermute | solution.py:428
  60.6 4.0 %collective-permute-start.8 = (f32[1,72,256]{2,1,0:T(8,128)S(1)}, f32[1,72,256]{2,1,0:T(8,128)S(1)}, u32[]{:S(2)}, u32[]{:S(2)}) collective-permute-start(f32[1,72,256]{2,1,0:T(8,128)S(1)} %add.18), channel_id=1, source_target_pairs={{0,16},{4,20},{8,24},{12,28},{16,0},{20,4},{24,8},{28,12},{1,17},{... | collective-permute-start | bytes 221192 | tf_op jit(solution)/shard_map/ppermute | solution.py:428
  64.6 2.3 %collective-permute-done.8 = f32[1,72,256]{2,1,0:T(8,128)S(1)} collective-permute-done((f32[1,72,256]{2,1,0:T(8,128)S(1)}, f32[1,72,256]{2,1,0:T(8,128)S(1)}, u32[]{:S(2)}, u32[]{:S(2)}) %collective-permute-start.8) | collective-permute-done | bytes 73760 | tf_op jit(solution)/shard_map/ppermute | solution.py:428
  67.0 2.2 %collective-permute-start.9 = (f32[1,72,256]{2,1,0:T(8,128)S(1)}, f32[1,72,256]{2,1,0:T(8,128)S(1)}, u32[]{:S(2)}, u32[]{:S(2)}) collective-permute-start(f32[1,72,256]{2,1,0:T(8,128)S(1)} %add.19), channel_id=1, source_target_pairs={{0,4},{4,0},{8,12},{12,8},{16,20},{20,16},{24,28},{28,24},{1,5},{5... | collective-permute-start | bytes 221192 | tf_op jit(solution)/shard_map/ppermute | solution.py:428
  69.1 2.3 %collective-permute-done.9 = f32[1,72,256]{2,1,0:T(8,128)S(1)} collective-permute-done((f32[1,72,256]{2,1,0:T(8,128)S(1)}, f32[1,72,256]{2,1,0:T(8,128)S(1)}, u32[]{:S(2)}, u32[]{:S(2)}) %collective-permute-start.9) | collective-permute-done | bytes 73760 | tf_op jit(solution)/shard_map/ppermute | solution.py:428
  71.5 1.6 %collective-permute-start.10 = (f32[2,72,256]{2,1,0:T(8,128)S(1)}, f32[2,72,256]{2,1,0:T(8,128)S(1)}, u32[]{:S(2)}, u32[]{:S(2)}) collective-permute-start(f32[2,72,256]{2,1,0:T(8,128)S(1)} %pad_maximum_fusion.1), channel_id=1, source_target_pairs={{0,2},{1,3},{2,0},{3,1},{4,6},{5,7},{6,4},{7,5},{8,10},{9,11},{10,... | collective-permute-start | bytes 442376 | tf_op jit(solution)/shard_map/ppermute | solution.py:428
  73.0 3.6 %collective-permute-done.10 = f32[2,72,256]{2,1,0:T(8,128)S(1)} collective-permute-done((f32[2,72,256]{2,1,0:T(8,128)S(1)}, f32[2,72,256]{2,1,0:T(8,128)S(1)}, u32[]{:S(2)}, u32[]{:S(2)}) %collective-permute-start.10) | collective-permute-done | bytes 147488 | tf_op jit(solution)/shard_map/ppermute | solution.py:428
  76.7 0.1 collective-permute-start.11
  76.8 1.6 %collective-permute-done.11.high_ref = f32[4,72,256]{2,1,0:T(8,128)S(1)} collective-permute-done((f32[4,72,256]{2,1,0:T(8,128)S(1)}, f32[4,72,256]{2,1,0:T(8,128)S(1)}, u32[]{:S(2)}, u32[]{:S(2)}) %collective-permute-start.11) | collective-permute-done | bytes 294944 | tf_op jit(solution)/shard_map/ppermute | solution.py:428
  78.4 20.3 %final.1 = (f32[8192,256]{1,0:T(8,128)}, f32[3,256]{1,0:T(4,128)}, f32[64,128]{1,0:T(8,128)}) custom-call(s32[1]{0:T(128)} %bitcast.place_ref, f32[4,72,256]{2,1,0:T(8,128)S(1)} %pad_maximum_fusion.low_ref, f32[4,72,256]{2,1,0:T(8,128)S(1)} %collective-permute-done.11.high_ref, s32[1,256]{1,0:T(1,128)S(1)} %bitcast.9, f32[64,128]{1,0:T(8,128)S(1)} %bitcast.8, ...), custom_call_target="tpu_custom_call" | custom-call | tf_op jit(solution)/shard_map/final/pallas_call | solution.py:391
  (19 shorter events, 0.2 us)
Async XLA Ops:
  1.9 26.2 %collective-permute-start.3 = (f32[512,256]{1,0:T(8,128)S(1)}, f32[512,256]{1,0:T(8,128)S(1)}, u32[]{:S(2)}, u32[]{:S(2)}) collective-permute-start(f32[512,256]{1,0:T(8,128)S(1)} %get-tuple-element.23), channel_id=1, source_target_pairs={{0,28},{4,0},{8,4},{12,8},{16,12},{20,16},{24,20},{28,24},{1,29},{... | collective-permute-start | bytes 1572872 | tf_op jit(solution)/shard_map/ppermute | solution.py:417
  8.0 20.1 %collective-permute-start.1 = (f32[512,256]{1,0:T(8,128)S(1)}, f32[512,256]{1,0:T(8,128)S(1)}, u32[]{:S(2)}, u32[]{:S(2)}) collective-permute-start(f32[512,256]{1,0:T(8,128)S(1)} %get-tuple-element.23), channel_id=1, source_target_pairs={{1,0},{2,1},{3,2},{5,4},{6,5},{7,6},{9,8},{10,9},{11,10},{13,12},{... | collective-permute-start | bytes 1572872 | tf_op jit(solution)/shard_map/ppermute | solution.py:423
  9.2 19.0 %collective-permute-start.2 = (f32[512,256]{1,0:T(8,128)S(1)}, f32[512,256]{1,0:T(8,128)S(1)}, u32[]{:S(2)}, u32[]{:S(2)}) collective-permute-start(f32[512,256]{1,0:T(8,128)S(1)} %get-tuple-element.24), channel_id=1, source_target_pairs={{0,4},{4,8},{8,12},{12,16},{16,20},{20,24},{24,28},{28,0},{1,5},{5... | collective-permute-start | bytes 1572872 | tf_op jit(solution)/shard_map/ppermute | solution.py:417
  9.3 18.9 %collective-permute-start = (f32[512,256]{1,0:T(8,128)S(1)}, f32[512,256]{1,0:T(8,128)S(1)}, u32[]{:S(2)}, u32[]{:S(2)}) collective-permute-start(f32[512,256]{1,0:T(8,128)S(1)} %get-tuple-element.24), channel_id=1, source_target_pairs={{0,1},{1,2},{2,3},{4,5},{5,6},{6,7},{8,9},{9,10},{10,11},{12,13},{... | collective-permute-start | bytes 1572872 | tf_op jit(solution)/shard_map/ppermute | solution.py:423
  13.2 3.4 %copy-start = (f32[8192,256]{1,0:T(8,128)S(1)}, f32[8192,256]{1,0:T(8,128)}, u32[]{:S(2)}) copy-start(f32[8192,256]{1,0:T(8,128)} %snap.1) | copy-start | bytes 25165828
  16.5 0.8 copy-start.2
  17.3 10.9 %copy-start.1 = (bf16[8192,512]{1,0:T(8,128)(2,1)S(1)}, bf16[8192,512]{1,0:T(8,128)(2,1)}, u32[]{:S(2)}) copy-start(bf16[8192,512]{1,0:T(8,128)(2,1)} %tangent_any.1) | copy-start | bytes 25165828
  28.2 50.1 %slice-start = ((s8[8388608]{0:T(1024)(128)(4,1)}), s8[4194304]{0:T(1024)(128)(4,1)S(1)}, s32[]{:S(2)}) async-start(s8[8388608]{0:T(1024)(128)(4,1)} %bitcast.4), calls=%async_computation | async-start | bytes 8388608
  28.2 50.1 %slice-start.1 = ((s8[8388608]{0:T(1024)(128)(4,1)}), s8[4194304]{0:T(1024)(128)(4,1)S(1)}, s32[]{:S(2)}) async-start(s8[8388608]{0:T(1024)(128)(4,1)} %bitcast.4), calls=%async_computation.1 | async-start | bytes 8388608
  28.2 50.1 %copy-start.3 = (s32[256]{0:T(256)S(1)}, s32[256]{0:T(256)}, u32[]{:S(2)}) copy-start(s32[256]{0:T(256)} %param.9) | copy-start | bytes 3076
  43.5 1.6 %collective-permute-start.4 = (f32[4,72,256]{2,1,0:T(8,128)S(1)}, f32[4,72,256]{2,1,0:T(8,128)S(1)}, u32[]{:S(2)}, u32[]{:S(2)}) collective-permute-start(f32[4,72,256]{2,1,0:T(8,128)S(1)} %get-tuple-element.18), channel_id=1, source_target_pairs={{0,1},{1,0},{2,3},{3,2},{4,5},{5,4},{6,7},{7,6},{8,9},{9,8},{10,11... | collective-permute-start | bytes 884744 | tf_op jit(solution)/shard_map/ppermute | solution.py:428
  45.3 6.0 %collective-permute-start.5 = (f32[2,72,256]{2,1,0:T(8,128)S(1)}, f32[2,72,256]{2,1,0:T(8,128)S(1)}, u32[]{:S(2)}, u32[]{:S(2)}) collective-permute-start(f32[2,72,256]{2,1,0:T(8,128)S(1)} %slice.25), channel_id=1, source_target_pairs={{0,2},{1,3},{2,0},{3,1},{4,6},{5,7},{6,4},{7,5},{8,10},{9,11},{10,... | collective-permute-start | bytes 442376 | tf_op jit(solution)/shard_map/ppermute | solution.py:428
  51.3 4.8 %collective-permute-start.6 = (f32[1,72,256]{2,1,0:T(8,128)S(1)}, f32[1,72,256]{2,1,0:T(8,128)S(1)}, u32[]{:S(2)}, u32[]{:S(2)}) collective-permute-start(f32[1,72,256]{2,1,0:T(8,128)S(1)} %slice.27), channel_id=1, source_target_pairs={{0,4},{4,0},{8,12},{12,8},{16,20},{20,16},{24,28},{28,24},{1,5},{5... | collective-permute-start | bytes 221192 | tf_op jit(solution)/shard_map/ppermute | solution.py:428
  56.1 4.4 %collective-permute-start.7 = (f32[1,72,256]{2,1,0:T(8,128)S(1)}, f32[1,72,256]{2,1,0:T(8,128)S(1)}, u32[]{:S(2)}, u32[]{:S(2)}) collective-permute-start(f32[1,72,256]{2,1,0:T(8,128)S(1)} %slice_add_fusion.1), channel_id=1, source_target_pairs={{0,8},{4,12},{8,0},{12,4},{16,24},{20,28},{24,16},{28,20},{1,9},{5... | collective-permute-start | bytes 221192 | tf_op jit(solution)/shard_map/ppermute | solution.py:428
  60.6 6.4 %collective-permute-start.8 = (f32[1,72,256]{2,1,0:T(8,128)S(1)}, f32[1,72,256]{2,1,0:T(8,128)S(1)}, u32[]{:S(2)}, u32[]{:S(2)}) collective-permute-start(f32[1,72,256]{2,1,0:T(8,128)S(1)} %add.18), channel_id=1, source_target_pairs={{0,16},{4,20},{8,24},{12,28},{16,0},{20,4},{24,8},{28,12},{1,17},{... | collective-permute-start | bytes 221192 | tf_op jit(solution)/shard_map/ppermute | solution.py:428
  67.0 4.5 %collective-permute-start.9 = (f32[1,72,256]{2,1,0:T(8,128)S(1)}, f32[1,72,256]{2,1,0:T(8,128)S(1)}, u32[]{:S(2)}, u32[]{:S(2)}) collective-permute-start(f32[1,72,256]{2,1,0:T(8,128)S(1)} %add.19), channel_id=1, source_target_pairs={{0,4},{4,0},{8,12},{12,8},{16,20},{20,16},{24,28},{28,24},{1,5},{5... | collective-permute-start | bytes 221192 | tf_op jit(solution)/shard_map/ppermute | solution.py:428
  71.5 5.2 %collective-permute-start.10 = (f32[2,72,256]{2,1,0:T(8,128)S(1)}, f32[2,72,256]{2,1,0:T(8,128)S(1)}, u32[]{:S(2)}, u32[]{:S(2)}) collective-permute-start(f32[2,72,256]{2,1,0:T(8,128)S(1)} %pad_maximum_fusion.1), channel_id=1, source_target_pairs={{0,2},{1,3},{2,0},{3,1},{4,6},{5,7},{6,4},{7,5},{8,10},{9,11},{10,... | collective-permute-start | bytes 442376 | tf_op jit(solution)/shard_map/ppermute | solution.py:428
  76.7 1.6 %collective-permute-start.11 = (f32[4,72,256]{2,1,0:T(8,128)S(1)}, f32[4,72,256]{2,1,0:T(8,128)S(1)}, u32[]{:S(2)}, u32[]{:S(2)}) collective-permute-start(f32[4,72,256]{2,1,0:T(8,128)S(1)} %pad_maximum_fusion.low_ref), channel_id=1, source_target_pairs={{0,1},{1,0},{2,3},{3,2},{4,5},{5,4},{6,7},{7,6},{8,9},{9,8},{10,11... | collective-permute-start | bytes 884744 | tf_op jit(solution)/shard_map/ppermute | solution.py:428

commit v8 on v7

--- a/solution.py
+++ b/solution.py
@@ -217,6 +217,13 @@
     )(pattern, place, field, turned, *halos, tangent, force, gram, load)
 
 
+def reciprocal(value):
+    result = pl.reciprocal(value, approx=True)
+    for _ in range(2):
+        result = result * (2.0 - value * result)
+    return result
+
+
 def inverse_factors(blocks):
     size = blocks[0].shape[0]
     groups = size // 8
@@ -235,29 +242,35 @@
         ]
         work = [jnp.where(inside, unit, rows[m][g]) for m in range(count)]
         kept = [jnp.zeros((8, size), F32) for _ in range(count)]
+        pivots = [spread(columns[m][0][0:1, :]) for m in range(count)]
         for j in range(8):
+            mine = sub == j
             for m in range(count):
-                pivot = spread(columns[m][j][j : j + 1, :])
-                inverse = 1.0 / pivot
+                pivot, column = pivots[m], columns[m][j]
+                inverse = reciprocal(pivot)
+                tops = [spread(columns[m][k][j : j + 1, :]) for k in range(j + 1, 8)]
+                if j < 7:
+                    below = spread(column[j + 1 : j + 2, :]) * tops[0]
+                    pivots[m] = spread(columns[m][j + 1][j + 1 : j + 2, :]) - below * inverse
+                for k in range(j + 1, 8):
+                    top = tops[k - j - 1]
+                    step = jnp.where(mine, -top, column * top)
+                    columns[m][k] = jnp.where(mine, 0.0, columns[m][k]) - step * inverse
+                row = spread(work[m][j : j + 1, :])
+                step = jnp.where(mine, -row, column * row)
+                work[m] = jnp.where(mine, 0.0, work[m]) - step * inverse
                 root = lax.rsqrt(pivot)
                 root = root * (1.5 - 0.5 * pivot * root * root)
-                mine = sub == j
-                for k in range(j + 1, 8):
-                    scaled = spread(columns[m][k][j : j + 1, :]) * inverse
-                    columns[m][k] = jnp.where(mine, scaled, columns[m][k] - columns[m][j] * scaled)
-                row = spread(work[m][j : j + 1, :])
                 kept[m] = jnp.where(mine, row * root, kept[m])
-                scaled = row * inverse
-                work[m] = jnp.where(mine, scaled, work[m] - columns[m][j] * scaled)
         for m in range(count):
             done[m].append(jnp.where(lane < first + 8, kept[m], 0.0))
-            pivots = [spread(work[m][j : j + 1, :]) for j in range(8)]
+            solved = [spread(work[m][j : j + 1, :]) for j in range(8)]
             for i in range(g + 1, groups):
                 old = rows[m][i]
-                new = jnp.where(inside, 0.0, old)
-                for j in range(8):
-                    new = new - spread(old[:, first + j : first + j + 1]) * pivots[j]
-                rows[m][i] = new
+                terms = [spread(old[:, first + j : first + j + 1]) * solved[j] for j in range(8)]
+                while len(terms) > 1:
+                    terms = [a + b for a, b in zip(terms[::2], terms[1::2])]
+                rows[m][i] = jnp.where(inside, 0.0, old) - terms[0]
     return [jnp.concatenate(values, 0) for values in done]
 
 
@@ -428,19 +441,24 @@
     return lax.ppermute(value, axis, [(i, i ^ bit) for i in range(count)])
 
 
+def across(value, line_bit, zone_bit):
+    zones = lax.axis_size("zone")
+    count = zones * lax.axis_size("rows")
+    pairs = [(i, (i // zones ^ line_bit) * zones + (i % zones ^ zone_bit)) for i in range(count)]
+    return lax.ppermute(value, ("rows", "zone"), pairs)
+
+
 def reduce_packed(keep, send):
-    core, x, y = ("zone", 1), ("zone", 2), ("rows", 1)
-    value = keep + partner(send, *core)
-    for way in (x, y):
-        half = value.shape[0] // 2
-        value = value[:half] + partner(value[half:], *way)
+    value = keep + partner(send, "zone", 1)
+    ways = ((1, 0), (0, 2), (1, 2))
+    others = [across(value[at + 1 : at + 2], *way) for at, way in enumerate(ways)]
+    value = value[:1] + others[0] + others[1] + others[2]
     for axis, bit in (("rows", 2), ("zone", 4)):
         while bit < lax.axis_size(axis):
             value = value + partner(value, axis, bit)
             bit *= 2
-    for way in (y, x):
-        value = jnp.concatenate([value, partner(value, *way)], 0)
-    return value, partner(value, *core)
+    value = jnp.concatenate([value] + [across(value, *way) for way in ways], 0)
+    return value, partner(value, "zone", 1)
 
 
 def shards(snapshots, tangent, pattern, forcing, step_index):

time: 99.5 us -> 95.2 us (0.957)
  waiting for transfers between devices: 25.8 us -> 21.3 us
    ppermute x8 -> x4, waiting for transfers between devices: 20.7 us -> 8.01 us  [partner(): return lax.ppermute(value, axis, [(i, i ^ bit) for i in range(count)])]
    ppermute x0 -> x6, waiting for transfers between devices: none -> 8.15 us  [across(): return lax.ppermute(value, ('rows', 'zone'), pairs)]
    ppermute x8 -> x4, starting transfers between devices: 13.9 us -> 6.08 us  [partner(): return lax.ppermute(value, axis, [(i, i ^ bit) for i in range(count)])]
    ppermute x0 -> x6, starting transfers between devices: none -> 7.65 us  [across(): return lax.ppermute(value, ('rows', 'zone'), pairs)]
  transfers between devices with their start and end apart: 12 -> 14, of which waited for: 10 -> 11; matrix products, arithmetic and copies ran while one was open for 1% -> 1% of each run, Pallas kernels for 6% -> 6%
where the time goes in v8:
time: 95.2 us; the launch traced here: 94.9 us
  Pallas kernels  42.2 us (44%)
  starting transfers between devices  24.2 us (25%)
  waiting for transfers between devices  21.3 us (22%)
  local copies, waits for them, and re-layouts  6.22 us (7%)
    pallas_call x1, Pallas kernels, final_call(): pl.pallas_call(functools.partial(final_kernel, inverse_count), out_shape=...  21.1 us
    pallas_call x1, Pallas kernels, tangent_call(): pl.pallas_call(tangent_kernel, out_shape=(jax.ShapeDtypeStruct((rows, sna...  15.3 us
    ppermute x6, waiting for transfers between devices, across(): return lax.ppermute(value, ('rows', 'zone'), pairs)  8.15 us
    ppermute x4, waiting for transfers between devices, partner(): return lax.ppermute(value, axis, [(i, i ^ bit) for i in range(count)])  8.01 us
    ppermute x6, starting transfers between devices, across(): return lax.ppermute(value, ('rows', 'zone'), pairs)  7.65 us
    ppermute x2, starting transfers between devices, shifted(): return lax.ppermute(value, axis, pairs)  6.12 us
    ppermute x4, starting transfers between devices, partner(): return lax.ppermute(value, axis, [(i, i ^ bit) for i in range(count)])  6.08 us
    pallas_call x1, Pallas kernels, gram_call(): pl.pallas_call(gram_kernel, out_shape=(jax.ShapeDtypeStruct((rows, 2 * sn...  5.78 us
  transfers between devices with their start and end apart: 14, of which 11 were waited for; matrix products, arithmetic and copies ran while one was open for 1% of the time, Pallas kernels for 6%

profile of v8, /device:TPU:0, one launch (start us, length us, event | category | flops | bytes accessed | tf_op | source)
XLA Modules:
  0.0 94.9 jit_solution(8250799606110981720)
XLA Ops:
  0.6 1.3 %fusion.2 = (f32[512,256]{1,0:T(8,128)S(1)}, f32[512,256]{1,0:T(8,128)S(1)}) fusion(f32[8192,256]{1,0:T(8,128)} %snap.1), kind=kLoop, calls=%fused_computation.4 | loop fusion | bytes 2097152 | tf_op jit(solution)/shard_map/slice | solution.py:473
  1.9 6.1 %collective-permute-start.3 = (f32[512,256]{1,0:T(8,128)S(1)}, f32[512,256]{1,0:T(8,128)S(1)}, u32[]{:S(2)}, u32[]{:S(2)}) collective-permute-start(f32[512,256]{1,0:T(8,128)S(1)} %get-tuple-element.23), channel_id=1, source_target_pairs={{0,28},{4,0},{8,4},{12,8},{16,12},{20,16},{24,20},{28,24},{1,29},{... | collective-permute-start | bytes 1572872 | tf_op jit(solution)/shard_map/ppermute | solution.py:430
  8.0 1.3 %collective-permute-start.1 = (f32[512,256]{1,0:T(8,128)S(1)}, f32[512,256]{1,0:T(8,128)S(1)}, u32[]{:S(2)}, u32[]{:S(2)}) collective-permute-start(f32[512,256]{1,0:T(8,128)S(1)} %get-tuple-element.23), channel_id=1, source_target_pairs={{1,0},{2,1},{3,2},{5,4},{6,5},{7,6},{9,8},{10,9},{11,10},{13,12},{... | collective-permute-start | bytes 1572872 | tf_op jit(solution)/shard_map/ppermute | solution.py:436
  9.2 0.1 collective-permute-start.2
  9.3 3.1 %collective-permute-start = (f32[512,256]{1,0:T(8,128)S(1)}, f32[512,256]{1,0:T(8,128)S(1)}, u32[]{:S(2)}, u32[]{:S(2)}) collective-permute-start(f32[512,256]{1,0:T(8,128)S(1)} %get-tuple-element.24), channel_id=1, source_target_pairs={{0,1},{1,2},{2,3},{4,5},{5,6},{6,7},{8,9},{9,10},{10,11},{12,13},{... | collective-permute-start | bytes 1572872 | tf_op jit(solution)/shard_map/ppermute | solution.py:436
  12.4 0.8 copy.8.pattern_ref
  13.2 3.4 %copy-done = f32[8192,256]{1,0:T(8,128)S(1)} copy-done((f32[8192,256]{1,0:T(8,128)S(1)}, f32[8192,256]{1,0:T(8,128)}, u32[]{:S(2)}) %copy-start) | copy-done | bytes 8388632
  16.5 0.8 copy-done.2
  17.3 5.8 %gram.1 = (bf16[8192,512]{1,0:T(8,128)(2,1)S(1)}, bf16[8,512,1024]{2,1,0:T(8,128)(2,1)S(1)}, f32[256,512]{1,0:T(8,128)S(1)}, f32[1,256]{1,0:T(1,128)S(1)}) custom-call(f32[8192,256]{1,0:T(8,128)S(1)} %copy-done, f32[64,128]{1,0:T(8,128)S(1)} %bitcast.6), custom_call_target="tpu_custom_call" | custom-call | flops 2147483648 | bytes 8388608 | tf_op jit(solution)/shard_map/gram/pallas_call | solution.py:75
  23.1 5.0 %collective-permute-done.3.next_ref = f32[512,256]{1,0:T(8,128)S(1)} collective-permute-done((f32[512,256]{1,0:T(8,128)S(1)}, f32[512,256]{1,0:T(8,128)S(1)}, u32[]{:S(2)}, u32[]{:S(2)}) %collective-permute-start.3) | collective-permute-done | bytes 524320 | tf_op jit(solution)/shard_map/ppermute | solution.py:430
  28.1 0.1 collective-permute-done.2.prev_ref
  28.2 15.3 %tangent.1 = (f32[8192,256]{1,0:T(8,128)S(1)}, f32[4,72,256]{2,1,0:T(8,128)S(1)}, f32[4,72,256]{2,1,0:T(8,128)S(1)}) custom-call(s32[64,4]{1,0:T(8,128)S(1)} %copy.8.pattern_ref, s32[1]{0:T(128)} %bitcast.place_ref, bf16[8192,512]{1,0:T(8,128)(2,1)S(1)} %get-tuple-element.13.field, bf16[8,512,1024]{2,1,0:T(8,128)(2,1)S(1)} %get-tuple-element.14.turned, ...), custom_call_target="tpu_custom_call" | custom-call | tf_op jit(solution)/shard_map/tangent/pallas_call | solution.py:201
  43.5 0.3 collective-permute-start.4
  43.8 1.4 %collective-permute-done.4 = f32[4,72,256]{2,1,0:T(8,128)S(1)} collective-permute-done((f32[4,72,256]{2,1,0:T(8,128)S(1)}, f32[4,72,256]{2,1,0:T(8,128)S(1)}, u32[]{:S(2)}, u32[]{:S(2)}) %collective-permute-start.4) | collective-permute-done | bytes 294944 | tf_op jit(solution)/shard_map/ppermute | solution.py:441
  45.3 2.6 %collective-permute-start.5 = (f32[1,72,256]{2,1,0:T(8,128)S(1)}, f32[1,72,256]{2,1,0:T(8,128)S(1)}, u32[]{:S(2)}, u32[]{:S(2)}) collective-permute-start(f32[1,72,256]{2,1,0:T(8,128)S(1)} %get-tuple-element.25), channel_id=1, source_target_pairs={{0,4},{1,5},{2,6},{3,7},{4,0},{5,1},{6,2},{7,3},{8,12},{9,13},{10,... | collective-permute-start | bytes 221192 | tf_op jit(solution)/shard_map/ppermute | solution.py:448
  47.8 1.0 %collective-permute-start.7 = (f32[1,72,256]{2,1,0:T(8,128)S(1)}, f32[1,72,256]{2,1,0:T(8,128)S(1)}, u32[]{:S(2)}, u32[]{:S(2)}) collective-permute-start(f32[1,72,256]{2,1,0:T(8,128)S(1)} %get-tuple-element.26), channel_id=1, source_target_pairs={{0,6},{1,7},{2,4},{3,5},{4,2},{5,3},{6,0},{7,1},{8,14},{9,15},{10,... | collective-permute-start | bytes 221192 | tf_op jit(solution)/shard_map/ppermute | solution.py:448
  48.9 0.5 collective-permute-start.6
  49.4 1.9 %collective-permute-done.5 = f32[1,72,256]{2,1,0:T(8,128)S(1)} collective-permute-done((f32[1,72,256]{2,1,0:T(8,128)S(1)}, f32[1,72,256]{2,1,0:T(8,128)S(1)}, u32[]{:S(2)}, u32[]{:S(2)}) %collective-permute-start.5) | collective-permute-done | bytes 73760 | tf_op jit(solution)/shard_map/ppermute | solution.py:448
  51.3 2.5 %collective-permute-done.7 = f32[1,72,256]{2,1,0:T(8,128)S(1)} collective-permute-done((f32[1,72,256]{2,1,0:T(8,128)S(1)}, f32[1,72,256]{2,1,0:T(8,128)S(1)}, u32[]{:S(2)}, u32[]{:S(2)}) %collective-permute-start.7) | collective-permute-done | bytes 73760 | tf_op jit(solution)/shard_map/ppermute | solution.py:448
  53.7 1.7 %collective-permute-start.8 = (f32[1,72,256]{2,1,0:T(8,128)S(1)}, f32[1,72,256]{2,1,0:T(8,128)S(1)}, u32[]{:S(2)}, u32[]{:S(2)}) collective-permute-start(f32[1,72,256]{2,1,0:T(8,128)S(1)} %fusion.1), channel_id=1, source_target_pairs={{0,8},{4,12},{8,0},{12,4},{16,24},{20,28},{24,16},{28,20},{1,9},{5... | collective-permute-start | bytes 221192 | tf_op jit(solution)/shard_map/ppermute | solution.py:441
  55.4 2.7 %collective-permute-done.8 = f32[1,72,256]{2,1,0:T(8,128)S(1)} collective-permute-done((f32[1,72,256]{2,1,0:T(8,128)S(1)}, f32[1,72,256]{2,1,0:T(8,128)S(1)}, u32[]{:S(2)}, u32[]{:S(2)}) %collective-permute-start.8) | collective-permute-done | bytes 73760 | tf_op jit(solution)/shard_map/ppermute | solution.py:441
  58.2 4.1 %collective-permute-start.9 = (f32[1,72,256]{2,1,0:T(8,128)S(1)}, f32[1,72,256]{2,1,0:T(8,128)S(1)}, u32[]{:S(2)}, u32[]{:S(2)}) collective-permute-start(f32[1,72,256]{2,1,0:T(8,128)S(1)} %add.22), channel_id=1, source_target_pairs={{0,16},{4,20},{8,24},{12,28},{16,0},{20,4},{24,8},{28,12},{1,17},{... | collective-permute-start | bytes 221192 | tf_op jit(solution)/shard_map/ppermute | solution.py:441
  62.2 2.3 %collective-permute-done.9 = f32[1,72,256]{2,1,0:T(8,128)S(1)} collective-permute-done((f32[1,72,256]{2,1,0:T(8,128)S(1)}, f32[1,72,256]{2,1,0:T(8,128)S(1)}, u32[]{:S(2)}, u32[]{:S(2)}) %collective-permute-start.9) | collective-permute-done | bytes 73760 | tf_op jit(solution)/shard_map/ppermute | solution.py:441
  64.6 2.1 %collective-permute-start.12 = (f32[1,72,256]{2,1,0:T(8,128)S(1)}, f32[1,72,256]{2,1,0:T(8,128)S(1)}, u32[]{:S(2)}, u32[]{:S(2)}) collective-permute-start(f32[1,72,256]{2,1,0:T(8,128)S(1)} %add.23), channel_id=1, source_target_pairs={{0,6},{1,7},{2,4},{3,5},{4,2},{5,3},{6,0},{7,1},{8,14},{9,15},{10,... | collective-permute-start | bytes 221192 | tf_op jit(solution)/shard_map/ppermute | solution.py:448
  66.7 0.8 collective-permute-start.11
  67.6 0.6 collective-permute-start.10
  68.1 1.8 %collective-permute-done.12 = f32[1,72,256]{2,1,0:T(8,128)S(1)} collective-permute-done((f32[1,72,256]{2,1,0:T(8,128)S(1)}, f32[1,72,256]{2,1,0:T(8,128)S(1)}, u32[]{:S(2)}, u32[]{:S(2)}) %collective-permute-start.12) | collective-permute-done | bytes 73760 | tf_op jit(solution)/shard_map/ppermute | solution.py:448
  69.9 1.2 %collective-permute-done.11 = f32[1,72,256]{2,1,0:T(8,128)S(1)} collective-permute-done((f32[1,72,256]{2,1,0:T(8,128)S(1)}, f32[1,72,256]{2,1,0:T(8,128)S(1)}, u32[]{:S(2)}, u32[]{:S(2)}) %collective-permute-start.11) | collective-permute-done | bytes 73760 | tf_op jit(solution)/shard_map/ppermute | solution.py:448
  71.1 0.8 collective-permute-done.10
  72.0 0.1 collective-permute-start.13
  72.0 1.6 %collective-permute-done.13.high_ref = f32[4,72,256]{2,1,0:T(8,128)S(1)} collective-permute-done((f32[4,72,256]{2,1,0:T(8,128)S(1)}, f32[4,72,256]{2,1,0:T(8,128)S(1)}, u32[]{:S(2)}, u32[]{:S(2)}) %collective-permute-start.13) | collective-permute-done | bytes 294944 | tf_op jit(solution)/shard_map/ppermute | solution.py:441
  73.6 21.1 %final.1 = (f32[8192,256]{1,0:T(8,128)}, f32[3,256]{1,0:T(4,128)}, f32[64,128]{1,0:T(8,128)}) custom-call(s32[1]{0:T(128)} %bitcast.place_ref, f32[4,72,256]{2,1,0:T(8,128)S(1)} %pad_maximum_fusion.low_ref, f32[4,72,256]{2,1,0:T(8,128)S(1)} %collective-permute-done.13.high_ref, s32[1,256]{1,0:T(1,128)S(1)} %bitcast.9, f32[64,128]{1,0:T(8,128)S(1)} %bitcast.8, ...), custom_call_target="tpu_custom_call" | custom-call | tf_op jit(solution)/shard_map/final/pallas_call | solution.py:404
  (20 shorter events, 0.2 us)
Async XLA Ops:
  1.9 26.2 %collective-permute-start.3 = (f32[512,256]{1,0:T(8,128)S(1)}, f32[512,256]{1,0:T(8,128)S(1)}, u32[]{:S(2)}, u32[]{:S(2)}) collective-permute-start(f32[512,256]{1,0:T(8,128)S(1)} %get-tuple-element.23), channel_id=1, source_target_pairs={{0,28},{4,0},{8,4},{12,8},{16,12},{20,16},{24,20},{28,24},{1,29},{... | collective-permute-start | bytes 1572872 | tf_op jit(solution)/shard_map/ppermute | solution.py:430
  8.0 20.1 %collective-permute-start.1 = (f32[512,256]{1,0:T(8,128)S(1)}, f32[512,256]{1,0:T(8,128)S(1)}, u32[]{:S(2)}, u32[]{:S(2)}) collective-permute-start(f32[512,256]{1,0:T(8,128)S(1)} %get-tuple-element.23), channel_id=1, source_target_pairs={{1,0},{2,1},{3,2},{5,4},{6,5},{7,6},{9,8},{10,9},{11,10},{13,12},{... | collective-permute-start | bytes 1572872 | tf_op jit(solution)/shard_map/ppermute | solution.py:436
  9.2 19.0 %collective-permute-start.2 = (f32[512,256]{1,0:T(8,128)S(1)}, f32[512,256]{1,0:T(8,128)S(1)}, u32[]{:S(2)}, u32[]{:S(2)}) collective-permute-start(f32[512,256]{1,0:T(8,128)S(1)} %get-tuple-element.24), channel_id=1, source_target_pairs={{0,4},{4,8},{8,12},{12,16},{16,20},{20,24},{24,28},{28,0},{1,5},{5... | collective-permute-start | bytes 1572872 | tf_op jit(solution)/shard_map/ppermute | solution.py:430
  9.3 18.9 %collective-permute-start = (f32[512,256]{1,0:T(8,128)S(1)}, f32[512,256]{1,0:T(8,128)S(1)}, u32[]{:S(2)}, u32[]{:S(2)}) collective-permute-start(f32[512,256]{1,0:T(8,128)S(1)} %get-tuple-element.24), channel_id=1, source_target_pairs={{0,1},{1,2},{2,3},{4,5},{5,6},{6,7},{8,9},{9,10},{10,11},{12,13},{... | collective-permute-start | bytes 1572872 | tf_op jit(solution)/shard_map/ppermute | solution.py:436
  13.2 3.4 %copy-start = (f32[8192,256]{1,0:T(8,128)S(1)}, f32[8192,256]{1,0:T(8,128)}, u32[]{:S(2)}) copy-start(f32[8192,256]{1,0:T(8,128)} %snap.1) | copy-start | bytes 25165828
  16.5 0.8 copy-start.2
  17.3 10.9 %copy-start.1 = (bf16[8192,512]{1,0:T(8,128)(2,1)S(1)}, bf16[8192,512]{1,0:T(8,128)(2,1)}, u32[]{:S(2)}) copy-start(bf16[8192,512]{1,0:T(8,128)(2,1)} %tangent_any.1) | copy-start | bytes 25165828
  28.2 45.4 %slice-start = ((s8[8388608]{0:T(1024)(128)(4,1)}), s8[4194304]{0:T(1024)(128)(4,1)S(1)}, s32[]{:S(2)}) async-start(s8[8388608]{0:T(1024)(128)(4,1)} %bitcast.4), calls=%async_computation | async-start | bytes 8388608
  28.2 45.4 %slice-start.1 = ((s8[8388608]{0:T(1024)(128)(4,1)}), s8[4194304]{0:T(1024)(128)(4,1)S(1)}, s32[]{:S(2)}) async-start(s8[8388608]{0:T(1024)(128)(4,1)} %bitcast.4), calls=%async_computation.1 | async-start | bytes 8388608
  28.2 45.4 %copy-start.3 = (s32[256]{0:T(256)S(1)}, s32[256]{0:T(256)}, u32[]{:S(2)}) copy-start(s32[256]{0:T(256)} %param.9) | copy-start | bytes 3076
  43.5 1.6 %collective-permute-start.4 = (f32[4,72,256]{2,1,0:T(8,128)S(1)}, f32[4,72,256]{2,1,0:T(8,128)S(1)}, u32[]{:S(2)}, u32[]{:S(2)}) collective-permute-start(f32[4,72,256]{2,1,0:T(8,128)S(1)} %get-tuple-element.18), channel_id=1, source_target_pairs={{0,1},{1,0},{2,3},{3,2},{4,5},{5,4},{6,7},{7,6},{8,9},{9,8},{10,11... | collective-permute-start | bytes 884744 | tf_op jit(solution)/shard_map/ppermute | solution.py:441
  45.3 6.0 %collective-permute-start.5 = (f32[1,72,256]{2,1,0:T(8,128)S(1)}, f32[1,72,256]{2,1,0:T(8,128)S(1)}, u32[]{:S(2)}, u32[]{:S(2)}) collective-permute-start(f32[1,72,256]{2,1,0:T(8,128)S(1)} %get-tuple-element.25), channel_id=1, source_target_pairs={{0,4},{1,5},{2,6},{3,7},{4,0},{5,1},{6,2},{7,3},{8,12},{9,13},{10,... | collective-permute-start | bytes 221192 | tf_op jit(solution)/shard_map/ppermute | solution.py:448
  47.8 5.9 %collective-permute-start.7 = (f32[1,72,256]{2,1,0:T(8,128)S(1)}, f32[1,72,256]{2,1,0:T(8,128)S(1)}, u32[]{:S(2)}, u32[]{:S(2)}) collective-permute-start(f32[1,72,256]{2,1,0:T(8,128)S(1)} %get-tuple-element.26), channel_id=1, source_target_pairs={{0,6},{1,7},{2,4},{3,5},{4,2},{5,3},{6,0},{7,1},{8,14},{9,15},{10,... | collective-permute-start | bytes 221192 | tf_op jit(solution)/shard_map/ppermute | solution.py:448
  48.9 4.9 %collective-permute-start.6 = (f32[1,72,256]{2,1,0:T(8,128)S(1)}, f32[1,72,256]{2,1,0:T(8,128)S(1)}, u32[]{:S(2)}, u32[]{:S(2)}) collective-permute-start(f32[1,72,256]{2,1,0:T(8,128)S(1)} %get-tuple-element.27), channel_id=1, source_target_pairs={{0,2},{1,3},{2,0},{3,1},{4,6},{5,7},{6,4},{7,5},{8,10},{9,11},{10,... | collective-permute-start | bytes 221192 | tf_op jit(solution)/shard_map/ppermute | solution.py:448
  53.7 4.4 %collective-permute-start.8 = (f32[1,72,256]{2,1,0:T(8,128)S(1)}, f32[1,72,256]{2,1,0:T(8,128)S(1)}, u32[]{:S(2)}, u32[]{:S(2)}) collective-permute-start(f32[1,72,256]{2,1,0:T(8,128)S(1)} %fusion.1), channel_id=1, source_target_pairs={{0,8},{4,12},{8,0},{12,4},{16,24},{20,28},{24,16},{28,20},{1,9},{5... | collective-permute-start | bytes 221192 | tf_op jit(solution)/shard_map/ppermute | solution.py:441
  58.2 6.4 %collective-permute-start.9 = (f32[1,72,256]{2,1,0:T(8,128)S(1)}, f32[1,72,256]{2,1,0:T(8,128)S(1)}, u32[]{:S(2)}, u32[]{:S(2)}) collective-permute-start(f32[1,72,256]{2,1,0:T(8,128)S(1)} %add.22), channel_id=1, source_target_pairs={{0,16},{4,20},{8,24},{12,28},{16,0},{20,4},{24,8},{28,12},{1,17},{... | collective-permute-start | bytes 221192 | tf_op jit(solution)/shard_map/ppermute | solution.py:441
  64.6 5.3 %collective-permute-start.12 = (f32[1,72,256]{2,1,0:T(8,128)S(1)}, f32[1,72,256]{2,1,0:T(8,128)S(1)}, u32[]{:S(2)}, u32[]{:S(2)}) collective-permute-start(f32[1,72,256]{2,1,0:T(8,128)S(1)} %add.23), channel_id=1, source_target_pairs={{0,6},{1,7},{2,4},{3,5},{4,2},{5,3},{6,0},{7,1},{8,14},{9,15},{10,... | collective-permute-start | bytes 221192 | tf_op jit(solution)/shard_map/ppermute | solution.py:448
  66.7 4.4 %collective-permute-start.11 = (f32[1,72,256]{2,1,0:T(8,128)S(1)}, f32[1,72,256]{2,1,0:T(8,128)S(1)}, u32[]{:S(2)}, u32[]{:S(2)}) collective-permute-start(f32[1,72,256]{2,1,0:T(8,128)S(1)} %add.23), channel_id=1, source_target_pairs={{0,2},{1,3},{2,0},{3,1},{4,6},{5,7},{6,4},{7,5},{8,10},{9,11},{10,... | collective-permute-start | bytes 221192 | tf_op jit(solution)/shard_map/ppermute | solution.py:448
  67.6 4.4 %collective-permute-start.10 = (f32[1,72,256]{2,1,0:T(8,128)S(1)}, f32[1,72,256]{2,1,0:T(8,128)S(1)}, u32[]{:S(2)}, u32[]{:S(2)}) collective-permute-start(f32[1,72,256]{2,1,0:T(8,128)S(1)} %add.23), channel_id=1, source_target_pairs={{0,4},{1,5},{2,6},{3,7},{4,0},{5,1},{6,2},{7,3},{8,12},{9,13},{10,... | collective-permute-start | bytes 221192 | tf_op jit(solution)/shard_map/ppermute | solution.py:448
  72.0 1.6 %collective-permute-start.13 = (f32[4,72,256]{2,1,0:T(8,128)S(1)}, f32[4,72,256]{2,1,0:T(8,128)S(1)}, u32[]{:S(2)}, u32[]{:S(2)}) collective-permute-start(f32[4,72,256]{2,1,0:T(8,128)S(1)} %pad_maximum_fusion.low_ref), channel_id=1, source_target_pairs={{0,1},{1,0},{2,3},{3,2},{4,5},{5,4},{6,7},{7,6},{8,9},{9,8},{10,11... | collective-permute-start | bytes 884744 | tf_op jit(solution)/shard_map/ppermute | solution.py:441

commit v9 on v7

--- a/solution.py
+++ b/solution.py
@@ -96,8 +96,8 @@
     field,
     turned,
     left_ref,
+    prev_ref,
     right_ref,
-    prev_ref,
     next_ref,
     tangent_any,
     force_ref,
@@ -251,13 +251,20 @@
                 work[m] = jnp.where(mine, scaled, work[m] - columns[m][j] * scaled)
         for m in range(count):
             done[m].append(jnp.where(lane < first + 8, kept[m], 0.0))
-            pivots = [spread(work[m][j : j + 1, :]) for j in range(8)]
-            for i in range(g + 1, groups):
-                old = rows[m][i]
+            if g + 1 < groups:
+                old = rows[m][g + 1]
                 new = jnp.where(inside, 0.0, old)
                 for j in range(8):
-                    new = new - spread(old[:, first + j : first + j + 1]) * pivots[j]
-                rows[m][i] = new
+                    new = new - spread(old[:, first + j : first + j + 1]) * spread(work[m][j : j + 1, :])
+                rows[m][g + 1] = new
+            if g + 2 < groups:
+                panel = [jnp.zeros((8, size), F32)] * groups
+                panel[g] = work[m]
+                old = jnp.concatenate(rows[m][g + 2 :], 0)
+                wide = jnp.concatenate([inside] * (groups - g - 2), 0)
+                change = matmul(jnp.where(wide, old, 0.0), jnp.concatenate(panel, 0), HIGHEST)
+                new = jnp.where(wide, 0.0, old) - change
+                rows[m][g + 2 :] = [new[8 * i : 8 * i + 8, :] for i in range(groups - g - 2)]
     return [jnp.concatenate(values, 0) for values in done]
 
 
@@ -428,19 +435,24 @@
     return lax.ppermute(value, axis, [(i, i ^ bit) for i in range(count)])
 
 
+def across(value, line_bit, zone_bit):
+    zones = lax.axis_size("zone")
+    count = zones * lax.axis_size("rows")
+    pairs = [(i, (i // zones ^ line_bit) * zones + (i % zones ^ zone_bit)) for i in range(count)]
+    return lax.ppermute(value, ("rows", "zone"), pairs)
+
+
 def reduce_packed(keep, send):
-    core, x, y = ("zone", 1), ("zone", 2), ("rows", 1)
-    value = keep + partner(send, *core)
-    for way in (x, y):
-        half = value.shape[0] // 2
-        value = value[:half] + partner(value[half:], *way)
+    value = keep + partner(send, "zone", 1)
+    ways = ((1, 0), (0, 2), (1, 2))
+    others = [across(value[at + 1 : at + 2], *way) for at, way in enumerate(ways)]
+    value = value[:1] + others[0] + others[1] + others[2]
     for axis, bit in (("rows", 2), ("zone", 4)):
         while bit < lax.axis_size(axis):
             value = value + partner(value, axis, bit)
             bit *= 2
-    for way in (y, x):
-        value = jnp.concatenate([value, partner(value, *way)], 0)
-    return value, partner(value, *core)
+    value = jnp.concatenate([value] + [across(value, *way) for way in ways], 0)
+    return value, partner(value, "zone", 1)
 
 
 def shards(snapshots, tangent, pattern, forcing, step_index):
@@ -456,7 +468,7 @@
     rows_prev = shifted(tail, "rows", 1)
     rows_next = shifted(head, "rows", -1)
     field, turned, gram, load = gram_call(snapshots, force)
-    halos = (from_behind(tail, "zone", 1), from_behind(head, "zone", -1), rows_prev, rows_next)
+    halos = (from_behind(tail, "zone", 1), rows_prev, from_behind(head, "zone", -1), rows_next)
     image, *packed = tangent_call(field, turned, halos, tangent, pattern, force, gram, load, place)
     pieces = reduce_packed(*packed)
     basis, coefficients, residual = final_call(

time: 99.5 us -> 91.8 us (0.923)
  waiting for transfers between devices: 25.8 us -> 21.3 us
  Pallas kernels: 41.4 us -> 38.8 us
    ppermute x8 -> x4, waiting for transfers between devices: 20.7 us -> 8.01 us  [partner(): return lax.ppermute(value, axis, [(i, i ^ bit) for i in range(count)])]
    ppermute x0 -> x6, waiting for transfers between devices: none -> 8.15 us  [across(): return lax.ppermute(value, ('rows', 'zone'), pairs)]
    ppermute x8 -> x4, starting transfers between devices: 13.9 us -> 6.08 us  [partner(): return lax.ppermute(value, axis, [(i, i ^ bit) for i in range(count)])]
    ppermute x0 -> x6, starting transfers between devices: none -> 7.65 us  [across(): return lax.ppermute(value, ('rows', 'zone'), pairs)]
    pallas_call x1, Pallas kernels: 20.3 us -> 17.7 us  [final_call(): pl.pallas_call(functools.partial(final_kernel, inverse_count), out_shape=...]
  transfers between devices with their start and end apart: 12 -> 14, of which waited for: 10 -> 11; matrix products, arithmetic and copies ran while one was open for 1% -> 1% of each run, Pallas kernels for 6% -> 6%
where the time goes in v9:
time: 91.8 us; the launch traced here: 91.5 us
  Pallas kernels  38.8 us (42%)
  starting transfers between devices  24.2 us (26%)
  waiting for transfers between devices  21.3 us (23%)
  local copies, waits for them, and re-layouts  6.22 us (7%)
    pallas_call x1, Pallas kernels, final_call(): pl.pallas_call(functools.partial(final_kernel, inverse_count), out_shape=...  17.7 us
    pallas_call x1, Pallas kernels, tangent_call(): pl.pallas_call(tangent_kernel, out_shape=(jax.ShapeDtypeStruct((rows, sna...  15.3 us
    ppermute x6, waiting for transfers between devices, across(): return lax.ppermute(value, ('rows', 'zone'), pairs)  8.15 us
    ppermute x4, waiting for transfers between devices, partner(): return lax.ppermute(value, axis, [(i, i ^ bit) for i in range(count)])  8.01 us
    ppermute x6, starting transfers between devices, across(): return lax.ppermute(value, ('rows', 'zone'), pairs)  7.65 us
    ppermute x2, starting transfers between devices, shifted(): return lax.ppermute(value, axis, pairs)  6.12 us
    ppermute x4, starting transfers between devices, partner(): return lax.ppermute(value, axis, [(i, i ^ bit) for i in range(count)])  6.08 us
    pallas_call x1, Pallas kernels, gram_call(): pl.pallas_call(gram_kernel, out_shape=(jax.ShapeDtypeStruct((rows, 2 * sn...  5.78 us
  transfers between devices with their start and end apart: 14, of which 11 were waited for; matrix products, arithmetic and copies ran while one was open for 1% of the time, Pallas kernels for 6%

profile of v9, /device:TPU:0, one launch (start us, length us, event | category | flops | bytes accessed | tf_op | source)
XLA Modules:
  0.0 91.5 jit_solution(8612217811842345445)
XLA Ops:
  0.6 1.3 %fusion.2 = (f32[512,256]{1,0:T(8,128)S(1)}, f32[512,256]{1,0:T(8,128)S(1)}) fusion(f32[8192,256]{1,0:T(8,128)} %snap.1), kind=kLoop, calls=%fused_computation.4 | loop fusion | bytes 2097152 | tf_op jit(solution)/shard_map/slice | solution.py:467
  1.9 6.1 %collective-permute-start.3 = (f32[512,256]{1,0:T(8,128)S(1)}, f32[512,256]{1,0:T(8,128)S(1)}, u32[]{:S(2)}, u32[]{:S(2)}) collective-permute-start(f32[512,256]{1,0:T(8,128)S(1)} %get-tuple-element.23), channel_id=1, source_target_pairs={{0,28},{4,0},{8,4},{12,8},{16,12},{20,16},{24,20},{28,24},{1,29},{... | collective-permute-start | bytes 1572872 | tf_op jit(solution)/shard_map/ppermute | solution.py:424
  8.0 1.3 %collective-permute-start.2 = (f32[512,256]{1,0:T(8,128)S(1)}, f32[512,256]{1,0:T(8,128)S(1)}, u32[]{:S(2)}, u32[]{:S(2)}) collective-permute-start(f32[512,256]{1,0:T(8,128)S(1)} %get-tuple-element.23), channel_id=1, source_target_pairs={{1,0},{2,1},{3,2},{5,4},{6,5},{7,6},{9,8},{10,9},{11,10},{13,12},{... | collective-permute-start | bytes 1572872 | tf_op jit(solution)/shard_map/ppermute | solution.py:430
  9.2 0.1 collective-permute-start.1
  9.3 3.1 %collective-permute-start = (f32[512,256]{1,0:T(8,128)S(1)}, f32[512,256]{1,0:T(8,128)S(1)}, u32[]{:S(2)}, u32[]{:S(2)}) collective-permute-start(f32[512,256]{1,0:T(8,128)S(1)} %get-tuple-element.24), channel_id=1, source_target_pairs={{0,1},{1,2},{2,3},{4,5},{5,6},{6,7},{8,9},{9,10},{10,11},{12,13},{... | collective-permute-start | bytes 1572872 | tf_op jit(solution)/shard_map/ppermute | solution.py:430
  12.4 0.8 copy.8.pattern_ref
  13.2 3.4 %copy-done = f32[8192,256]{1,0:T(8,128)S(1)} copy-done((f32[8192,256]{1,0:T(8,128)S(1)}, f32[8192,256]{1,0:T(8,128)}, u32[]{:S(2)}) %copy-start) | copy-done | bytes 8388632
  16.5 0.8 copy-done.2
  17.3 5.8 %gram.1 = (bf16[8192,512]{1,0:T(8,128)(2,1)S(1)}, bf16[8,512,1024]{2,1,0:T(8,128)(2,1)S(1)}, f32[256,512]{1,0:T(8,128)S(1)}, f32[1,256]{1,0:T(1,128)S(1)}) custom-call(f32[8192,256]{1,0:T(8,128)S(1)} %copy-done, f32[64,128]{1,0:T(8,128)S(1)} %bitcast.6), custom_call_target="tpu_custom_call" | custom-call | flops 2147483648 | bytes 8388608 | tf_op jit(solution)/shard_map/gram/pallas_call | solution.py:75
  23.1 5.0 %collective-permute-done.3.next_ref = f32[512,256]{1,0:T(8,128)S(1)} collective-permute-done((f32[512,256]{1,0:T(8,128)S(1)}, f32[512,256]{1,0:T(8,128)S(1)}, u32[]{:S(2)}, u32[]{:S(2)}) %collective-permute-start.3) | collective-permute-done | bytes 524320 | tf_op jit(solution)/shard_map/ppermute | solution.py:424
  28.1 0.1 collective-permute-done.1.prev_ref
  28.2 15.3 %tangent.1 = (f32[8192,256]{1,0:T(8,128)S(1)}, f32[4,72,256]{2,1,0:T(8,128)S(1)}, f32[4,72,256]{2,1,0:T(8,128)S(1)}) custom-call(s32[64,4]{1,0:T(8,128)S(1)} %copy.8.pattern_ref, s32[1]{0:T(128)} %bitcast.place_ref, bf16[8192,512]{1,0:T(8,128)(2,1)S(1)} %get-tuple-element.13.field, bf16[8,512,1024]{2,1,0:T(8,128)(2,1)S(1)} %get-tuple-element.14.turned, ...), custom_call_target="tpu_custom_call" | custom-call | tf_op jit(solution)/shard_map/tangent/pallas_call | solution.py:201
  43.5 0.3 collective-permute-start.4
  43.8 1.4 %collective-permute-done.4 = f32[4,72,256]{2,1,0:T(8,128)S(1)} collective-permute-done((f32[4,72,256]{2,1,0:T(8,128)S(1)}, f32[4,72,256]{2,1,0:T(8,128)S(1)}, u32[]{:S(2)}, u32[]{:S(2)}) %collective-permute-start.4) | collective-permute-done | bytes 294944 | tf_op jit(solution)/shard_map/ppermute | solution.py:435
  45.3 2.6 %collective-permute-start.5 = (f32[1,72,256]{2,1,0:T(8,128)S(1)}, f32[1,72,256]{2,1,0:T(8,128)S(1)}, u32[]{:S(2)}, u32[]{:S(2)}) collective-permute-start(f32[1,72,256]{2,1,0:T(8,128)S(1)} %get-tuple-element.25), channel_id=1, source_target_pairs={{0,4},{1,5},{2,6},{3,7},{4,0},{5,1},{6,2},{7,3},{8,12},{9,13},{10,... | collective-permute-start | bytes 221192 | tf_op jit(solution)/shard_map/ppermute | solution.py:442
  47.8 1.0 %collective-permute-start.7 = (f32[1,72,256]{2,1,0:T(8,128)S(1)}, f32[1,72,256]{2,1,0:T(8,128)S(1)}, u32[]{:S(2)}, u32[]{:S(2)}) collective-permute-start(f32[1,72,256]{2,1,0:T(8,128)S(1)} %get-tuple-element.26), channel_id=1, source_target_pairs={{0,6},{1,7},{2,4},{3,5},{4,2},{5,3},{6,0},{7,1},{8,14},{9,15},{10,... | collective-permute-start | bytes 221192 | tf_op jit(solution)/shard_map/ppermute | solution.py:442
  48.9 0.5 collective-permute-start.6
  49.4 1.9 %collective-permute-done.5 = f32[1,72,256]{2,1,0:T(8,128)S(1)} collective-permute-done((f32[1,72,256]{2,1,0:T(8,128)S(1)}, f32[1,72,256]{2,1,0:T(8,128)S(1)}, u32[]{:S(2)}, u32[]{:S(2)}) %collective-permute-start.5) | collective-permute-done | bytes 73760 | tf_op jit(solution)/shard_map/ppermute | solution.py:442
  51.3 2.5 %collective-permute-done.7 = f32[1,72,256]{2,1,0:T(8,128)S(1)} collective-permute-done((f32[1,72,256]{2,1,0:T(8,128)S(1)}, f32[1,72,256]{2,1,0:T(8,128)S(1)}, u32[]{:S(2)}, u32[]{:S(2)}) %collective-permute-start.7) | collective-permute-done | bytes 73760 | tf_op jit(solution)/shard_map/ppermute | solution.py:442
  53.7 1.7 %collective-permute-start.8 = (f32[1,72,256]{2,1,0:T(8,128)S(1)}, f32[1,72,256]{2,1,0:T(8,128)S(1)}, u32[]{:S(2)}, u32[]{:S(2)}) collective-permute-start(f32[1,72,256]{2,1,0:T(8,128)S(1)} %fusion.1), channel_id=1, source_target_pairs={{0,8},{4,12},{8,0},{12,4},{16,24},{20,28},{24,16},{28,20},{1,9},{5... | collective-permute-start | bytes 221192 | tf_op jit(solution)/shard_map/ppermute | solution.py:435
  55.4 2.7 %collective-permute-done.8 = f32[1,72,256]{2,1,0:T(8,128)S(1)} collective-permute-done((f32[1,72,256]{2,1,0:T(8,128)S(1)}, f32[1,72,256]{2,1,0:T(8,128)S(1)}, u32[]{:S(2)}, u32[]{:S(2)}) %collective-permute-start.8) | collective-permute-done | bytes 73760 | tf_op jit(solution)/shard_map/ppermute | solution.py:435
  58.2 4.1 %collective-permute-start.9 = (f32[1,72,256]{2,1,0:T(8,128)S(1)}, f32[1,72,256]{2,1,0:T(8,128)S(1)}, u32[]{:S(2)}, u32[]{:S(2)}) collective-permute-start(f32[1,72,256]{2,1,0:T(8,128)S(1)} %add.22), channel_id=1, source_target_pairs={{0,16},{4,20},{8,24},{12,28},{16,0},{20,4},{24,8},{28,12},{1,17},{... | collective-permute-start | bytes 221192 | tf_op jit(solution)/shard_map/ppermute | solution.py:435
  62.2 2.3 %collective-permute-done.9 = f32[1,72,256]{2,1,0:T(8,128)S(1)} collective-permute-done((f32[1,72,256]{2,1,0:T(8,128)S(1)}, f32[1,72,256]{2,1,0:T(8,128)S(1)}, u32[]{:S(2)}, u32[]{:S(2)}) %collective-permute-start.9) | collective-permute-done | bytes 73760 | tf_op jit(solution)/shard_map/ppermute | solution.py:435
  64.6 2.1 %collective-permute-start.12 = (f32[1,72,256]{2,1,0:T(8,128)S(1)}, f32[1,72,256]{2,1,0:T(8,128)S(1)}, u32[]{:S(2)}, u32[]{:S(2)}) collective-permute-start(f32[1,72,256]{2,1,0:T(8,128)S(1)} %add.23), channel_id=1, source_target_pairs={{0,6},{1,7},{2,4},{3,5},{4,2},{5,3},{6,0},{7,1},{8,14},{9,15},{10,... | collective-permute-start | bytes 221192 | tf_op jit(solution)/shard_map/ppermute | solution.py:442
  66.7 0.8 collective-permute-start.11
  67.6 0.6 collective-permute-start.10
  68.1 1.8 %collective-permute-done.12 = f32[1,72,256]{2,1,0:T(8,128)S(1)} collective-permute-done((f32[1,72,256]{2,1,0:T(8,128)S(1)}, f32[1,72,256]{2,1,0:T(8,128)S(1)}, u32[]{:S(2)}, u32[]{:S(2)}) %collective-permute-start.12) | collective-permute-done | bytes 73760 | tf_op jit(solution)/shard_map/ppermute | solution.py:442
  69.9 1.2 %collective-permute-done.11 = f32[1,72,256]{2,1,0:T(8,128)S(1)} collective-permute-done((f32[1,72,256]{2,1,0:T(8,128)S(1)}, f32[1,72,256]{2,1,0:T(8,128)S(1)}, u32[]{:S(2)}, u32[]{:S(2)}) %collective-permute-start.11) | collective-permute-done | bytes 73760 | tf_op jit(solution)/shard_map/ppermute | solution.py:442
  71.1 0.8 collective-permute-done.10
  72.0 0.1 collective-permute-start.13
  72.0 1.6 %collective-permute-done.13.high_ref = f32[4,72,256]{2,1,0:T(8,128)S(1)} collective-permute-done((f32[4,72,256]{2,1,0:T(8,128)S(1)}, f32[4,72,256]{2,1,0:T(8,128)S(1)}, u32[]{:S(2)}, u32[]{:S(2)}) %collective-permute-start.13) | collective-permute-done | bytes 294944 | tf_op jit(solution)/shard_map/ppermute | solution.py:435
  73.6 17.7 %final.1 = (f32[8192,256]{1,0:T(8,128)}, f32[3,256]{1,0:T(4,128)}, f32[64,128]{1,0:T(8,128)}) custom-call(s32[1]{0:T(128)} %bitcast.place_ref, f32[4,72,256]{2,1,0:T(8,128)S(1)} %pad_maximum_fusion.low_ref, f32[4,72,256]{2,1,0:T(8,128)S(1)} %collective-permute-done.13.high_ref, s32[1,256]{1,0:T(1,128)S(1)} %bitcast.9, f32[64,128]{1,0:T(8,128)S(1)} %bitcast.8, ...), custom_call_target="tpu_custom_call" | custom-call | tf_op jit(solution)/shard_map/final/pallas_call | solution.py:398
  (20 shorter events, 0.2 us)
Async XLA Ops:
  1.9 26.2 %collective-permute-start.3 = (f32[512,256]{1,0:T(8,128)S(1)}, f32[512,256]{1,0:T(8,128)S(1)}, u32[]{:S(2)}, u32[]{:S(2)}) collective-permute-start(f32[512,256]{1,0:T(8,128)S(1)} %get-tuple-element.23), channel_id=1, source_target_pairs={{0,28},{4,0},{8,4},{12,8},{16,12},{20,16},{24,20},{28,24},{1,29},{... | collective-permute-start | bytes 1572872 | tf_op jit(solution)/shard_map/ppermute | solution.py:424
  8.0 20.1 %collective-permute-start.2 = (f32[512,256]{1,0:T(8,128)S(1)}, f32[512,256]{1,0:T(8,128)S(1)}, u32[]{:S(2)}, u32[]{:S(2)}) collective-permute-start(f32[512,256]{1,0:T(8,128)S(1)} %get-tuple-element.23), channel_id=1, source_target_pairs={{1,0},{2,1},{3,2},{5,4},{6,5},{7,6},{9,8},{10,9},{11,10},{13,12},{... | collective-permute-start | bytes 1572872 | tf_op jit(solution)/shard_map/ppermute | solution.py:430
  9.2 19.0 %collective-permute-start.1 = (f32[512,256]{1,0:T(8,128)S(1)}, f32[512,256]{1,0:T(8,128)S(1)}, u32[]{:S(2)}, u32[]{:S(2)}) collective-permute-start(f32[512,256]{1,0:T(8,128)S(1)} %get-tuple-element.24), channel_id=1, source_target_pairs={{0,4},{4,8},{8,12},{12,16},{16,20},{20,24},{24,28},{28,0},{1,5},{5... | collective-permute-start | bytes 1572872 | tf_op jit(solution)/shard_map/ppermute | solution.py:424
  9.3 18.9 %collective-permute-start = (f32[512,256]{1,0:T(8,128)S(1)}, f32[512,256]{1,0:T(8,128)S(1)}, u32[]{:S(2)}, u32[]{:S(2)}) collective-permute-start(f32[512,256]{1,0:T(8,128)S(1)} %get-tuple-element.24), channel_id=1, source_target_pairs={{0,1},{1,2},{2,3},{4,5},{5,6},{6,7},{8,9},{9,10},{10,11},{12,13},{... | collective-permute-start | bytes 1572872 | tf_op jit(solution)/shard_map/ppermute | solution.py:430
  13.2 3.4 %copy-start = (f32[8192,256]{1,0:T(8,128)S(1)}, f32[8192,256]{1,0:T(8,128)}, u32[]{:S(2)}) copy-start(f32[8192,256]{1,0:T(8,128)} %snap.1) | copy-start | bytes 25165828
  16.5 0.8 copy-start.2
  17.3 10.9 %copy-start.1 = (bf16[8192,512]{1,0:T(8,128)(2,1)S(1)}, bf16[8192,512]{1,0:T(8,128)(2,1)}, u32[]{:S(2)}) copy-start(bf16[8192,512]{1,0:T(8,128)(2,1)} %tangent_any.1) | copy-start | bytes 25165828
  28.2 45.4 %slice-start = ((s8[8388608]{0:T(1024)(128)(4,1)}), s8[4194304]{0:T(1024)(128)(4,1)S(1)}, s32[]{:S(2)}) async-start(s8[8388608]{0:T(1024)(128)(4,1)} %bitcast.4), calls=%async_computation | async-start | bytes 8388608
  28.2 45.4 %slice-start.1 = ((s8[8388608]{0:T(1024)(128)(4,1)}), s8[4194304]{0:T(1024)(128)(4,1)S(1)}, s32[]{:S(2)}) async-start(s8[8388608]{0:T(1024)(128)(4,1)} %bitcast.4), calls=%async_computation.1 | async-start | bytes 8388608
  28.2 45.4 %copy-start.3 = (s32[256]{0:T(256)S(1)}, s32[256]{0:T(256)}, u32[]{:S(2)}) copy-start(s32[256]{0:T(256)} %param.9) | copy-start | bytes 3076
  43.5 1.6 %collective-permute-start.4 = (f32[4,72,256]{2,1,0:T(8,128)S(1)}, f32[4,72,256]{2,1,0:T(8,128)S(1)}, u32[]{:S(2)}, u32[]{:S(2)}) collective-permute-start(f32[4,72,256]{2,1,0:T(8,128)S(1)} %get-tuple-element.18), channel_id=1, source_target_pairs={{0,1},{1,0},{2,3},{3,2},{4,5},{5,4},{6,7},{7,6},{8,9},{9,8},{10,11... | collective-permute-start | bytes 884744 | tf_op jit(solution)/shard_map/ppermute | solution.py:435
  45.3 6.0 %collective-permute-start.5 = (f32[1,72,256]{2,1,0:T(8,128)S(1)}, f32[1,72,256]{2,1,0:T(8,128)S(1)}, u32[]{:S(2)}, u32[]{:S(2)}) collective-permute-start(f32[1,72,256]{2,1,0:T(8,128)S(1)} %get-tuple-element.25), channel_id=1, source_target_pairs={{0,4},{1,5},{2,6},{3,7},{4,0},{5,1},{6,2},{7,3},{8,12},{9,13},{10,... | collective-permute-start | bytes 221192 | tf_op jit(solution)/shard_map/ppermute | solution.py:442
  47.8 5.9 %collective-permute-start.7 = (f32[1,72,256]{2,1,0:T(8,128)S(1)}, f32[1,72,256]{2,1,0:T(8,128)S(1)}, u32[]{:S(2)}, u32[]{:S(2)}) collective-permute-start(f32[1,72,256]{2,1,0:T(8,128)S(1)} %get-tuple-element.26), channel_id=1, source_target_pairs={{0,6},{1,7},{2,4},{3,5},{4,2},{5,3},{6,0},{7,1},{8,14},{9,15},{10,... | collective-permute-start | bytes 221192 | tf_op jit(solution)/shard_map/ppermute | solution.py:442
  48.9 4.9 %collective-permute-start.6 = (f32[1,72,256]{2,1,0:T(8,128)S(1)}, f32[1,72,256]{2,1,0:T(8,128)S(1)}, u32[]{:S(2)}, u32[]{:S(2)}) collective-permute-start(f32[1,72,256]{2,1,0:T(8,128)S(1)} %get-tuple-element.27), channel_id=1, source_target_pairs={{0,2},{1,3},{2,0},{3,1},{4,6},{5,7},{6,4},{7,5},{8,10},{9,11},{10,... | collective-permute-start | bytes 221192 | tf_op jit(solution)/shard_map/ppermute | solution.py:442
  53.7 4.4 %collective-permute-start.8 = (f32[1,72,256]{2,1,0:T(8,128)S(1)}, f32[1,72,256]{2,1,0:T(8,128)S(1)}, u32[]{:S(2)}, u32[]{:S(2)}) collective-permute-start(f32[1,72,256]{2,1,0:T(8,128)S(1)} %fusion.1), channel_id=1, source_target_pairs={{0,8},{4,12},{8,0},{12,4},{16,24},{20,28},{24,16},{28,20},{1,9},{5... | collective-permute-start | bytes 221192 | tf_op jit(solution)/shard_map/ppermute | solution.py:435
  58.2 6.4 %collective-permute-start.9 = (f32[1,72,256]{2,1,0:T(8,128)S(1)}, f32[1,72,256]{2,1,0:T(8,128)S(1)}, u32[]{:S(2)}, u32[]{:S(2)}) collective-permute-start(f32[1,72,256]{2,1,0:T(8,128)S(1)} %add.22), channel_id=1, source_target_pairs={{0,16},{4,20},{8,24},{12,28},{16,0},{20,4},{24,8},{28,12},{1,17},{... | collective-permute-start | bytes 221192 | tf_op jit(solution)/shard_map/ppermute | solution.py:435
  64.6 5.3 %collective-permute-start.12 = (f32[1,72,256]{2,1,0:T(8,128)S(1)}, f32[1,72,256]{2,1,0:T(8,128)S(1)}, u32[]{:S(2)}, u32[]{:S(2)}) collective-permute-start(f32[1,72,256]{2,1,0:T(8,128)S(1)} %add.23), channel_id=1, source_target_pairs={{0,6},{1,7},{2,4},{3,5},{4,2},{5,3},{6,0},{7,1},{8,14},{9,15},{10,... | collective-permute-start | bytes 221192 | tf_op jit(solution)/shard_map/ppermute | solution.py:442
  66.7 4.4 %collective-permute-start.11 = (f32[1,72,256]{2,1,0:T(8,128)S(1)}, f32[1,72,256]{2,1,0:T(8,128)S(1)}, u32[]{:S(2)}, u32[]{:S(2)}) collective-permute-start(f32[1,72,256]{2,1,0:T(8,128)S(1)} %add.23), channel_id=1, source_target_pairs={{0,2},{1,3},{2,0},{3,1},{4,6},{5,7},{6,4},{7,5},{8,10},{9,11},{10,... | collective-permute-start | bytes 221192 | tf_op jit(solution)/shard_map/ppermute | solution.py:442
  67.6 4.4 %collective-permute-start.10 = (f32[1,72,256]{2,1,0:T(8,128)S(1)}, f32[1,72,256]{2,1,0:T(8,128)S(1)}, u32[]{:S(2)}, u32[]{:S(2)}) collective-permute-start(f32[1,72,256]{2,1,0:T(8,128)S(1)} %add.23), channel_id=1, source_target_pairs={{0,4},{1,5},{2,6},{3,7},{4,0},{5,1},{6,2},{7,3},{8,12},{9,13},{10,... | collective-permute-start | bytes 221192 | tf_op jit(solution)/shard_map/ppermute | solution.py:442
  72.0 1.6 %collective-permute-start.13 = (f32[4,72,256]{2,1,0:T(8,128)S(1)}, f32[4,72,256]{2,1,0:T(8,128)S(1)}, u32[]{:S(2)}, u32[]{:S(2)}) collective-permute-start(f32[4,72,256]{2,1,0:T(8,128)S(1)} %pad_maximum_fusion.low_ref), channel_id=1, source_target_pairs={{0,1},{1,0},{2,3},{3,2},{4,5},{5,4},{6,7},{7,6},{8,9},{9,8},{10,11... | collective-permute-start | bytes 884744 | tf_op jit(solution)/shard_map/ppermute | solution.py:435

commit v10 on v8

--- a/solution.py
+++ b/solution.py
@@ -96,8 +96,8 @@
     field,
     turned,
     left_ref,
+    prev_ref,
     right_ref,
-    prev_ref,
     next_ref,
     tangent_any,
     force_ref,
@@ -264,13 +264,20 @@
                 kept[m] = jnp.where(mine, row * root, kept[m])
         for m in range(count):
             done[m].append(jnp.where(lane < first + 8, kept[m], 0.0))
-            solved = [spread(work[m][j : j + 1, :]) for j in range(8)]
-            for i in range(g + 1, groups):
-                old = rows[m][i]
-                terms = [spread(old[:, first + j : first + j + 1]) * solved[j] for j in range(8)]
-                while len(terms) > 1:
-                    terms = [a + b for a, b in zip(terms[::2], terms[1::2])]
-                rows[m][i] = jnp.where(inside, 0.0, old) - terms[0]
+            if g + 1 < groups:
+                old = rows[m][g + 1]
+                new = jnp.where(inside, 0.0, old)
+                for j in range(8):
+                    new = new - spread(old[:, first + j : first + j + 1]) * spread(work[m][j : j + 1, :])
+                rows[m][g + 1] = new
+            if g + 2 < groups:
+                panel = [jnp.zeros((8, size), F32)] * groups
+                panel[g] = work[m]
+                old = jnp.concatenate(rows[m][g + 2 :], 0)
+                wide = jnp.concatenate([inside] * (groups - g - 2), 0)
+                change = matmul(jnp.where(wide, old, 0.0), jnp.concatenate(panel, 0), HIGHEST)
+                new = jnp.where(wide, 0.0, old) - change
+                rows[m][g + 2 :] = [new[8 * i : 8 * i + 8, :] for i in range(groups - g - 2)]
     return [jnp.concatenate(values, 0) for values in done]
 
 
@@ -474,7 +481,7 @@
     rows_prev = shifted(tail, "rows", 1)
     rows_next = shifted(head, "rows", -1)
     field, turned, gram, load = gram_call(snapshots, force)
-    halos = (from_behind(tail, "zone", 1), from_behind(head, "zone", -1), rows_prev, rows_next)
+    halos = (from_behind(tail, "zone", 1), rows_prev, from_behind(head, "zone", -1), rows_next)
     image, *packed = tangent_call(field, turned, halos, tangent, pattern, force, gram, load, place)
     pieces = reduce_packed(*packed)
     basis, coefficients, residual = final_call(

time: 95.2 us -> 92.6 us (0.973)
  Pallas kernels: 42.2 us -> 39.6 us
    pallas_call x1, Pallas kernels: 21.1 us -> 18.5 us  [final_call(): pl.pallas_call(functools.partial(final_kernel, inverse_count), out_shape=...]
where the time goes in v10:
time: 92.6 us; the launch traced here: 92.3 us
  Pallas kernels  39.6 us (43%)
  starting transfers between devices  24.2 us (26%)
  waiting for transfers between devices  21.3 us (23%)
  local copies, waits for them, and re-layouts  6.22 us (7%)
    pallas_call x1, Pallas kernels, final_call(): pl.pallas_call(functools.partial(final_kernel, inverse_count), out_shape=...  18.5 us
    pallas_call x1, Pallas kernels, tangent_call(): pl.pallas_call(tangent_kernel, out_shape=(jax.ShapeDtypeStruct((rows, sna...  15.3 us
    ppermute x6, waiting for transfers between devices, across(): return lax.ppermute(value, ('rows', 'zone'), pairs)  8.15 us
    ppermute x4, waiting for transfers between devices, partner(): return lax.ppermute(value, axis, [(i, i ^ bit) for i in range(count)])  8.01 us
    ppermute x6, starting transfers between devices, across(): return lax.ppermute(value, ('rows', 'zone'), pairs)  7.65 us
    ppermute x2, starting transfers between devices, shifted(): return lax.ppermute(value, axis, pairs)  6.12 us
    ppermute x4, starting transfers between devices, partner(): return lax.ppermute(value, axis, [(i, i ^ bit) for i in range(count)])  6.08 us
    pallas_call x1, Pallas kernels, gram_call(): pl.pallas_call(gram_kernel, out_shape=(jax.ShapeDtypeStruct((rows, 2 * sn...  5.78 us
  transfers between devices with their start and end apart: 14, of which 11 were waited for; matrix products, arithmetic and copies ran while one was open for 1% of the time, Pallas kernels for 6%

profile of v10, /device:TPU:0, one launch (start us, length us, event | category | flops | bytes accessed | tf_op | source)
XLA Modules:
  0.0 92.3 jit_solution(12219126189412009832)
XLA Ops:
  0.6 1.3 %fusion.2 = (f32[512,256]{1,0:T(8,128)S(1)}, f32[512,256]{1,0:T(8,128)S(1)}) fusion(f32[8192,256]{1,0:T(8,128)} %snap.1), kind=kLoop, calls=%fused_computation.4 | loop fusion | bytes 2097152 | tf_op jit(solution)/shard_map/slice | solution.py:480
  1.9 6.1 %collective-permute-start.3 = (f32[512,256]{1,0:T(8,128)S(1)}, f32[512,256]{1,0:T(8,128)S(1)}, u32[]{:S(2)}, u32[]{:S(2)}) collective-permute-start(f32[512,256]{1,0:T(8,128)S(1)} %get-tuple-element.23), channel_id=1, source_target_pairs={{0,28},{4,0},{8,4},{12,8},{16,12},{20,16},{24,20},{28,24},{1,29},{... | collective-permute-start | bytes 1572872 | tf_op jit(solution)/shard_map/ppermute | solution.py:437
  8.0 1.3 %collective-permute-start.2 = (f32[512,256]{1,0:T(8,128)S(1)}, f32[512,256]{1,0:T(8,128)S(1)}, u32[]{:S(2)}, u32[]{:S(2)}) collective-permute-start(f32[512,256]{1,0:T(8,128)S(1)} %get-tuple-element.23), channel_id=1, source_target_pairs={{1,0},{2,1},{3,2},{5,4},{6,5},{7,6},{9,8},{10,9},{11,10},{13,12},{... | collective-permute-start | bytes 1572872 | tf_op jit(solution)/shard_map/ppermute | solution.py:443
  9.2 0.1 collective-permute-start.1
  9.3 3.1 %collective-permute-start = (f32[512,256]{1,0:T(8,128)S(1)}, f32[512,256]{1,0:T(8,128)S(1)}, u32[]{:S(2)}, u32[]{:S(2)}) collective-permute-start(f32[512,256]{1,0:T(8,128)S(1)} %get-tuple-element.24), channel_id=1, source_target_pairs={{0,1},{1,2},{2,3},{4,5},{5,6},{6,7},{8,9},{9,10},{10,11},{12,13},{... | collective-permute-start | bytes 1572872 | tf_op jit(solution)/shard_map/ppermute | solution.py:443
  12.4 0.8 copy.8.pattern_ref
  13.2 3.4 %copy-done = f32[8192,256]{1,0:T(8,128)S(1)} copy-done((f32[8192,256]{1,0:T(8,128)S(1)}, f32[8192,256]{1,0:T(8,128)}, u32[]{:S(2)}) %copy-start) | copy-done | bytes 8388632
  16.5 0.8 copy-done.2
  17.3 5.8 %gram.1 = (bf16[8192,512]{1,0:T(8,128)(2,1)S(1)}, bf16[8,512,1024]{2,1,0:T(8,128)(2,1)S(1)}, f32[256,512]{1,0:T(8,128)S(1)}, f32[1,256]{1,0:T(1,128)S(1)}) custom-call(f32[8192,256]{1,0:T(8,128)S(1)} %copy-done, f32[64,128]{1,0:T(8,128)S(1)} %bitcast.6), custom_call_target="tpu_custom_call" | custom-call | flops 2147483648 | bytes 8388608 | tf_op jit(solution)/shard_map/gram/pallas_call | solution.py:75
  23.1 5.0 %collective-permute-done.3.next_ref = f32[512,256]{1,0:T(8,128)S(1)} collective-permute-done((f32[512,256]{1,0:T(8,128)S(1)}, f32[512,256]{1,0:T(8,128)S(1)}, u32[]{:S(2)}, u32[]{:S(2)}) %collective-permute-start.3) | collective-permute-done | bytes 524320 | tf_op jit(solution)/shard_map/ppermute | solution.py:437
  28.1 0.1 collective-permute-done.1.prev_ref
  28.2 15.3 %tangent.1 = (f32[8192,256]{1,0:T(8,128)S(1)}, f32[4,72,256]{2,1,0:T(8,128)S(1)}, f32[4,72,256]{2,1,0:T(8,128)S(1)}) custom-call(s32[64,4]{1,0:T(8,128)S(1)} %copy.8.pattern_ref, s32[1]{0:T(128)} %bitcast.place_ref, bf16[8192,512]{1,0:T(8,128)(2,1)S(1)} %get-tuple-element.13.field, bf16[8,512,1024]{2,1,0:T(8,128)(2,1)S(1)} %get-tuple-element.14.turned, ...), custom_call_target="tpu_custom_call" | custom-call | tf_op jit(solution)/shard_map/tangent/pallas_call | solution.py:201
  43.5 0.3 collective-permute-start.4
  43.8 1.4 %collective-permute-done.4 = f32[4,72,256]{2,1,0:T(8,128)S(1)} collective-permute-done((f32[4,72,256]{2,1,0:T(8,128)S(1)}, f32[4,72,256]{2,1,0:T(8,128)S(1)}, u32[]{:S(2)}, u32[]{:S(2)}) %collective-permute-start.4) | collective-permute-done | bytes 294944 | tf_op jit(solution)/shard_map/ppermute | solution.py:448
  45.3 2.6 %collective-permute-start.5 = (f32[1,72,256]{2,1,0:T(8,128)S(1)}, f32[1,72,256]{2,1,0:T(8,128)S(1)}, u32[]{:S(2)}, u32[]{:S(2)}) collective-permute-start(f32[1,72,256]{2,1,0:T(8,128)S(1)} %get-tuple-element.25), channel_id=1, source_target_pairs={{0,4},{1,5},{2,6},{3,7},{4,0},{5,1},{6,2},{7,3},{8,12},{9,13},{10,... | collective-permute-start | bytes 221192 | tf_op jit(solution)/shard_map/ppermute | solution.py:455
  47.8 1.0 %collective-permute-start.7 = (f32[1,72,256]{2,1,0:T(8,128)S(1)}, f32[1,72,256]{2,1,0:T(8,128)S(1)}, u32[]{:S(2)}, u32[]{:S(2)}) collective-permute-start(f32[1,72,256]{2,1,0:T(8,128)S(1)} %get-tuple-element.26), channel_id=1, source_target_pairs={{0,6},{1,7},{2,4},{3,5},{4,2},{5,3},{6,0},{7,1},{8,14},{9,15},{10,... | collective-permute-start | bytes 221192 | tf_op jit(solution)/shard_map/ppermute | solution.py:455
  48.9 0.5 collective-permute-start.6
  49.4 1.9 %collective-permute-done.5 = f32[1,72,256]{2,1,0:T(8,128)S(1)} collective-permute-done((f32[1,72,256]{2,1,0:T(8,128)S(1)}, f32[1,72,256]{2,1,0:T(8,128)S(1)}, u32[]{:S(2)}, u32[]{:S(2)}) %collective-permute-start.5) | collective-permute-done | bytes 73760 | tf_op jit(solution)/shard_map/ppermute | solution.py:455
  51.3 2.5 %collective-permute-done.7 = f32[1,72,256]{2,1,0:T(8,128)S(1)} collective-permute-done((f32[1,72,256]{2,1,0:T(8,128)S(1)}, f32[1,72,256]{2,1,0:T(8,128)S(1)}, u32[]{:S(2)}, u32[]{:S(2)}) %collective-permute-start.7) | collective-permute-done | bytes 73760 | tf_op jit(solution)/shard_map/ppermute | solution.py:455
  53.7 1.7 %collective-permute-start.8 = (f32[1,72,256]{2,1,0:T(8,128)S(1)}, f32[1,72,256]{2,1,0:T(8,128)S(1)}, u32[]{:S(2)}, u32[]{:S(2)}) collective-permute-start(f32[1,72,256]{2,1,0:T(8,128)S(1)} %fusion.1), channel_id=1, source_target_pairs={{0,8},{4,12},{8,0},{12,4},{16,24},{20,28},{24,16},{28,20},{1,9},{5... | collective-permute-start | bytes 221192 | tf_op jit(solution)/shard_map/ppermute | solution.py:448
  55.4 2.7 %collective-permute-done.8 = f32[1,72,256]{2,1,0:T(8,128)S(1)} collective-permute-done((f32[1,72,256]{2,1,0:T(8,128)S(1)}, f32[1,72,256]{2,1,0:T(8,128)S(1)}, u32[]{:S(2)}, u32[]{:S(2)}) %collective-permute-start.8) | collective-permute-done | bytes 73760 | tf_op jit(solution)/shard_map/ppermute | solution.py:448
  58.2 4.1 %collective-permute-start.9 = (f32[1,72,256]{2,1,0:T(8,128)S(1)}, f32[1,72,256]{2,1,0:T(8,128)S(1)}, u32[]{:S(2)}, u32[]{:S(2)}) collective-permute-start(f32[1,72,256]{2,1,0:T(8,128)S(1)} %add.22), channel_id=1, source_target_pairs={{0,16},{4,20},{8,24},{12,28},{16,0},{20,4},{24,8},{28,12},{1,17},{... | collective-permute-start | bytes 221192 | tf_op jit(solution)/shard_map/ppermute | solution.py:448
  62.2 2.3 %collective-permute-done.9 = f32[1,72,256]{2,1,0:T(8,128)S(1)} collective-permute-done((f32[1,72,256]{2,1,0:T(8,128)S(1)}, f32[1,72,256]{2,1,0:T(8,128)S(1)}, u32[]{:S(2)}, u32[]{:S(2)}) %collective-permute-start.9) | collective-permute-done | bytes 73760 | tf_op jit(solution)/shard_map/ppermute | solution.py:448
  64.6 2.1 %collective-permute-start.12 = (f32[1,72,256]{2,1,0:T(8,128)S(1)}, f32[1,72,256]{2,1,0:T(8,128)S(1)}, u32[]{:S(2)}, u32[]{:S(2)}) collective-permute-start(f32[1,72,256]{2,1,0:T(8,128)S(1)} %add.23), channel_id=1, source_target_pairs={{0,6},{1,7},{2,4},{3,5},{4,2},{5,3},{6,0},{7,1},{8,14},{9,15},{10,... | collective-permute-start | bytes 221192 | tf_op jit(solution)/shard_map/ppermute | solution.py:455
  66.7 0.8 collective-permute-start.11
  67.6 0.6 collective-permute-start.10
  68.1 1.8 %collective-permute-done.12 = f32[1,72,256]{2,1,0:T(8,128)S(1)} collective-permute-done((f32[1,72,256]{2,1,0:T(8,128)S(1)}, f32[1,72,256]{2,1,0:T(8,128)S(1)}, u32[]{:S(2)}, u32[]{:S(2)}) %collective-permute-start.12) | collective-permute-done | bytes 73760 | tf_op jit(solution)/shard_map/ppermute | solution.py:455
  69.9 1.2 %collective-permute-done.11 = f32[1,72,256]{2,1,0:T(8,128)S(1)} collective-permute-done((f32[1,72,256]{2,1,0:T(8,128)S(1)}, f32[1,72,256]{2,1,0:T(8,128)S(1)}, u32[]{:S(2)}, u32[]{:S(2)}) %collective-permute-start.11) | collective-permute-done | bytes 73760 | tf_op jit(solution)/shard_map/ppermute | solution.py:455
  71.1 0.8 collective-permute-done.10
  72.0 0.1 collective-permute-start.13
  72.0 1.6 %collective-permute-done.13.high_ref = f32[4,72,256]{2,1,0:T(8,128)S(1)} collective-permute-done((f32[4,72,256]{2,1,0:T(8,128)S(1)}, f32[4,72,256]{2,1,0:T(8,128)S(1)}, u32[]{:S(2)}, u32[]{:S(2)}) %collective-permute-start.13) | collective-permute-done | bytes 294944 | tf_op jit(solution)/shard_map/ppermute | solution.py:448
  73.6 18.5 %final.1 = (f32[8192,256]{1,0:T(8,128)}, f32[3,256]{1,0:T(4,128)}, f32[64,128]{1,0:T(8,128)}) custom-call(s32[1]{0:T(128)} %bitcast.place_ref, f32[4,72,256]{2,1,0:T(8,128)S(1)} %pad_maximum_fusion.low_ref, f32[4,72,256]{2,1,0:T(8,128)S(1)} %collective-permute-done.13.high_ref, s32[1,256]{1,0:T(1,128)S(1)} %bitcast.9, f32[64,128]{1,0:T(8,128)S(1)} %bitcast.8, ...), custom_call_target="tpu_custom_call" | custom-call | tf_op jit(solution)/shard_map/final/pallas_call | solution.py:411
  (20 shorter events, 0.2 us)
Async XLA Ops:
  1.9 26.2 %collective-permute-start.3 = (f32[512,256]{1,0:T(8,128)S(1)}, f32[512,256]{1,0:T(8,128)S(1)}, u32[]{:S(2)}, u32[]{:S(2)}) collective-permute-start(f32[512,256]{1,0:T(8,128)S(1)} %get-tuple-element.23), channel_id=1, source_target_pairs={{0,28},{4,0},{8,4},{12,8},{16,12},{20,16},{24,20},{28,24},{1,29},{... | collective-permute-start | bytes 1572872 | tf_op jit(solution)/shard_map/ppermute | solution.py:437
  8.0 20.1 %collective-permute-start.2 = (f32[512,256]{1,0:T(8,128)S(1)}, f32[512,256]{1,0:T(8,128)S(1)}, u32[]{:S(2)}, u32[]{:S(2)}) collective-permute-start(f32[512,256]{1,0:T(8,128)S(1)} %get-tuple-element.23), channel_id=1, source_target_pairs={{1,0},{2,1},{3,2},{5,4},{6,5},{7,6},{9,8},{10,9},{11,10},{13,12},{... | collective-permute-start | bytes 1572872 | tf_op jit(solution)/shard_map/ppermute | solution.py:443
  9.2 19.0 %collective-permute-start.1 = (f32[512,256]{1,0:T(8,128)S(1)}, f32[512,256]{1,0:T(8,128)S(1)}, u32[]{:S(2)}, u32[]{:S(2)}) collective-permute-start(f32[512,256]{1,0:T(8,128)S(1)} %get-tuple-element.24), channel_id=1, source_target_pairs={{0,4},{4,8},{8,12},{12,16},{16,20},{20,24},{24,28},{28,0},{1,5},{5... | collective-permute-start | bytes 1572872 | tf_op jit(solution)/shard_map/ppermute | solution.py:437
  9.3 18.9 %collective-permute-start = (f32[512,256]{1,0:T(8,128)S(1)}, f32[512,256]{1,0:T(8,128)S(1)}, u32[]{:S(2)}, u32[]{:S(2)}) collective-permute-start(f32[512,256]{1,0:T(8,128)S(1)} %get-tuple-element.24), channel_id=1, source_target_pairs={{0,1},{1,2},{2,3},{4,5},{5,6},{6,7},{8,9},{9,10},{10,11},{12,13},{... | collective-permute-start | bytes 1572872 | tf_op jit(solution)/shard_map/ppermute | solution.py:443
  13.2 3.4 %copy-start = (f32[8192,256]{1,0:T(8,128)S(1)}, f32[8192,256]{1,0:T(8,128)}, u32[]{:S(2)}) copy-start(f32[8192,256]{1,0:T(8,128)} %snap.1) | copy-start | bytes 25165828
  16.5 0.8 copy-start.2
  17.3 10.9 %copy-start.1 = (bf16[8192,512]{1,0:T(8,128)(2,1)S(1)}, bf16[8192,512]{1,0:T(8,128)(2,1)}, u32[]{:S(2)}) copy-start(bf16[8192,512]{1,0:T(8,128)(2,1)} %tangent_any.1) | copy-start | bytes 25165828
  28.2 45.4 %slice-start = ((s8[8388608]{0:T(1024)(128)(4,1)}), s8[4194304]{0:T(1024)(128)(4,1)S(1)}, s32[]{:S(2)}) async-start(s8[8388608]{0:T(1024)(128)(4,1)} %bitcast.4), calls=%async_computation | async-start | bytes 8388608
  28.2 45.4 %slice-start.1 = ((s8[8388608]{0:T(1024)(128)(4,1)}), s8[4194304]{0:T(1024)(128)(4,1)S(1)}, s32[]{:S(2)}) async-start(s8[8388608]{0:T(1024)(128)(4,1)} %bitcast.4), calls=%async_computation.1 | async-start | bytes 8388608
  28.2 45.4 %copy-start.3 = (s32[256]{0:T(256)S(1)}, s32[256]{0:T(256)}, u32[]{:S(2)}) copy-start(s32[256]{0:T(256)} %param.9) | copy-start | bytes 3076
  43.5 1.6 %collective-permute-start.4 = (f32[4,72,256]{2,1,0:T(8,128)S(1)}, f32[4,72,256]{2,1,0:T(8,128)S(1)}, u32[]{:S(2)}, u32[]{:S(2)}) collective-permute-start(f32[4,72,256]{2,1,0:T(8,128)S(1)} %get-tuple-element.18), channel_id=1, source_target_pairs={{0,1},{1,0},{2,3},{3,2},{4,5},{5,4},{6,7},{7,6},{8,9},{9,8},{10,11... | collective-permute-start | bytes 884744 | tf_op jit(solution)/shard_map/ppermute | solution.py:448
  45.3 6.0 %collective-permute-start.5 = (f32[1,72,256]{2,1,0:T(8,128)S(1)}, f32[1,72,256]{2,1,0:T(8,128)S(1)}, u32[]{:S(2)}, u32[]{:S(2)}) collective-permute-start(f32[1,72,256]{2,1,0:T(8,128)S(1)} %get-tuple-element.25), channel_id=1, source_target_pairs={{0,4},{1,5},{2,6},{3,7},{4,0},{5,1},{6,2},{7,3},{8,12},{9,13},{10,... | collective-permute-start | bytes 221192 | tf_op jit(solution)/shard_map/ppermute | solution.py:455
  47.8 5.9 %collective-permute-start.7 = (f32[1,72,256]{2,1,0:T(8,128)S(1)}, f32[1,72,256]{2,1,0:T(8,128)S(1)}, u32[]{:S(2)}, u32[]{:S(2)}) collective-permute-start(f32[1,72,256]{2,1,0:T(8,128)S(1)} %get-tuple-element.26), channel_id=1, source_target_pairs={{0,6},{1,7},{2,4},{3,5},{4,2},{5,3},{6,0},{7,1},{8,14},{9,15},{10,... | collective-permute-start | bytes 221192 | tf_op jit(solution)/shard_map/ppermute | solution.py:455
  48.9 4.9 %collective-permute-start.6 = (f32[1,72,256]{2,1,0:T(8,128)S(1)}, f32[1,72,256]{2,1,0:T(8,128)S(1)}, u32[]{:S(2)}, u32[]{:S(2)}) collective-permute-start(f32[1,72,256]{2,1,0:T(8,128)S(1)} %get-tuple-element.27), channel_id=1, source_target_pairs={{0,2},{1,3},{2,0},{3,1},{4,6},{5,7},{6,4},{7,5},{8,10},{9,11},{10,... | collective-permute-start | bytes 221192 | tf_op jit(solution)/shard_map/ppermute | solution.py:455
  53.7 4.4 %collective-permute-start.8 = (f32[1,72,256]{2,1,0:T(8,128)S(1)}, f32[1,72,256]{2,1,0:T(8,128)S(1)}, u32[]{:S(2)}, u32[]{:S(2)}) collective-permute-start(f32[1,72,256]{2,1,0:T(8,128)S(1)} %fusion.1), channel_id=1, source_target_pairs={{0,8},{4,12},{8,0},{12,4},{16,24},{20,28},{24,16},{28,20},{1,9},{5... | collective-permute-start | bytes 221192 | tf_op jit(solution)/shard_map/ppermute | solution.py:448
  58.2 6.4 %collective-permute-start.9 = (f32[1,72,256]{2,1,0:T(8,128)S(1)}, f32[1,72,256]{2,1,0:T(8,128)S(1)}, u32[]{:S(2)}, u32[]{:S(2)}) collective-permute-start(f32[1,72,256]{2,1,0:T(8,128)S(1)} %add.22), channel_id=1, source_target_pairs={{0,16},{4,20},{8,24},{12,28},{16,0},{20,4},{24,8},{28,12},{1,17},{... | collective-permute-start | bytes 221192 | tf_op jit(solution)/shard_map/ppermute | solution.py:448
  64.6 5.3 %collective-permute-start.12 = (f32[1,72,256]{2,1,0:T(8,128)S(1)}, f32[1,72,256]{2,1,0:T(8,128)S(1)}, u32[]{:S(2)}, u32[]{:S(2)}) collective-permute-start(f32[1,72,256]{2,1,0:T(8,128)S(1)} %add.23), channel_id=1, source_target_pairs={{0,6},{1,7},{2,4},{3,5},{4,2},{5,3},{6,0},{7,1},{8,14},{9,15},{10,... | collective-permute-start | bytes 221192 | tf_op jit(solution)/shard_map/ppermute | solution.py:455
  66.7 4.4 %collective-permute-start.11 = (f32[1,72,256]{2,1,0:T(8,128)S(1)}, f32[1,72,256]{2,1,0:T(8,128)S(1)}, u32[]{:S(2)}, u32[]{:S(2)}) collective-permute-start(f32[1,72,256]{2,1,0:T(8,128)S(1)} %add.23), channel_id=1, source_target_pairs={{0,2},{1,3},{2,0},{3,1},{4,6},{5,7},{6,4},{7,5},{8,10},{9,11},{10,... | collective-permute-start | bytes 221192 | tf_op jit(solution)/shard_map/ppermute | solution.py:455
  67.6 4.4 %collective-permute-start.10 = (f32[1,72,256]{2,1,0:T(8,128)S(1)}, f32[1,72,256]{2,1,0:T(8,128)S(1)}, u32[]{:S(2)}, u32[]{:S(2)}) collective-permute-start(f32[1,72,256]{2,1,0:T(8,128)S(1)} %add.23), channel_id=1, source_target_pairs={{0,4},{1,5},{2,6},{3,7},{4,0},{5,1},{6,2},{7,3},{8,12},{9,13},{10,... | collective-permute-start | bytes 221192 | tf_op jit(solution)/shard_map/ppermute | solution.py:455
  72.0 1.6 %collective-permute-start.13 = (f32[4,72,256]{2,1,0:T(8,128)S(1)}, f32[4,72,256]{2,1,0:T(8,128)S(1)}, u32[]{:S(2)}, u32[]{:S(2)}) collective-permute-start(f32[4,72,256]{2,1,0:T(8,128)S(1)} %pad_maximum_fusion.low_ref), channel_id=1, source_target_pairs={{0,1},{1,0},{2,3},{3,2},{4,5},{5,4},{6,7},{7,6},{8,9},{9,8},{10,11... | collective-permute-start | bytes 884744 | tf_op jit(solution)/shard_map/ppermute | solution.py:448
